TPU v7x, 32 devices: a whole 2x2x4 slice. The times are simulated.
32 devices in a mesh: dp: 8 (over z, core), seq: 4 (over y, x).
Axes of the slice: x: 2, y: 2, z: 4, core: 2. Of those that a mesh axis runs over, the one named last changes fastest.
Arguments:
- frames: bfloat16 [16, 1024, 1024], P('dp', 'seq'), may hold values from -6 to 6
- skip_in: bfloat16 [16, 1024, 1024], P('dp', 'seq'), may hold values from -6 to 6
- cond: bfloat16 [16, 1024, 1024], P('dp', 'seq'), may hold values from -6 to 6
- seg_ids: int32 [16, 1024], P('dp', 'seq'), may hold values from 0 to 2, as said below
- drop_flags: int32 [16, 3], P('dp'), may hold values 0 or 1
- flow_times: float32 [16, 3], P('dp'), may hold values from 0 to 1
- w_skip: bfloat16 [2048, 1024], P('dp', 'seq'), may hold values from -0.125 to 0.125
- w_qkv: bfloat16 [1024, 3072], P('dp', 'seq'), may hold values from -0.1875 to 0.1875
- w_out: bfloat16 [1024, 1024], P('seq', 'dp'), may hold values from -1.5 to 1.5
- w_up: bfloat16 [1024, 4096], P('dp', 'seq'), may hold values from -0.1875 to 0.1875
- w_down: bfloat16 [4096, 1024], P('seq', 'dp'), may hold values from -0.09375 to 0.09375
- w_mod: bfloat16 [1024, 6144], P('dp', 'seq'), may hold values from -0.375 to 0.375
- cotangent: bfloat16 [16, 1024, 1024], P('dp', 'seq'), may hold values from -6 to 6
Outputs:
- output: bfloat16 [16, 1024, 1024], P('dp', 'seq')
- grad_frames: bfloat16 [16, 1024, 1024], P('dp', 'seq')
- grad_skip: bfloat16 [16, 1024, 1024], P('dp', 'seq')
- grad_w_skip: float32 [2048, 1024], P('dp', 'seq')
- grad_w_qkv: float32 [1024, 3072], P('dp', 'seq')
- grad_w_out: float32 [1024, 1024], P('seq', 'dp')
- grad_w_up: float32 [1024, 4096], P('dp', 'seq')
- grad_w_down: float32 [4096, 1024], P('seq', 'dp')
- grad_w_mod: float32 [1024, 6144], P('dp', 'seq')
Inputs may be any that keep to these rules, and one draw needn't show every extreme that they name: `seg_ids`: in each row the ids never fall; utterance 1 begins within the first 256 frames and ends within the last 256 frames; utterances 0 and 2 are never empty.
All inputs are finite; a program needn't handle non-finite values. No bound on the sum of `drop_flags` on one device may be relied on, other than what follows from the above.
Results may differ from a plain program's by a relative error of at most 0.023.
Values may be sent and summed in bfloat16 or wider, within the bound.
No kernel may reach another device: no remote copies, remote signals or barrier semaphores. Data moves between devices by JAX's collectives and lax.ppermute only.
A program may use at most 256 MiB of HBM per device.

v0:
```python
import math

import jax
import jax.numpy as jnp
from jax import lax
from jax.sharding import PartitionSpec as P

HEADS = 16


EPSILON = 1e-06
MASKED = -1e30


def norm_mod(hidden, offset, factor):
    centre = hidden - jnp.mean(hidden, -1, keepdims=True)
    variance = jnp.mean(centre * centre, -1, keepdims=True)
    return centre * lax.rsqrt(variance + EPSILON) * (1.0 + factor) + offset


def gelu_tanh(values):
    return jax.nn.gelu(values, approximate=True)


def rope_tables(positions, head_dim):
    half_dim = head_dim // 2
    frequency = jnp.exp(
        jnp.arange(half_dim, dtype=jnp.float32) * (-2.0 * math.log(10000.0) / head_dim)
    )
    angles = positions.astype(jnp.float32)[:, None] * frequency[None, :]
    return (jnp.cos(angles), jnp.sin(angles))


def rotate(values, cosine, sine_table):
    half_dim = values.shape[-1] // 2
    lower_half = values[..., :half_dim]
    upper_half = values[..., half_dim:]
    cos_part = cosine[:, None, :]
    sin_part = sine_table[:, None, :]
    return jnp.concatenate(
        [
            lower_half * cos_part - upper_half * sin_part,
            upper_half * cos_part + lower_half * sin_part,
        ],
        -1,
    )


def time_embed(flow_values, model_width):
    half_dim = model_width // 2
    frequency = jnp.exp(jnp.arange(half_dim, dtype=jnp.float32) * (-math.log(10000.0) / half_dim))
    angles = 1000.0 * flow_values[..., None] * frequency
    return jnp.concatenate([jnp.sin(angles), jnp.cos(angles)], -1)


def spread(per_utterance, onehot):
    result = onehot[:, :, 0, None] * per_utterance[:, 0, None, :]
    for position in range(1, onehot.shape[2]):
        result = result + onehot[:, :, position, None] * per_utterance[:, position, None, :]
    return result


def over_rows(left, right):
    return lax.dot_general(
        left, right, (((0,), (0,)), ((), ())), preferred_element_type=jnp.float32
    )


def against(left, right):
    return lax.dot_general(
        left, right, (((1,), (1,)), ((), ())), preferred_element_type=jnp.float32
    )


def split_heads(projected, cosine, sine_table, heads, head_dim):
    lead_shape = projected.shape[:2]
    grouped = projected.reshape(lead_shape + (heads, 3, head_dim))
    queries = rotate(grouped[:, :, :, 0], cosine, sine_table).astype(jnp.bfloat16)
    key_part = rotate(grouped[:, :, :, 1], cosine, sine_table).astype(jnp.bfloat16)
    value_part = grouped[:, :, :, 2].astype(jnp.bfloat16)
    return (queries, key_part, value_part)


def pack_back(grad_q, grad_k, grad_v, cosine, sine_table, split_shape):
    unrotated_q = rotate(
        grad_q.astype(jnp.float32).reshape(split_shape), cosine, -sine_table
    ).astype(jnp.bfloat16)
    unrotated_k = rotate(
        grad_k.astype(jnp.float32).reshape(split_shape), cosine, -sine_table
    ).astype(jnp.bfloat16)
    stacked = jnp.stack([unrotated_q, unrotated_k, grad_v.reshape(split_shape)], 3)
    return stacked.reshape(split_shape[0], split_shape[1], 3 * split_shape[2] * split_shape[3])


def second_norm_back(middle, shift_two, scale_two, grad_norm_two, grad_out, branch, gate_one):
    grad_middle_norm, grad_shift_two, grad_scale_two = jax.vjp(
        norm_mod, middle, shift_two, scale_two
    )[1](grad_norm_two)
    grad_middle = grad_out + grad_middle_norm
    grad_gate_one = grad_middle * branch
    grad_branch = (gate_one * grad_middle).astype(jnp.bfloat16)
    return (grad_middle, grad_shift_two, grad_scale_two, grad_gate_one, grad_branch)


def attend_row(query_row, key_row, value_row, seg_row):
    length, local_heads, head_dim = query_row.shape
    block_rows = min(512, length)
    blocks = length // block_rows
    factor = head_dim ** (-0.5)

    def one_block(inputs):
        query_block, seg_block = inputs
        scores = (
            jnp.einsum("qhd,khd->hqk", query_block, key_row, preferred_element_type=jnp.float32)
            * factor
        )
        allowed = (seg_block[:, None] == seg_row[None, :])[None]
        scores = jnp.where(allowed, scores, MASKED)
        highest = jnp.max(scores, -1, keepdims=True)
        raised = jnp.exp(scores - highest)
        totals = jnp.sum(raised, -1, keepdims=True)
        weights_p = (raised / totals).astype(jnp.bfloat16)
        result = jnp.einsum(
            "hqk,khd->qhd", weights_p, value_row, preferred_element_type=jnp.float32
        )
        return (result.astype(jnp.bfloat16), (highest + jnp.log(totals))[..., 0])

    result, log_totals = lax.map(
        one_block,
        (
            query_row.reshape(blocks, block_rows, local_heads, head_dim),
            seg_row.reshape(blocks, block_rows),
        ),
    )
    return (result.reshape(length, local_heads * head_dim), log_totals)


def attend_back_row(query_row, key_row, value_row, seg_row, grad_row, log_totals):
    length, local_heads, head_dim = query_row.shape
    block_rows = min(512, length)
    blocks = length // block_rows
    factor = head_dim ** (-0.5)

    def one_block(running, inputs):
        key_grad, value_grad = running
        query_block, grad_block, seg_block, lse_block = inputs
        scores = (
            jnp.einsum("qhd,khd->hqk", query_block, key_row, preferred_element_type=jnp.float32)
            * factor
        )
        allowed = (seg_block[:, None] == seg_row[None, :])[None]
        weights_p = jnp.where(allowed, jnp.exp(scores - lse_block[:, :, None]), 0.0)
        grad_weights = jnp.einsum(
            "qhd,khd->hqk", grad_block, value_row, preferred_element_type=jnp.float32
        )
        inner_sum = jnp.sum(weights_p * grad_weights, -1, keepdims=True)
        grad_scores = (weights_p * (grad_weights - inner_sum)).astype(jnp.bfloat16)
        query_grad = (
            jnp.einsum("hqk,khd->qhd", grad_scores, key_row, preferred_element_type=jnp.float32)
            * factor
        )
        key_grad = (
            key_grad
            + jnp.einsum(
                "hqk,qhd->khd", grad_scores, query_block, preferred_element_type=jnp.float32
            )
            * factor
        )
        value_grad = value_grad + jnp.einsum(
            "hqk,qhd->khd",
            weights_p.astype(jnp.bfloat16),
            grad_block,
            preferred_element_type=jnp.float32,
        )
        return ((key_grad, value_grad), query_grad)

    zeros_start = jnp.zeros(key_row.shape, jnp.float32)
    block_shape = (blocks, block_rows, local_heads, head_dim)
    (key_grad, value_grad), query_grad = lax.scan(
        one_block,
        (zeros_start, zeros_start),
        (
            query_row.reshape(block_shape),
            grad_row.reshape(block_shape),
            seg_row.reshape(blocks, block_rows),
            log_totals,
        ),
    )
    flat_shape = (length, local_heads * head_dim)
    return (
        query_grad.reshape(flat_shape).astype(jnp.bfloat16),
        key_grad.reshape(flat_shape).astype(jnp.bfloat16),
        value_grad.reshape(flat_shape).astype(jnp.bfloat16),
    )


def forward_row(inputs):
    return attend_row(inputs[0], inputs[1], inputs[2], inputs[3])


def backward_row(inputs):
    return attend_back_row(inputs[0], inputs[1], inputs[2], inputs[3], inputs[4], inputs[5])


def body(
    frames,
    skip_in,
    cond,
    seg_ids,
    drop_flags,
    flow_times,
    w_skip,
    w_qkv,
    w_out,
    w_up,
    w_down,
    w_mod,
    cotangent,
):
    row_count, frame_count, model_width = frames.shape
    seq_devices = lax.axis_size("seq")
    head_dim = model_width // HEADS
    local_heads = HEADS // seq_devices
    length = frame_count * seq_devices
    tokens = row_count * frame_count
    seg_count = drop_flags.shape[1]
    frame_shape = (row_count, frame_count, model_width)
    head_shape = (row_count, length, local_heads, head_dim)
    skip_dp, qkv_dp, out_dp, up_dp, down_dp, mod_dp = (
        lax.all_gather(w_skip, "dp", axis=0, tiled=True),
        lax.all_gather(w_qkv, "dp", axis=0, tiled=True),
        lax.all_gather(w_out, "dp", axis=1, tiled=True),
        lax.all_gather(w_up, "dp", axis=0, tiled=True),
        lax.all_gather(w_down, "dp", axis=1, tiled=True),
        lax.all_gather(w_mod, "dp", axis=0, tiled=True),
    )
    full_skip, full_qkv, full_out, full_up, full_down, full_mod = (
        lax.all_gather(skip_dp, "seq", axis=1, tiled=True),
        lax.all_gather(qkv_dp, "seq", axis=1, tiled=True),
        lax.all_gather(out_dp, "seq", axis=0, tiled=True),
        lax.all_gather(up_dp, "seq", axis=1, tiled=True),
        lax.all_gather(down_dp, "seq", axis=0, tiled=True),
        lax.all_gather(mod_dp, "seq", axis=1, tiled=True),
    )
    dropped = lax.psum(jnp.sum(drop_flags).astype(jnp.float32), "dp")
    slots = float(row_count * seg_count * lax.axis_size("dp"))
    cond_scale = slots / jnp.maximum(slots - dropped, 1.0)
    onehot = (seg_ids[:, :, None] == jnp.arange(seg_count, dtype=jnp.int32)).astype(jnp.float32)
    activity = (
        jax.nn.silu(time_embed(flow_times, model_width))
        .astype(jnp.bfloat16)
        .reshape(row_count * seg_count, model_width)
    )
    modulation = jnp.dot(activity, full_mod, preferred_element_type=jnp.float32).reshape(
        row_count, seg_count, 6 * model_width
    )
    per_frame = spread(modulation, onehot).reshape(tokens, 6 * model_width)
    shift_one, scale_one, gate_one, shift_two, scale_two, gate_two = jnp.split(per_frame, 6, axis=1)
    keep_frame = (1.0 - jnp.sum(onehot * drop_flags.astype(jnp.float32)[:, None, :], -1)).reshape(
        tokens, 1
    )
    joined = jnp.concatenate([frames, skip_in], -1).reshape(tokens, 2 * model_width)
    hidden = jnp.dot(
        joined, full_skip, preferred_element_type=jnp.float32
    ) + keep_frame * cond_scale * cond.reshape(tokens, model_width).astype(jnp.float32)
    normed = norm_mod(hidden, shift_one, scale_one).astype(jnp.bfloat16)
    seg_rows = lax.all_gather(seg_ids, "seq", axis=1, tiled=True)
    grad_out = cotangent.reshape(tokens, model_width).astype(jnp.float32)
    projected = jnp.dot(normed, full_qkv, preferred_element_type=jnp.float32).reshape(
        row_count, frame_count, 3 * model_width
    )
    positions = lax.axis_index("seq") * frame_count + jnp.arange(frame_count, dtype=jnp.int32)
    cosine, sine_table = rope_tables(positions, head_dim)
    queries, key_frames, value_frames = split_heads(projected, cosine, sine_table, HEADS, head_dim)
    head_q, head_k, head_v = (
        lax.all_to_all(
            queries.reshape(frame_shape), "seq", split_axis=2, concat_axis=1, tiled=True
        ),
        lax.all_to_all(
            key_frames.reshape(frame_shape), "seq", split_axis=2, concat_axis=1, tiled=True
        ),
        lax.all_to_all(
            value_frames.reshape(frame_shape), "seq", split_axis=2, concat_axis=1, tiled=True
        ),
    )
    head_q = head_q.reshape(head_shape)
    head_k = head_k.reshape(head_shape)
    head_v = head_v.reshape(head_shape)
    attended, log_totals = lax.map(forward_row, (head_q, head_k, head_v, seg_rows))
    back_frames = lax.all_to_all(attended, "seq", split_axis=1, concat_axis=2, tiled=True)
    attn_flat = back_frames.reshape(tokens, model_width)
    branch = jnp.dot(attn_flat, full_out, preferred_element_type=jnp.float32)
    middle = hidden + gate_one * branch
    normed_two = norm_mod(middle, shift_two, scale_two).astype(jnp.bfloat16)
    pre_act = jnp.dot(normed_two, full_up, preferred_element_type=jnp.float32)
    activated = gelu_tanh(pre_act).astype(jnp.bfloat16)
    fed = jnp.dot(activated, full_down, preferred_element_type=jnp.float32)
    output = (middle + gate_two * fed).astype(jnp.bfloat16).reshape(frame_shape)
    grad_gate_two = grad_out * fed
    grad_fed = (gate_two * grad_out).astype(jnp.bfloat16)
    grad_act = against(grad_fed, full_down)
    grad_w_down = over_rows(activated, grad_fed)
    grad_pre = jax.vjp(gelu_tanh, pre_act)[1](grad_act)[0].astype(jnp.bfloat16)
    grad_norm_two = against(grad_pre, full_up)
    grad_w_up = over_rows(normed_two, grad_pre)
    grad_middle, grad_shift_two, grad_scale_two, grad_gate_one, grad_branch = second_norm_back(
        middle, shift_two, scale_two, grad_norm_two, grad_out, branch, gate_one
    )
    grad_attended = against(grad_branch, full_out).astype(jnp.bfloat16)
    grad_w_out = over_rows(attn_flat, grad_branch)
    grad_head_rows = lax.all_to_all(
        grad_attended.reshape(frame_shape), "seq", split_axis=2, concat_axis=1, tiled=True
    ).reshape(head_shape)
    grad_q, grad_k, grad_v = lax.map(
        backward_row, (head_q, head_k, head_v, seg_rows, grad_head_rows, log_totals)
    )
    frame_q, frame_k, frame_v = (
        lax.all_to_all(grad_q, "seq", split_axis=1, concat_axis=2, tiled=True),
        lax.all_to_all(grad_k, "seq", split_axis=1, concat_axis=2, tiled=True),
        lax.all_to_all(grad_v, "seq", split_axis=1, concat_axis=2, tiled=True),
    )
    grad_projected = pack_back(
        frame_q, frame_k, frame_v, cosine, sine_table, (row_count, frame_count, HEADS, head_dim)
    ).reshape(tokens, 3 * model_width)
    grad_normed = against(grad_projected, full_qkv)
    grad_w_qkv = over_rows(normed, grad_projected)
    grad_hidden_norm, grad_shift_one, grad_scale_one = jax.vjp(
        norm_mod, hidden, shift_one, scale_one
    )[1](grad_normed)
    grad_hidden = (grad_middle + grad_hidden_norm).astype(jnp.bfloat16)
    grad_joined = against(grad_hidden, full_skip)
    grad_frames = grad_joined[:, :model_width].astype(jnp.bfloat16).reshape(frame_shape)
    grad_skip = grad_joined[:, model_width:].astype(jnp.bfloat16).reshape(frame_shape)
    grad_w_skip = over_rows(joined, grad_hidden)
    grad_per_frame = jnp.concatenate(
        [
            grad_shift_one,
            grad_scale_one,
            grad_gate_one,
            grad_shift_two,
            grad_scale_two,
            grad_gate_two,
        ],
        -1,
    ).reshape(row_count, frame_count, 6 * model_width)
    grad_modulation = jnp.einsum(
        "rfs,rfc->rsc", onehot, grad_per_frame, precision=lax.Precision.HIGHEST
    ).reshape(row_count * seg_count, 6 * model_width)
    grad_w_mod = jnp.dot(
        activity.astype(jnp.float32).T, grad_modulation, precision=lax.Precision.HIGHEST
    )
    seq_skip, seq_qkv, seq_out, seq_up, seq_down, seq_mod = (
        lax.psum_scatter(
            grad_w_skip.astype(jnp.bfloat16), "seq", scatter_dimension=1, tiled=True
        ).astype(jnp.float32),
        lax.psum_scatter(
            grad_w_qkv.astype(jnp.bfloat16), "seq", scatter_dimension=1, tiled=True
        ).astype(jnp.float32),
        lax.psum_scatter(
            grad_w_out.astype(jnp.bfloat16), "seq", scatter_dimension=0, tiled=True
        ).astype(jnp.float32),
        lax.psum_scatter(
            grad_w_up.astype(jnp.bfloat16), "seq", scatter_dimension=1, tiled=True
        ).astype(jnp.float32),
        lax.psum_scatter(
            grad_w_down.astype(jnp.bfloat16), "seq", scatter_dimension=0, tiled=True
        ).astype(jnp.float32),
        lax.psum_scatter(
            grad_w_mod.astype(jnp.bfloat16), "seq", scatter_dimension=1, tiled=True
        ).astype(jnp.float32),
    )
    sum_skip, sum_qkv, sum_out, sum_up, sum_down, sum_mod = (
        lax.psum_scatter(
            seq_skip.astype(jnp.bfloat16), "dp", scatter_dimension=0, tiled=True
        ).astype(jnp.float32),
        lax.psum_scatter(
            seq_qkv.astype(jnp.bfloat16), "dp", scatter_dimension=0, tiled=True
        ).astype(jnp.float32),
        lax.psum_scatter(
            seq_out.astype(jnp.bfloat16), "dp", scatter_dimension=1, tiled=True
        ).astype(jnp.float32),
        lax.psum_scatter(seq_up.astype(jnp.bfloat16), "dp", scatter_dimension=0, tiled=True).astype(
            jnp.float32
        ),
        lax.psum_scatter(
            seq_down.astype(jnp.bfloat16), "dp", scatter_dimension=1, tiled=True
        ).astype(jnp.float32),
        lax.psum_scatter(
            seq_mod.astype(jnp.bfloat16), "dp", scatter_dimension=0, tiled=True
        ).astype(jnp.float32),
    )
    return (output, grad_frames, grad_skip, sum_skip, sum_qkv, sum_out, sum_up, sum_down, sum_mod)


def solution(mesh):
    in_specs = (
        P("dp", "seq", None),
        P("dp", "seq", None),
        P("dp", "seq", None),
        P("dp", "seq"),
        P("dp", None),
        P("dp", None),
        P("dp", "seq"),
        P("dp", "seq"),
        P("seq", "dp"),
        P("dp", "seq"),
        P("seq", "dp"),
        P("dp", "seq"),
        P("dp", "seq", None),
    )
    out_specs = (
        P("dp", "seq", None),
        P("dp", "seq", None),
        P("dp", "seq", None),
        P("dp", "seq"),
        P("dp", "seq"),
        P("seq", "dp"),
        P("dp", "seq"),
        P("seq", "dp"),
        P("dp", "seq"),
    )
    return jax.shard_map(body, mesh=mesh, in_specs=in_specs, out_specs=out_specs, check_vma=False)
```

profile of v0, /device:TPU:0, one launch (start us, length us, event | category | flops | bytes accessed | tf_op | source)
XLA Modules:
  0.0 1554.5 jit_solution(18012724902142785347)
XLA Ops:
  10.0 24.4 %all-gather.12.cloned.1.call-done = bf16[2048,256]{1,0:T(8,128)(2,1)} async-done(((bf16[256,256]{1,0:T(8,128)(2,1)}), bf16[2048,256]{1,0:T(8,128)(2,1)}) %all-gather.12.cloned.1.call-update) | async-done | bytes 1048592 | tf_op jit(solution)/shard_map/all_gather | solution.py:230
  34.6 39.5 %all-gather.16.cloned.1.call-done = bf16[1024,1536]{1,0:T(8,128)(2,1)} async-done(((bf16[128,1536]{1,0:T(8,128)(2,1)}), bf16[1024,1536]{1,0:T(8,128)(2,1)}) %all-gather.16.cloned.1.call-update) | async-done | bytes 3145744 | tf_op jit(solution)/shard_map/all_gather | solution.py:235
  74.1 25.5 %all-gather.20.cloned.1.call-done = bf16[1024,768]{1,0:T(8,128)(2,1)} async-done(((bf16[128,768]{1,0:T(8,128)(2,1)}), bf16[1024,768]{1,0:T(8,128)(2,1)}) %all-gather.20.cloned.1.call-update) | async-done | bytes 1572880 | tf_op jit(solution)/shard_map/all_gather | solution.py:231
  100.5 15.1 all_gather.46
  115.7 16.8 %all-gather.30.cloned.1.call-done = bf16[1024,1024]{1,0:T(8,128)(2,1)} async-done(((bf16[1024,128]{1,0:T(8,128)(2,1)}), bf16[1024,1024]{1,0:T(8,128)(2,1)}) %all-gather.30.cloned.1.call-update) | async-done | bytes 2097168 | tf_op jit(solution)/shard_map/all_gather | solution.py:234
  133.8 15.1 psum.7
  153.0 32.5 %all-gather.14.cloned.1.call-done = bf16[2048,1024]{1,0:T(8,128)(2,1)} async-done(((bf16[2048,256]{1,0:T(8,128)(2,1)}), bf16[2048,1024]{1,0:T(8,128)(2,1)}) %all-gather.14.cloned.1.call-update) | async-done | bytes 4194320 | tf_op jit(solution)/shard_map/all_gather | solution.py:238
  191.4 118.3 %all-gather.18.cloned.1.call-done = bf16[1024,6144]{1,0:T(8,128)(2,1)} async-done(((bf16[1024,1536]{1,0:T(8,128)(2,1)}), bf16[1024,6144]{1,0:T(8,128)(2,1)}) %all-gather.18.cloned.1.call-update) | async-done | bytes 12582928 | tf_op jit(solution)/shard_map/all_gather | solution.py:243
  309.7 6.4 fusion.44
  324.7 57.1 %all-gather.22.cloned.1.call-done = bf16[1024,3072]{1,0:T(8,128)(2,1)} async-done(((bf16[1024,768]{1,0:T(8,128)(2,1)}), bf16[1024,3072]{1,0:T(8,128)(2,1)}) %all-gather.22.cloned.1.call-update) | async-done | bytes 6291472 | tf_op jit(solution)/shard_map/all_gather | solution.py:239
  381.8 9.7 fusion.85
  391.4 8.4 reshape_reshape.6
  415.1 5.7 all-to-all-done.2
  426.7 14.6 all-to-all-done.1
  445.6 26.2 %all_gather.45 = s32[2,1024]{1,0:T(2,128)S(1)} all-gather(s32[2,256]{1,0:T(2,128)S(1)} %copy-done.59), channel_id=1, replica_groups=mesh['dp'=8,'seq'=4] {'seq'}, dimensions={1}, use_global_device_ids=true | all-gather | bytes 10240 | tf_op jit(solution)/shard_map/all_gather | solution.py:267
  482.5 46.9 %while.54 = (s32[]{:T(128)}, bf16[2,1024,256]{1,2,0:T(8,128)(2,1)}, f32[2,2,4,512]{3,2,1,0:T(4,128)S(1)}, bf16[2,1024,4,64]{1,3,2,0:T(8,128)(2,1)}, s32[2,1024]{...) while((s32[]{:T(128)}, bf16[2,1024,256]{1,2,0:T(8,128)(2,1)}, ...), condition=%wide.region_10.11_spmd, body=%wide.region_5.10_spmd.sunk | while | flops 562690048 | bytes 43645348 | solution.py:289
  486.1 17.0 %while.57 = (s32[]{:T(128)}, bf16[2,512,4,64]{1,3,2,0:T(8,128)(2,1)}, f32[2,4,512]{2,1,0:T(4,128)S(1)}, s32[2,512]{1,0:T(2,128)S(1)}, s32[1024]{0:T(1024)S(1)}, ...) while((s32[]{:T(128)}, ...), condition=%wide.region_9.9_spmd, body=%wide.region_6.8_spmd.sunk | while | flops 562690048 | bytes 35203272 | solution.py:128
  509.6 17.0 %while.57 = (s32[]{:T(128)}, bf16[2,512,4,64]{1,3,2,0:T(8,128)(2,1)}, f32[2,4,512]{2,1,0:T(4,128)S(1)}, s32[2,512]{1,0:T(2,128)S(1)}, s32[1024]{0:T(1024)S(1)}, ...) while((s32[]{:T(128)}, ...), condition=%wide.region_9.9_spmd, body=%wide.region_6.8_spmd.sunk | while | flops 562690048 | bytes 35203272 | solution.py:128
  531.9 28.3 %all_to_all.108 = bf16[2,1024,256]{2,0,1:T(2,128)(2,1)S(1)} all-to-all(bf16[2,1024,256]{2,0,1:T(2,128)(2,1)S(1)} %copy.100), channel_id=1, replica_groups=mesh['dp'=8,'seq'=4] {'seq'}, dimensions={1} | all-to-all | bytes 2097152 | tf_op jit(solution)/shard_map/all_to_all | solution.py:290
  562.2 5.9 fusion.78
  572.6 11.5 fusion.86
  584.1 74.0 %all-gather.28.cloned.1.call-done = bf16[1024,4096]{1,0:T(8,128)(2,1)} async-done(((bf16[1024,1024]{1,0:T(8,128)(2,1)}), bf16[1024,4096]{1,0:T(8,128)(2,1)}) %all-gather.28.cloned.1.call-update) | async-done | bytes 8388624 | tf_op jit(solution)/shard_map/all_gather | solution.py:241
  658.1 16.0 %fusion.52 = (bf16[512,4096]{1,0:T(8,128)(2,1)}, f32[512,4096]{1,0:T(8,128)}) fusion(f32[512,4096]{1,0:T(8,128)} %fusion.86, bf16[512,1024]{1,0:T(8,128)(2,1)} %get-tuple-element.407, bf16[1024,4096]{1,0:T(8,128)(2,1)} %all-gather.28.cloned.1.call-done), kind=kOutput, calls=%fused_computation.82 | convolution fusion | flops 4336910336 | bytes 30408704 | tf_op jit(solution)/shard_map/dot_general | solution.py:295
  674.2 10.2 multiply_reduce_fusion.2
  684.5 10.9 fusion.77
  705.8 13.9 all-to-all-done.4
  725.6 75.1 %while.56 = (s32[]{:T(128)}, bf16[2,1024,256]{1,2,0:T(8,128)(2,1)}, bf16[2,1024,256]{1,2,0:T(8,128)(2,1)}, bf16[2,1024,256]{1,2,0:T(8,128)(2,1)}, bf16[2,1024,4,...) while((s32[]{:T(128)}, bf16[2,1024,256]{1,2,0:T(8,128)(2,1)}, ...), condition=%wide.region_19.20_spmd, body=%wide.region_15.19_spmd.sunk | while | flops 1376122880 | bytes 131193600 | solution.py:314
  734.1 24.1 %while.58 = (s32[]{:T(128)}, f32[1024,4,64]{0,2,1:T(8,128)S(1)}, f32[1024,4,64]{0,2,1:T(8,128)}, bf16[2,512,4,64]{1,3,2,0:T(8,128)(2,1)}, bf16[2,512,4,64]{1,3,2...) while((s32[]{:T(128)}, f32[1024,4,64]{0,2,1:T(8,128)S(1)}, ...), condition=%wide.region_18.18_spmd.clone, body=%wide.region_16.17_spmd.clone.sunk | while | flops 1375598592 | bytes 85002520 | solution.py:179
  771.6 24.1 %while.58 = (s32[]{:T(128)}, f32[1024,4,64]{0,2,1:T(8,128)S(1)}, f32[1024,4,64]{0,2,1:T(8,128)}, bf16[2,512,4,64]{1,3,2,0:T(8,128)(2,1)}, bf16[2,512,4,64]{1,3,2...) while((s32[]{:T(128)}, f32[1024,4,64]{0,2,1:T(8,128)S(1)}, ...), condition=%wide.region_18.18_spmd.clone, body=%wide.region_16.17_spmd.clone.sunk | while | flops 1375598592 | bytes 85002520 | solution.py:179
  810.0 11.0 all-to-all-done.7
  828.6 9.4 all-to-all-done.5
  865.5 11.1 pad_maximum_fusion
  882.5 6.4 constant_dynamic-update-slice_fusion.5
  899.9 6.7 convolution_convert_fusion.2
  907.9 12.8 convolution_convert_fusion
  922.0 9.2 convolution_convert_fusion.1
  939.3 7.5 fusion.66
  946.8 12.7 bitcast_convert_fusion
  962.4 64.7 %reduce-scatter.21.cloned.1.call-done = bf16[1024,768]{1,0:T(8,128)(2,1)} async-done(((bf16[1024,3072]{1,0:T(8,128)(2,1)}), bf16[1024,768]{1,0:T(8,128)(2,1)}) %reduce-scatter.21.cloned.1.call-update) | async-done | bytes 1572880 | tf_op jit(solution)/shard_map/reduce_scatter | solution.py:356
  1027.2 89.3 %reduce-scatter.31.cloned.1.call-done = bf16[1024,1024]{1,0:T(8,128)(2,1)} async-done(((bf16[4096,1024]{1,0:T(8,128)(2,1)}), bf16[1024,1024]{1,0:T(8,128)(2,1)}) %reduce-scatter.31.cloned.1.call-update) | async-done | bytes 2097168 | tf_op jit(solution)/shard_map/reduce_scatter | solution.py:365
  1120.5 85.6 %reduce-scatter.27.cloned.1.call-done = bf16[1024,1024]{1,0:T(8,128)(2,1)} async-done(((bf16[1024,4096]{1,0:T(8,128)(2,1)}), bf16[1024,1024]{1,0:T(8,128)(2,1)}) %reduce-scatter.27.cloned.1.call-update) | async-done | bytes 2097168 | tf_op jit(solution)/shard_map/reduce_scatter | solution.py:362
  1206.2 123.6 %reduce-scatter.33.cloned.1.call-done = bf16[1024,1536]{1,0:T(8,128)(2,1)} async-done(((bf16[1024,6144]{1,0:T(8,128)(2,1)}), bf16[1024,1536]{1,0:T(8,128)(2,1)}) %reduce-scatter.33.cloned.1.call-update) | async-done | bytes 3145744 | tf_op jit(solution)/shard_map/reduce_scatter | solution.py:368
  1335.9 27.5 %reduce-scatter.37.cloned.1.call-done = bf16[128,256]{1,0:T(8,128)(2,1)} async-done(((bf16[1024,256]{1,0:T(8,128)(2,1)}), bf16[128,256]{1,0:T(8,128)(2,1)}) %reduce-scatter.37.cloned.1.call-update) | async-done | bytes 65552
  1365.1 31.1 %reduce-scatter.19.cloned.1.call-done = bf16[256,256]{1,0:T(8,128)(2,1)} async-done(((bf16[2048,256]{1,0:T(8,128)(2,1)}), bf16[256,256]{1,0:T(8,128)(2,1)}) %reduce-scatter.19.cloned.1.call-update) | async-done | bytes 131088 | tf_op jit(solution)/shard_map/reduce_scatter | solution.py:373
  1397.8 33.4 %reduce-scatter.23.cloned.1.call-done = bf16[128,768]{1,0:T(8,128)(2,1)} async-done(((bf16[1024,768]{1,0:T(8,128)(2,1)}), bf16[128,768]{1,0:T(8,128)(2,1)}) %reduce-scatter.23.cloned.1.call-update) | async-done | bytes 196624 | tf_op jit(solution)/shard_map/reduce_scatter | solution.py:376
  1432.9 34.5 %reduce-scatter.39.cloned.1.call-done = bf16[128,1024]{1,0:T(8,128)(2,1)} async-done(((bf16[1024,1024]{1,0:T(8,128)(2,1)}), bf16[128,1024]{1,0:T(8,128)(2,1)}) %reduce-scatter.39.cloned.1.call-update) | async-done | bytes 262160
  1469.4 34.8 %reduce-scatter.29.cloned.1.call-done = bf16[128,1024]{1,0:T(8,128)(2,1)} async-done(((bf16[1024,1024]{1,0:T(8,128)(2,1)}), bf16[128,1024]{1,0:T(8,128)(2,1)}) %reduce-scatter.29.cloned.1.call-update) | async-done | bytes 262160 | tf_op jit(solution)/shard_map/reduce_scatter | solution.py:382
  1506.0 39.6 %reduce-scatter.35.cloned.1.call-done = bf16[128,1536]{1,0:T(8,128)(2,1)} async-done(((bf16[1024,1536]{1,0:T(8,128)(2,1)}), bf16[128,1536]{1,0:T(8,128)(2,1)}) %reduce-scatter.35.cloned.1.call-update) | async-done | bytes 393232 | tf_op jit(solution)/shard_map/reduce_scatter | solution.py:388
  (481 shorter events, 299.3 us)
Async XLA Ops:
  7.2 93.3 %copy-start.52 = (bf16[256,128]{1,0:T(8,128)(2,1)S(1)}, bf16[256,128]{1,0:T(8,128)(2,1)}, u32[]{:S(2)}) copy-start(bf16[256,128]{1,0:T(8,128)(2,1)} %param.29) | copy-start | bytes 196612
  7.2 27.3 %all-gather.12.cloned.1.call-start = ((), (), s32[]{:S(2)}) async-start(), calls=%async_computation.20 | async-start | bytes 1179648 | tf_op jit(solution)/shard_map/all_gather | solution.py:230
  7.9 66.1 %all-gather.16.cloned.1.call-start = ((), (), s32[]{:S(2)}) async-start(), calls=%async_computation.22 | async-start | bytes 3538944 | tf_op jit(solution)/shard_map/all_gather | solution.py:235
  8.7 91.0 %all-gather.20.cloned.1.call-start = ((), (), s32[]{:S(2)}) async-start(), calls=%async_computation.24 | async-start | bytes 1769472 | tf_op jit(solution)/shard_map/all_gather | solution.py:231
  9.4 123.1 %all-gather.30.cloned.1.call-start = ((), (), s32[]{:S(2)}) async-start(), calls=%async_computation.29 | async-start | bytes 2359296 | tf_op jit(solution)/shard_map/all_gather | solution.py:234
  10.0 175.5 %all-gather.14.cloned.1.call-start = ((), (), s32[]{:S(2)}) async-start(), calls=%async_computation.21 | async-start | bytes 5242880 | tf_op jit(solution)/shard_map/all_gather | solution.py:238
  34.5 98.0 %copy-start.65 = (s32[2,3]{1,0:T(2,128)S(1)}, s32[2,3]{1,0:T(2,128)}, u32[]{:S(2)}) copy-start(s32[2,3]{1,0:T(2,128)} %param.25) | copy-start | bytes 76
  34.5 115.2 %copy-start.59 = (s32[2,256]{1,0:T(2,128)S(1)}, s32[2,256]{1,0:T(2,128)}, u32[]{:S(2)}) copy-start(s32[2,256]{1,0:T(2,128)} %param.24) | copy-start | bytes 6148
  34.5 115.9 %copy-start.66 = (f32[2,3]{1,0:T(2,128)S(1)}, f32[2,3]{1,0:T(2,128)}, u32[]{:S(2)}) copy-start(f32[2,3]{1,0:T(2,128)} %param.26) | copy-start | bytes 76
  34.5 275.2 %all-gather.18.cloned.1.call-start = ((), (), s32[]{:S(2)}) async-start(), calls=%async_computation.23 | async-start | bytes 15728640 | tf_op jit(solution)/shard_map/all_gather | solution.py:243
  74.0 77.4 %copy-start.41 = (bf16[2,256,1024]{2,1,0:T(8,128)(2,1)S(1)}, bf16[2,256,1024]{2,1,0:T(8,128)(2,1)}, u32[]{:S(2)}) copy-start(bf16[2,256,1024]{2,1,0:T(8,128)(2,1)} %param.22) | copy-start | bytes 3145732
  74.0 77.4 %copy-start.42 = (bf16[2,256,1024]{2,1,0:T(8,128)(2,1)S(1)}, bf16[2,256,1024]{2,1,0:T(8,128)(2,1)}, u32[]{:S(2)}) copy-start(bf16[2,256,1024]{2,1,0:T(8,128)(2,1)} %param.21) | copy-start | bytes 3145732
  74.1 307.7 %all-gather.22.cloned.1.call-start = ((), (), s32[]{:S(2)}) async-start(), calls=%async_computation.25 | async-start | bytes 7864320 | tf_op jit(solution)/shard_map/all_gather | solution.py:239
  99.7 372.1 %all-gather.26.cloned.1.call-start = ((), (), s32[]{:S(2)}) async-start(), calls=%async_computation.27 | async-start | bytes 2359296 | tf_op jit(solution)/shard_map/all_gather | solution.py:233
  100.4 461.8 %all-gather.24.cloned.1.call-start = ((), (), s32[]{:S(2)}) async-start(), calls=%async_computation.26 | async-start | bytes 2621440 | tf_op jit(solution)/shard_map/all_gather | solution.py:240
  115.6 457.0 %all-gather.32.cloned.1.call-start = ((), (), s32[]{:S(2)}) async-start(), calls=%async_computation.30 | async-start | bytes 10485760 | tf_op jit(solution)/shard_map/all_gather | solution.py:242
  150.6 159.1 %copy-start.47 = (f32[2,3,512]{2,1,0:T(4,128)}, f32[2,3,512]{2,1,0:T(4,128)S(1)}, u32[]{:S(2)}) copy-start(f32[2,3,512]{2,1,0:T(4,128)S(1)} %get-tuple-element.439) | copy-start | bytes 36868
  150.7 159.1 %copy-start.49 = (f32[2,3,512]{2,1,0:T(4,128)}, f32[2,3,512]{2,1,0:T(4,128)S(1)}, u32[]{:S(2)}) copy-start(f32[2,3,512]{2,1,0:T(4,128)S(1)} %get-tuple-element.440) | copy-start | bytes 36868
  151.5 259.0 %copy-start.45 = (f32[256,32]{0,1:T(8,128)}, f32[256,32]{0,1:T(8,128)S(1)}, u32[]{:S(2)}) copy-start(f32[256,32]{0,1:T(8,128)S(1)} %get-tuple-element.445) | copy-start | bytes 98308
  191.0 128.1 %copy-start.6 = (f32[512,1024]{1,0:T(8,128)}, f32[512,1024]{1,0:T(8,128)S(1)}, u32[]{:S(2)}) copy-start(f32[512,1024]{1,0:T(8,128)S(1)} %get-tuple-element.449) | copy-start | bytes 6291460
  191.0 128.1 %copy-start.53 = (f32[512]{0:T(512)}, f32[512]{0:T(512)S(1)}, u32[]{:S(2)}) copy-start(f32[512]{0:T(512)S(1)} %broadcast_multiply_fusion.1) | copy-start | bytes 6148
  191.4 124.8 %copy-start.60 = (f32[512]{0:T(512)}, f32[512]{0:T(512)S(1)}, u32[]{:S(2)}) copy-start(f32[512]{0:T(512)S(1)} %multiply_reduce_fusion.4) | copy-start | bytes 6148
  191.4 127.7 %copy-start.57 = (f32[512]{0:T(512)}, f32[512]{0:T(512)S(1)}, u32[]{:S(2)}) copy-start(f32[512]{0:T(512)S(1)} %fusion.68) | copy-start | bytes 6148
  324.7 66.8 %copy-start.37 = (bf16[512,1024]{1,0:T(8,128)(2,1)}, bf16[512,1024]{1,0:T(8,128)(2,1)S(1)}, u32[]{:S(2)}) copy-start(bf16[512,1024]{1,0:T(8,128)(2,1)S(1)} %fusion.56) | copy-start | bytes 3145732
  403.3 17.5 %all-to-all-start.2 = ((bf16[2,256,1024]{1,0,2:T(2,128)(2,1)}), bf16[2,256,1024]{1,0,2:T(2,128)(2,1)S(1)}, u32[]{:S(2)}, u32[]{:S(2)}) async-start(bf16[2,256,1024]{1,0,2:T(2,128)(2,1)} %bitcast.29), calls=%async_computation.2 | async-start | bytes 2097152 | tf_op jit(solution)/shard_map/all_to_all | solution.py:282
  420.8 20.4 %all-to-all-start.1 = ((bf16[2,256,1024]{1,0,2:T(2,128)(2,1)}), bf16[2,256,1024]{1,0,2:T(2,128)(2,1)S(1)}, u32[]{:S(2)}, u32[]{:S(2)}) async-start(bf16[2,256,1024]{1,0,2:T(2,128)(2,1)} %bitcast.26), calls=%async_computation.1 | async-start | bytes 2097152 | tf_op jit(solution)/shard_map/all_to_all | solution.py:279
  441.2 34.2 %all-to-all-start = ((bf16[2,256,1024]{1,0,2:T(2,128)(2,1)}), bf16[2,256,1024]{1,0,2:T(2,128)(2,1)}, u32[]{:S(2)}, u32[]{:S(2)}) async-start(bf16[2,256,1024]{1,0,2:T(2,128)(2,1)} %bitcast.22), calls=%async_computation | async-start | bytes 2097152 | tf_op jit(solution)/shard_map/all_to_all | solution.py:276
  445.5 212.6 %all-gather.28.cloned.1.call-start = ((), (), s32[]{:S(2)}) async-start(), calls=%async_computation.28 | async-start | bytes 10485760 | tf_op jit(solution)/shard_map/all_gather | solution.py:241
  568.1 116.3 %copy-start.55 = (f32[512]{0:T(512)}, f32[512]{0:T(512)S(1)}, u32[]{:S(2)}) copy-start(f32[512]{0:T(512)S(1)} %broadcast_multiply_fusion) | copy-start | bytes 6148
  570.7 113.8 %copy-start.62 = (f32[512]{0:T(512)}, f32[512]{0:T(512)S(1)}, u32[]{:S(2)}) copy-start(f32[512]{0:T(512)S(1)} %fusion.69) | copy-start | bytes 6148
  702.2 17.4 %all-to-all-start.4 = ((bf16[2,256,1024]{1,0,2:T(2,128)(2,1)}), bf16[2,256,1024]{1,0,2:T(2,128)(2,1)S(1)}, u32[]{:S(2)}, u32[]{:S(2)}) async-start(bf16[2,256,1024]{1,0,2:T(2,128)(2,1)} %copy.102), calls=%async_computation.4 | async-start | bytes 2097152 | tf_op jit(solution)/shard_map/all_to_all | solution.py:311
  804.4 16.6 %all-to-all-start.7 = ((bf16[2,1024,256]{2,0,1:T(2,128)(2,1)}), bf16[2,1024,256]{2,0,1:T(2,128)(2,1)S(1)}, u32[]{:S(2)}, u32[]{:S(2)}) async-start(bf16[2,1024,256]{2,0,1:T(2,128)(2,1)} %copy.115), calls=%async_computation.7 | async-start | bytes 2097152 | tf_op jit(solution)/shard_map/all_to_all | solution.py:320
  808.0 34.6 %copy-start.25 = (bf16[64,8,4,256]{3,1,2,0:T(8,128)(2,1)S(1)}, bf16[64,8,4,256]{3,1,2,0:T(8,128)(2,1)}, u32[]{:S(2)}) copy-start(bf16[64,8,4,256]{3,1,2,0:T(8,128)(2,1)} %copy.141) | copy-start | bytes 3145732
  821.0 17.0 %all-to-all-start.5 = ((bf16[2,1024,256]{2,0,1:T(2,128)(2,1)}), bf16[2,1024,256]{2,0,1:T(2,128)(2,1)S(1)}, u32[]{:S(2)}, u32[]{:S(2)}) async-start(bf16[2,1024,256]{2,0,1:T(2,128)(2,1)} %copy.105), calls=%async_computation.5 | async-start | bytes 2097152 | tf_op jit(solution)/shard_map/all_to_all | solution.py:318
  839.0 17.2 %all-to-all-start.6 = ((bf16[2,1024,256]{2,0,1:T(2,128)(2,1)}), bf16[2,1024,256]{2,0,1:T(2,128)(2,1)S(1)}, u32[]{:S(2)}, u32[]{:S(2)}) async-start(bf16[2,1024,256]{2,0,1:T(2,128)(2,1)} %copy.110), calls=%async_computation.6 | async-start | bytes 2097152 | tf_op jit(solution)/shard_map/all_to_all | solution.py:319
  842.5 117.0 %reduce-scatter.25.cloned.1.call-start = ((), (), s32[]{:S(2)}) async-start(), calls=%async_computation.35 | async-start | bytes 2621440 | tf_op jit(solution)/shard_map/reduce_scatter | solution.py:359
  846.4 115.3 %reduce-scatter.17.cloned.1.call-start = ((), (), s32[]{:S(2)}) async-start(), calls=%async_computation.31 | async-start | bytes 5242880 | tf_op jit(solution)/shard_map/reduce_scatter | solution.py:353
  899.9 127.3 %reduce-scatter.21.cloned.1.call-start = ((), (), s32[]{:S(2)}) async-start(), calls=%async_computation.33 | async-start | bytes 7864320 | tf_op jit(solution)/shard_map/reduce_scatter | solution.py:356
  906.7 209.8 %reduce-scatter.31.cloned.1.call-start = ((), (), s32[]{:S(2)}) async-start(), calls=%async_computation.38 | async-start | bytes 10485760 | tf_op jit(solution)/shard_map/reduce_scatter | solution.py:365
  920.8 285.3 %reduce-scatter.27.cloned.1.call-start = ((), (), s32[]{:S(2)}) async-start(), calls=%async_computation.36 | async-start | bytes 10485760 | tf_op jit(solution)/shard_map/reduce_scatter | solution.py:362
  931.3 398.6 %reduce-scatter.33.cloned.1.call-start = ((), (), s32[]{:S(2)}) async-start(), calls=%async_computation.39 | async-start | bytes 15728640 | tf_op jit(solution)/shard_map/reduce_scatter | solution.py:368
  959.5 404.0 %reduce-scatter.37.cloned.1.call-start = ((), (), s32[]{:S(2)}) async-start(), calls=%async_computation.41 | async-start | bytes 589824
  961.6 434.6 %reduce-scatter.19.cloned.1.call-start = ((), (), s32[]{:S(2)}) async-start(), calls=%async_computation.32 | async-start | bytes 1179648 | tf_op jit(solution)/shard_map/reduce_scatter | solution.py:373
  962.4 468.9 %reduce-scatter.23.cloned.1.call-start = ((), (), s32[]{:S(2)}) async-start(), calls=%async_computation.34 | async-start | bytes 1769472 | tf_op jit(solution)/shard_map/reduce_scatter | solution.py:376
  1027.2 440.3 %reduce-scatter.39.cloned.1.call-start = ((), (), s32[]{:S(2)}) async-start(), calls=%async_computation.42 | async-start | bytes 2359296
  1120.4 209.4 %copy-start.40 = (bf16[512,1024]{1,0:T(8,128)(2,1)S(1)}, bf16[512,1024]{1,0:T(8,128)(2,1)}, u32[]{:S(2)}) copy-start(bf16[512,1024]{1,0:T(8,128)(2,1)} %copy-done.39) | copy-start | bytes 3145732
  1120.4 383.7 %reduce-scatter.29.cloned.1.call-start = ((), (), s32[]{:S(2)}) async-start(), calls=%async_computation.37 | async-start | bytes 2359296 | tf_op jit(solution)/shard_map/reduce_scatter | solution.py:382
  1206.1 339.5 %reduce-scatter.35.cloned.1.call-start = ((), (), s32[]{:S(2)}) async-start(), calls=%async_computation.40 | async-start | bytes 3538944 | tf_op jit(solution)/shard_map/reduce_scatter | solution.py:388
  (80 other events, 264.7 us)
Sparse Core Ops, SparseCore 0:
  9.6 24.7 all-gather.11
  36.1 37.8 all-gather.15
  75.7 23.9 all-gather.19
  101.1 31.3 all-gather.29
  134.1 51.2 all-gather.13
  187.2 122.5 all-gather.17
  311.6 70.1 all-gather.21
  383.4 29.0 all-gather.25
  414.4 54.4 all-gather.23
  470.6 97.9 all-gather.31
  570.4 87.6 all-gather.27
  846.5 36.5 reduce-scatter.24
  900.0 54.0 reduce-scatter.16
  956.9 70.1 reduce-scatter.20
  1030.1 86.3 reduce-scatter.30
  1119.7 86.3 reduce-scatter.26
  1209.1 120.7 reduce-scatter.32
  1332.5 30.9 reduce-scatter.36
  1365.9 30.2 reduce-scatter.18
  1398.5 32.7 reduce-scatter.22
  1433.6 33.7 reduce-scatter.38
  1469.9 34.2 reduce-scatter.28
  1506.6 38.9 reduce-scatter.34
where the time goes:
time: 1570 us; the launch traced here: 1550 us
  waiting for transfers between devices  1010 us (64%)
  matrix products  201 us (13%)
  local copies, waits for them, and re-layouts  133 us (8%)
  blocking collectives  84.7 us (5%)
  other arithmetic  78.7 us (5%)
  starting transfers between devices  27.2 us (2%)
  between operations  16.7 us (1%)
    reduce_scatter x1, waiting for transfers between devices, body(): lax.psum_scatter(grad_w_mod.astype(jnp.bfloat16), 'seq', scatter_dimensio...  124 us
    all_gather x1, waiting for transfers between devices, body(): lax.all_gather(mod_dp, 'seq', axis=1, tiled=True)  118 us
    reduce_scatter x1, waiting for transfers between devices, body(): lax.psum_scatter(grad_w_down.astype(jnp.bfloat16), 'seq', scatter_dimensi...  89.3 us
    reduce_scatter x1, waiting for transfers between devices, body(): lax.psum_scatter(grad_w_up.astype(jnp.bfloat16), 'seq', scatter_dimension...  85.6 us
    all_gather x1, waiting for transfers between devices, body(): lax.all_gather(up_dp, 'seq', axis=1, tiled=True)  74 us
    unnamed x25, waiting for transfers between devices  66.3 us
    reduce_scatter x1, waiting for transfers between devices, body(): lax.psum_scatter(grad_w_qkv.astype(jnp.bfloat16), 'seq', scatter_dimensio...  64.7 us
    all_gather x1, waiting for transfers between devices, body(): lax.all_gather(qkv_dp, 'seq', axis=1, tiled=True)  57.1 us
  transfers between devices with their start and end apart: 30, of which 23 were waited for; matrix products, arithmetic and copies ran while one was open for 17% of the time, Pallas kernels for 0%

commit v1 on v0

v1 whole, which is shorter than its diff:
```python
import functools
import math

import jax
import jax.numpy as jnp
from jax import lax
from jax.experimental import pallas as pl
from jax.experimental.pallas import tpu as pltpu
from jax.sharding import PartitionSpec as P

HEADS = 16
CORES = 2
EPSILON = 1e-06
MASKED = -1e30
VMEM_LIMIT = 60 * 1024 * 1024
F32 = jnp.float32
BF16 = jnp.bfloat16
NT = (((1,), (1,)), ((), ()))
TN = (((0,), (0,)), ((), ()))


def dot(left, right):
    return jnp.dot(left, right, preferred_element_type=F32)


def against(left, right):
    return lax.dot_general(left, right, NT, preferred_element_type=F32)


def over_rows(left, right):
    return lax.dot_general(left, right, TN, preferred_element_type=F32)


def swap(values, axis, mask):
    return lax.ppermute(values, axis, [(i, i ^ mask) for i in range(lax.axis_size(axis))])


def chip_masks():
    return [CORES * k for k in range(1, lax.axis_size("dp") // CORES)]


def seq_halves():
    count = lax.axis_size("seq")
    fast = 1
    while fast * fast < count:
        fast *= 2
    slow = count // fast
    return [list(range(1, fast)), [fast * k for k in range(1, slow)]]


def gather_steps(shard, steps):
    held = shard
    for axis, masks in steps:
        held = jnp.stack([held] + [swap(held, axis, mask) for mask in masks])
    return held


def assemble_kernel(steps, rows, columns, relative, place_ref, mine_ref, other_ref, out_ref, sems):
    lead = mine_ref.shape[:-2]
    copies = []
    for flat in range(math.prod(lead)):
        index, rest = [], flat
        for size in reversed(lead):
            index.insert(0, rest % size)
            rest //= size
        dp_mask, seq_mask = 0, 0
        for position, (axis, masks) in zip(index, reversed(steps)):
            mask = ([0] + masks)[position]
            if axis == "dp":
                dp_mask ^= mask
            else:
                seq_mask ^= mask
        for core, source in ((0, mine_ref), (1, other_ref)):
            row = pl.multiple_of((place_ref[0] ^ (dp_mask ^ core)) * rows, rows)
            if relative == "blocks":
                target = out_ref.at[seq_mask, pl.ds(row, rows), :]
            elif relative == "columns":
                target = out_ref.at[pl.ds(row, rows), pl.ds(seq_mask * columns, columns)]
            elif len(steps) == 1:
                target = out_ref.at[pl.ds(row, rows), :]
            else:
                column = pl.multiple_of((place_ref[1] ^ seq_mask) * columns, columns)
                target = out_ref.at[pl.ds(row, rows), pl.ds(column, columns)]
            copies.append(pltpu.make_async_copy(source.at[tuple(index)], target, sems.at[len(copies)]))
    for copy in copies:
        copy.start()
    for copy in copies:
        copy.wait()


def fetch(shard, place, seq_order, relative):
    rows, columns = shard.shape
    dp_size, seq_size = lax.axis_size("dp"), lax.axis_size("seq")
    seqs = 1 if seq_order is None else seq_size
    if columns % 128 and seqs > 1:
        held = lax.all_gather(lax.all_gather(shard, "dp", axis=0, tiled=True), "seq", axis=0)
        if relative:
            held = jnp.take(held, jnp.arange(seqs) ^ place[1], axis=0)
        if relative == "blocks":
            return held
        return jnp.moveaxis(held, 0, 1).reshape(dp_size * rows, seqs * columns)
    steps = [("dp", chip_masks())]
    if seqs > 1:
        halves = seq_halves()
        steps += [("seq", halves[k]) for k in seq_order]
    mine = gather_steps(shard, steps)
    other = swap(mine, "dp", 1)
    if relative == "blocks":
        shape = (seqs, dp_size * rows, columns)
    else:
        shape = (dp_size * rows, seqs * columns)
    return pl.pallas_call(
        functools.partial(assemble_kernel, steps, rows, columns, relative),
        out_shape=jax.ShapeDtypeStruct(shape, shard.dtype),
        in_specs=[
            pl.BlockSpec(memory_space=pltpu.SMEM),
            pl.BlockSpec(memory_space=pl.ANY),
            pl.BlockSpec(memory_space=pl.ANY),
        ],
        out_specs=pl.BlockSpec(memory_space=pltpu.VMEM),
        scratch_shapes=[pltpu.SemaphoreType.DMA((dp_size * seqs,))],
        compiler_params=pltpu.CompilerParams(vmem_limit_bytes=VMEM_LIMIT),
        cost_estimate=pl.CostEstimate(flops=0, bytes_accessed=4 * dp_size * seqs * rows * columns, transcendentals=0),
        name="assemble",
    )(place, mine, other)


def pick(values, index, axis):
    return lax.dynamic_index_in_dim(values, index, axis, keepdims=False)


def reduce_weight(blocks, rows, dp):
    chips = lax.axis_size("dp") // CORES
    core, chip = dp % CORES, dp // CORES
    columns = blocks[0].shape[-1]
    shaped = [block.reshape(chips, CORES, rows, columns) for block in blocks]
    give = jnp.stack([pick(block, 1 - core, 1).astype(BF16) for block in shaped])
    got = swap(give, "dp", 1)
    held = [pick(block, core, 1).astype(F32) + got[m].astype(F32) for m, block in enumerate(shaped)]
    if len(held) > 1:
        fast, slow = seq_halves()
        sent = {}
        for mask in fast:
            sent[mask] = swap(jnp.stack([held[s ^ mask] for s in [0] + slow]).astype(BF16), "seq", mask)
        kept = []
        for position, base in enumerate([0] + slow):
            total = held[base]
            for mask in fast:
                total = total + sent[mask][position].astype(F32)
            kept.append(total)
        total = kept[0]
        for position, mask in enumerate(slow):
            total = total + swap(kept[1 + position].astype(BF16), "seq", mask).astype(F32)
    else:
        total = held[0]
    result = pick(total, chip, 0)
    for mask in chip_masks():
        result = result + swap(pick(total, chip ^ (mask // CORES), 0).astype(BF16), "dp", mask).astype(F32)
    return result


def qkv_kernel(width, scale, x_ref, w_ref, cos_ref, sin_ref, *rest):
    out_ref = rest[-1]
    half = width // 2
    projected = dot(x_ref[0], w_ref[...])
    cosine, sine = cos_ref[0], sin_ref[0]
    for part, factor in ((0, scale), (1, 1.0)):
        low = projected[:, part * width : part * width + half]
        high = projected[:, part * width + half : (part + 1) * width]
        out_ref[0, 0, :, part * width : part * width + half] = ((low * cosine - high * sine) * factor).astype(BF16)
        out_ref[0, 0, :, part * width + half : (part + 1) * width] = ((high * cosine + low * sine) * factor).astype(BF16)
    out_ref[0, 0, :, 2 * width :] = projected[:, 2 * width :].astype(BF16)


def project_piece(piece, normed, weights, cos_table, sin_table, held, scale):
    rows, frames, model = normed.shape
    pieces = cos_table.shape[0]
    width = weights.shape[1] // 3
    in_specs = [
        pl.BlockSpec((1, frames, model), lambda r: (r, 0, 0)),
        pl.BlockSpec((model, 3 * width), lambda r: (0, 0)),
        pl.BlockSpec((1, frames, width // 2), lambda r: (piece, 0, 0)),
        pl.BlockSpec((1, frames, width // 2), lambda r: (piece, 0, 0)),
    ]
    arrays = [normed, weights, cos_table, sin_table]
    aliases = {}
    if held is not None:
        in_specs.append(pl.BlockSpec(memory_space=pl.ANY))
        arrays.append(held)
        aliases = {4: 0}
    return pl.pallas_call(
        functools.partial(qkv_kernel, width, scale),
        grid=(rows,),
        out_shape=jax.ShapeDtypeStruct((pieces, rows, frames, 3 * width), BF16),
        in_specs=in_specs,
        out_specs=pl.BlockSpec((1, 1, frames, 3 * width), lambda r: (piece, r, 0, 0)),
        input_output_aliases=aliases,
        compiler_params=pltpu.CompilerParams(vmem_limit_bytes=VMEM_LIMIT),
        cost_estimate=pl.CostEstimate(
            flops=2 * rows * frames * model * 3 * width, bytes_accessed=5 * rows * frames * model, transcendentals=0
        ),
        name="project",
    )(*arrays)


def head_lanes(shape, heads, width, split):
    lane = lax.broadcasted_iota(jnp.int32, shape, 1)
    size = width // heads
    if split:
        return (lane % (width // 2)) // (size // 2)
    return lane // size


def attend_kernel(heads, width, qkv_ref, seg_col_ref, seg_row_ref, out_ref, lse_ref, vt_ref, ot_ref):
    pieces, _, frames, _ = qkv_ref.shape
    length = pieces * frames
    step = pl.program_id(1)
    size = width // heads
    keys = qkv_ref[:, 0, :, width : 2 * width].reshape(length, width)

    @pl.when(step == 0)
    def _():
        vt_ref[...] = qkv_ref[:, 0, :, 2 * width :].reshape(length, width).T

    queries = qkv_ref[step, 0, :, :width]
    owner = head_lanes((frames, width), heads, width, True)
    allowed = seg_col_ref[0] == seg_row_ref[0, 0]
    for head in range(heads):
        masked = jnp.where(owner == head, queries, jnp.zeros_like(queries))
        scores = jnp.where(allowed, against(keys, masked), MASKED)
        highest = jnp.max(scores, 0, keepdims=True)
        raised = jnp.exp(scores - highest)
        total = jnp.sum(raised, 0, keepdims=True)
        lse_ref[0, 0, head : head + 1, :] = highest + jnp.log(total)
        result = dot(vt_ref[head * size : (head + 1) * size, :], raised.astype(BF16))
        ot_ref[head * size : (head + 1) * size, :] = result / total
    out_ref[0, 0] = ot_ref[...].T.astype(BF16)


def attend(qkv, seg_col, seg_row, heads):
    pieces, rows, frames, triple = qkv.shape
    width = triple // 3
    length = pieces * frames
    return pl.pallas_call(
        functools.partial(attend_kernel, heads, width),
        grid=(rows, pieces),
        out_shape=(
            jax.ShapeDtypeStruct((pieces, rows, frames, width), BF16),
            jax.ShapeDtypeStruct((rows, pieces, heads, frames), F32),
        ),
        in_specs=[
            pl.BlockSpec((pieces, 1, frames, triple), lambda r, s: (0, r, 0, 0)),
            pl.BlockSpec((1, length, 1), lambda r, s: (r, 0, 0)),
            pl.BlockSpec((1, 1, 1, frames), lambda r, s: (r, s, 0, 0)),
        ],
        out_specs=(
            pl.BlockSpec((1, 1, frames, width), lambda r, s: (s, r, 0, 0)),
            pl.BlockSpec((1, 1, heads, frames), lambda r, s: (r, s, 0, 0)),
        ),
        scratch_shapes=[pltpu.VMEM((width, length), BF16), pltpu.VMEM((width, frames), F32)],
        compiler_params=pltpu.CompilerParams(vmem_limit_bytes=VMEM_LIMIT),
        cost_estimate=pl.CostEstimate(
            flops=4 * rows * length * length * 256 * heads,
            bytes_accessed=8 * rows * length * width,
            transcendentals=rows * heads * length * length,
        ),
        name="attend",
    )(qkv, seg_col, seg_row)


def attend_back_kernel(
    heads, width, scale, qkv_ref, seg_col_ref, seg_row_ref, out_ref, lse_ref, grad_ref, cos_ref, sin_ref,
    result_ref, kt_ref, dk_ref, dv_ref, dqt_ref,
):
    pieces, _, frames, _ = qkv_ref.shape
    length = pieces * frames
    step = pl.program_id(1)
    size, half = width // heads, width // 2
    keys = qkv_ref[:, 0, :, width : 2 * width].reshape(length, width)
    values = qkv_ref[:, 0, :, 2 * width :].reshape(length, width)

    @pl.when(step == 0)
    def _():
        kt_ref[...] = keys.T
        dk_ref[...] = jnp.zeros_like(dk_ref)
        dv_ref[...] = jnp.zeros_like(dv_ref)

    queries = qkv_ref[step, 0, :, :width]
    grad = grad_ref[0, 0]
    query_owner = head_lanes((frames, width), heads, width, True)
    value_owner = head_lanes((frames, width), heads, width, False)
    allowed = seg_col_ref[0] == seg_row_ref[0, 0]
    product = grad.astype(F32) * out_ref[0, 0].astype(F32)
    picker = lax.broadcasted_iota(jnp.int32, (8, width), 1) // size == lax.broadcasted_iota(jnp.int32, (8, width), 0)
    inner = lax.dot_general(
        picker.astype(F32), product, NT, precision=lax.Precision.HIGHEST, preferred_element_type=F32
    )
    for head in range(heads):
        masked = jnp.where(query_owner == head, queries, jnp.zeros_like(queries))
        masked_grad = jnp.where(value_owner == head, grad, jnp.zeros_like(grad))
        scores = against(keys, masked)
        weights = jnp.where(allowed, jnp.exp(scores - lse_ref[0, 0, head : head + 1, :]), 0.0)
        grad_weights = against(values, masked_grad)
        grad_scores = (weights * (grad_weights - inner[head : head + 1, :])).astype(BF16)
        dv_ref[...] += dot(weights.astype(BF16), masked_grad)
        dk_ref[...] += dot(grad_scores, masked)
        low, high = head * size // 2, half + head * size // 2
        head_keys = jnp.concatenate([kt_ref[low : low + size // 2, :], kt_ref[high : high + size // 2, :]], 0)
        part = dot(head_keys, grad_scores)
        dqt_ref[low : low + size // 2, :] = part[: size // 2]
        dqt_ref[high : high + size // 2, :] = part[size // 2 :]

    def unrotate(values, cosine, sine):
        low, high = values[:, :half], values[:, half:]
        return (low * cosine + high * sine).astype(BF16), (high * cosine - low * sine).astype(BF16)

    low, high = unrotate(dqt_ref[...].T * scale, cos_ref[step], sin_ref[step])
    result_ref[step, 0, :, :half] = low
    result_ref[step, 0, :, half:width] = high

    @pl.when(step == pieces - 1)
    def _():
        for piece in range(pieces):
            span = slice(piece * frames, (piece + 1) * frames)
            low, high = unrotate(dk_ref[span, :], cos_ref[piece], sin_ref[piece])
            result_ref[piece, 0, :, width : width + half] = low
            result_ref[piece, 0, :, width + half : 2 * width] = high
            result_ref[piece, 0, :, 2 * width :] = dv_ref[span, :].astype(BF16)


def attend_back(qkv, seg_col, seg_row, out, lse, grad, cos_table, sin_table, heads, scale):
    pieces, rows, frames, triple = qkv.shape
    width = triple // 3
    length = pieces * frames
    whole = pl.BlockSpec((pieces, 1, frames, triple), lambda r, s: (0, r, 0, 0))
    table = pl.BlockSpec((pieces, frames, width // 2), lambda r, s: (0, 0, 0))
    block = pl.BlockSpec((1, 1, frames, width), lambda r, s: (s, r, 0, 0))
    return pl.pallas_call(
        functools.partial(attend_back_kernel, heads, width, scale),
        grid=(rows, pieces),
        out_shape=jax.ShapeDtypeStruct(qkv.shape, BF16),
        in_specs=[
            whole,
            pl.BlockSpec((1, length, 1), lambda r, s: (r, 0, 0)),
            pl.BlockSpec((1, 1, 1, frames), lambda r, s: (r, s, 0, 0)),
            block,
            pl.BlockSpec((1, 1, heads, frames), lambda r, s: (r, s, 0, 0)),
            block,
            table,
            table,
        ],
        out_specs=whole,
        scratch_shapes=[
            pltpu.VMEM((width, length), BF16),
            pltpu.VMEM((length, width), F32),
            pltpu.VMEM((length, width), F32),
            pltpu.VMEM((width, frames), F32),
        ],
        compiler_params=pltpu.CompilerParams(vmem_limit_bytes=VMEM_LIMIT),
        cost_estimate=pl.CostEstimate(
            flops=10 * rows * length * length * 256 * heads,
            bytes_accessed=16 * rows * length * width,
            transcendentals=rows * heads * length * length,
        ),
        name="attend_back",
    )(qkv, seg_col, seg_row, out, lse, grad, cos_table, sin_table)


def mlp_kernel(normed_ref, grad_ref, up_ref, down_ref, fed_ref, gn_ref, gup_ref, gdown_ref, nt_ref, gt_ref):
    @pl.when(pl.program_id(0) == 0)
    def _():
        nt_ref[...] = normed_ref[...].T
        gt_ref[...] = grad_ref[...].T
        fed_ref[...] = jnp.zeros_like(fed_ref)
        gn_ref[...] = jnp.zeros_like(gn_ref)

    up, down = up_ref[0], down_ref[0]
    before = dot(normed_ref[...], up)
    square = before * before
    factor = math.sqrt(2.0 / math.pi)
    bent = jnp.tanh(factor * (before + 0.044715 * (square * before)))
    activated = (0.5 * before * (1.0 + bent)).astype(BF16)
    slope = 0.5 * (1.0 + bent) + 0.5 * before * (1.0 - bent * bent) * (factor * (1.0 + 3 * 0.044715 * square))
    grad_before = (dot(grad_ref[...], down) * slope).astype(BF16)
    fed_ref[...] += against(activated, down)
    gn_ref[...] += against(grad_before, up)
    gup_ref[0] = dot(nt_ref[...], grad_before).astype(BF16)
    gdown_ref[0] = dot(gt_ref[...], activated).astype(BF16)


def mlp(normed, grad, up, down):
    tokens, model = normed.shape
    blocks, _, columns = up.shape
    chunk = min(512, columns)
    per_block = columns // chunk
    whole = pl.BlockSpec((tokens, model), lambda i: (0, 0))
    weight = pl.BlockSpec((1, model, chunk), lambda i: (i // per_block, 0, i % per_block))
    return pl.pallas_call(
        mlp_kernel,
        grid=(blocks * per_block,),
        out_shape=(
            jax.ShapeDtypeStruct((tokens, model), F32),
            jax.ShapeDtypeStruct((tokens, model), F32),
            jax.ShapeDtypeStruct(up.shape, BF16),
            jax.ShapeDtypeStruct(up.shape, BF16),
        ),
        in_specs=[whole, whole, weight, weight],
        out_specs=(whole, whole, weight, weight),
        scratch_shapes=[pltpu.VMEM((model, tokens), BF16), pltpu.VMEM((model, tokens), BF16)],
        compiler_params=pltpu.CompilerParams(vmem_limit_bytes=VMEM_LIMIT),
        cost_estimate=pl.CostEstimate(
            flops=12 * tokens * model * blocks * columns,
            bytes_accessed=8 * model * blocks * columns + 12 * tokens * model,
            transcendentals=tokens * blocks * columns,
        ),
        name="mlp",
    )(normed, grad, up, down)


def standardize(values):
    centre = values - jnp.mean(values, -1, keepdims=True)
    inverse = lax.rsqrt(jnp.mean(centre * centre, -1, keepdims=True) + EPSILON)
    return centre * inverse, inverse


def standardize_back(grad, standard, inverse):
    return inverse * (
        grad - jnp.mean(grad, -1, keepdims=True) - standard * jnp.mean(grad * standard, -1, keepdims=True)
    )


def time_embed(flow_values, model_width):
    half_dim = model_width // 2
    frequency = jnp.exp(jnp.arange(half_dim, dtype=F32) * (-math.log(10000.0) / half_dim))
    angles = 1000.0 * flow_values[..., None] * frequency
    return jnp.concatenate([jnp.sin(angles), jnp.cos(angles)], -1)


def body(
    frames, skip_in, cond, seg_ids, drop_flags, flow_times, w_skip, w_qkv, w_out, w_up, w_down, w_mod, cotangent
):
    row_count, frame_count, model = frames.shape
    seq_size, dp_size = lax.axis_size("seq"), lax.axis_size("dp")
    chips = dp_size // CORES
    dp, seq = lax.axis_index("dp"), lax.axis_index("seq")
    place = jnp.stack([dp, seq]).astype(jnp.int32)
    head_dim = model // HEADS
    heads = HEADS // seq_size
    width = heads * head_dim
    half = head_dim // 2
    scale = head_dim ** (-0.5)
    length = frame_count * seq_size
    tokens = row_count * frame_count
    segs = drop_flags.shape[1]
    frame_shape = (row_count, frame_count, model)
    partners = range(1, seq_size)

    by_head = w_qkv.reshape(w_qkv.shape[0], heads, 3, 2, half)
    qkv_shard = jnp.concatenate(
        [
            by_head[:, :, 0].swapaxes(1, 2).reshape(-1, width),
            by_head[:, :, 1].swapaxes(1, 2).reshape(-1, width),
            by_head[:, :, 2].reshape(-1, width),
        ],
        1,
    )

    small = jnp.concatenate([flow_times, drop_flags.astype(F32)], 1)
    small = gather_steps(small, [("dp", chip_masks()), ("dp", [1])])
    dropped = jnp.sum(small[..., segs:])
    slots = float(row_count * segs * dp_size)
    cond_scale = slots / jnp.maximum(slots - dropped, 1.0)
    utterances = row_count * segs
    activity = jax.nn.silu(time_embed(small[..., :segs], model)).astype(BF16).reshape(dp_size * utterances, model)
    mod_rows, mod_columns = w_mod.shape
    activity = lax.dynamic_slice_in_dim(activity, dp * mod_rows, mod_rows, 1)

    skip_full = fetch(w_skip, place, [1, 0], "")
    partial = dot(activity, w_mod).reshape(CORES, chips, utterances, mod_columns)
    partial = partial[0] + swap(partial[1], "dp", 1)
    modulation = partial[0]
    for mask in chip_masks():
        modulation = modulation + swap(partial[mask // CORES], "dp", mask)
    modulation = jnp.stack([modulation] + [swap(modulation, "seq", mask) for mask in partners])
    modulation = jnp.take(modulation, jnp.arange(seq_size) ^ seq, axis=0)
    modulation = modulation.swapaxes(0, 1).reshape(row_count, segs, 6, model)

    onehot = (seg_ids[:, :, None] == jnp.arange(segs, dtype=jnp.int32)).astype(F32)

    def spread(part):
        result = onehot[:, :, 0, None] * modulation[:, 0, None, part, :]
        for position in range(1, segs):
            result = result + onehot[:, :, position, None] * modulation[:, position, None, part, :]
        return result.reshape(tokens, model)

    shift_one, scale_one, gate_one, shift_two, scale_two, gate_two = (spread(part) for part in range(6))
    keep_frame = (1.0 - jnp.sum(onehot * drop_flags.astype(F32)[:, None, :], -1)).reshape(tokens, 1)

    qkv_full = fetch(qkv_shard, place, None, "")
    out_full = fetch(w_out.T, place, [0, 1], "columns")
    up_full = fetch(w_up, place, [1, 0], "blocks")
    down_full = fetch(w_down.T, place, [0, 1], "blocks")

    joined = jnp.concatenate([frames, skip_in], -1).reshape(tokens, 2 * model)
    hidden = dot(joined, skip_full) + keep_frame * cond_scale * cond.reshape(tokens, model).astype(F32)
    standard_one, inverse_one = standardize(hidden)
    normed = (standard_one * (1.0 + scale_one) + shift_one).astype(BF16).reshape(frame_shape)

    segments = jnp.stack([seg_ids] + [swap(seg_ids, "seq", mask) for mask in partners])
    seg_row = segments.swapaxes(0, 1).reshape(row_count, seq_size, 1, frame_count)
    seg_col = segments.swapaxes(0, 1).reshape(row_count, length, 1)
    positions = (jnp.arange(seq_size) ^ seq)[:, None] * frame_count + jnp.arange(frame_count)
    frequency = jnp.exp(jnp.arange(half, dtype=F32) * (-2.0 * math.log(10000.0) / head_dim))
    angles = positions.astype(F32)[..., None] * frequency
    cos_table = jnp.tile(jnp.cos(angles), (1, 1, heads))
    sin_table = jnp.tile(jnp.sin(angles), (1, 1, heads))

    pieces = [normed] + [swap(normed, "seq", mask) for mask in partners]
    qkv = None
    for position, piece in enumerate(pieces):
        qkv = project_piece(position, piece, qkv_full, cos_table, sin_table, qkv, scale)
    attended, lse = attend(qkv, seg_col, seg_row, heads)
    blocks = [attended[0]] + [swap(attended[mask], "seq", mask) for mask in partners]
    attn = jnp.concatenate(blocks, -1).reshape(tokens, model)

    branch = against(attn, out_full)
    middle = hidden + gate_one * branch
    standard_two, inverse_two = standardize(middle)
    normed_two = (standard_two * (1.0 + scale_two) + shift_two).astype(BF16)
    grad_out = cotangent.reshape(tokens, model).astype(F32)
    grad_fed = (gate_two * grad_out).astype(BF16)
    fed, grad_norm_two, grad_up, grad_down = mlp(normed_two, grad_fed, up_full, down_full)
    output = (middle + gate_two * fed).astype(BF16).reshape(frame_shape)

    rows = w_up.shape[0]
    sum_down = reduce_weight([grad_down[m] for m in range(seq_size)], rows, dp).T
    sum_up = reduce_weight([grad_up[m] for m in range(seq_size)], rows, dp)

    grad_middle = grad_out + standardize_back(grad_norm_two * (1.0 + scale_two), standard_two, inverse_two)
    grad_branch = (gate_one * grad_middle).astype(BF16)
    grad_attn = dot(grad_branch, out_full).astype(BF16).reshape(row_count, frame_count, seq_size, width)
    grad_blocks = [grad_attn[:, :, m] for m in range(seq_size)]
    grad_heads = jnp.stack([grad_blocks[0]] + [swap(grad_blocks[m], "seq", m) for m in partners])
    grad_w_out = over_rows(grad_branch, attn).astype(BF16)
    sum_out = reduce_weight([grad_w_out[:, m * width : (m + 1) * width] for m in range(seq_size)], rows, dp).T

    grad_qkv = attend_back(qkv, seg_col, seg_row, attended, lse, grad_heads, cos_table, sin_table, heads, scale)
    flat_grad = grad_qkv.reshape(seq_size, tokens, 3 * width)
    grad_normed = None
    for mask in list(partners) + [0]:
        part = against(flat_grad[mask], qkv_full)
        if mask:
            part = swap(part.astype(BF16), "seq", mask).astype(F32)
        grad_normed = part if grad_normed is None else grad_normed + part
    grad_w_qkv = over_rows(
        jnp.concatenate([piece.reshape(tokens, model) for piece in pieces]),
        flat_grad.reshape(seq_size * tokens, 3 * width),
    ).astype(BF16)
    sum_qkv = reduce_weight([grad_w_qkv], rows, dp)
    sum_qkv = jnp.stack(
        [
            sum_qkv[:, :width].reshape(rows, 2, heads, half).swapaxes(1, 2).reshape(rows, heads, head_dim),
            sum_qkv[:, width : 2 * width].reshape(rows, 2, heads, half).swapaxes(1, 2).reshape(rows, heads, head_dim),
            sum_qkv[:, 2 * width :].reshape(rows, heads, head_dim),
        ],
        2,
    ).reshape(rows, 3 * width)

    grad_hidden = (
        grad_middle + standardize_back(grad_normed * (1.0 + scale_one), standard_one, inverse_one)
    ).astype(BF16)
    grad_joined = against(grad_hidden, skip_full).astype(BF16)
    grad_frames = grad_joined[:, :model].reshape(frame_shape)
    grad_skip = grad_joined[:, model:].reshape(frame_shape)
    grad_columns = jnp.concatenate(
        [lax.dynamic_slice_in_dim(grad_hidden, (seq ^ m) * width, width, 1) for m in range(seq_size)], 1
    )
    grad_w_skip = over_rows(joined, grad_columns).astype(BF16)
    sum_skip = reduce_weight(
        [grad_w_skip[:, m * width : (m + 1) * width] for m in range(seq_size)], w_skip.shape[0], dp
    )

    def per_utterance(values):
        return jnp.einsum(
            "rfs,rfc->rsc", onehot, values.reshape(frame_shape), precision=lax.Precision.HIGHEST
        ).reshape(utterances, model)

    grad_modulation = jnp.concatenate(
        [
            per_utterance(grad_normed),
            per_utterance(grad_normed * standard_one),
            per_utterance(grad_middle * branch),
            per_utterance(grad_norm_two),
            per_utterance(grad_norm_two * standard_two),
            per_utterance(grad_out * fed),
        ],
        1,
    )
    own = lax.dynamic_slice_in_dim(grad_modulation, seq * mod_columns, mod_columns, 1)
    for mask in partners:
        own = own + swap(
            lax.dynamic_slice_in_dim(grad_modulation, (seq ^ mask) * mod_columns, mod_columns, 1), "seq", mask
        )
    own = gather_steps(own, [("dp", chip_masks()), ("dp", [1])]).reshape(dp_size * utterances, mod_columns)
    sum_mod = jnp.dot(activity.astype(F32).T, own, precision=lax.Precision.HIGHEST)
    return (output, grad_frames, grad_skip, sum_skip, sum_qkv, sum_out, sum_up, sum_down, sum_mod)


def solution(mesh):
    tokens, rows, both, turned = P("dp", "seq", None), P("dp", None), P("dp", "seq"), P("seq", "dp")
    in_specs = (tokens, tokens, tokens, both, rows, rows, both, both, turned, both, turned, both, tokens)
    out_specs = (tokens, tokens, tokens, both, both, turned, both, turned, both)
    return jax.shard_map(body, mesh=mesh, in_specs=in_specs, out_specs=out_specs, check_vma=False)
```

time: 1570 us -> 822 us (0.52)
  waiting for transfers between devices: 1010 us -> 309 us
  matrix products: 201 us -> 51.8 us
  Pallas kernels: 0 us -> 131 us
  blocking collectives: 84.7 us -> 0 us
  starting transfers between devices: 27.2 us -> 105 us
  other arithmetic: 78.7 us -> 106 us
  local copies, waits for them, and re-layouts: 133 us -> 106 us
    reduce_scatter x10 -> x0, waiting for transfers between devices: 502 us -> none  [the longest x1 124 us: body(): lax.psum_scatter(grad_w_mod.astype(jnp.bfloat16), 'seq', scatter_dimensio...]
    all_gather x11 -> x0, waiting for transfers between devices: 388 us -> none  [the longest x1 118 us: body(): lax.all_gather(mod_dp, 'seq', axis=1, tiled=True)]
    ppermute x0 -> x89, waiting for transfers between devices: none -> 309 us  [swap(): lax.ppermute(values, axis, [(i, i ^ mask) for i in range(lax.axis_size(ax...]
    dot_general x46 -> x19, matrix products: 201 us -> 51.8 us  [the longest x6 19.5 us: against(): return lax.dot_general(left, right, NT, preferred_element_type=F32)]
    pallas_call x0 -> x12, Pallas kernels: none -> 131 us  [the longest x1 33 us: mlp(): pl.pallas_call(mlp_kernel, grid=(blocks * per_block,), out_shape=(jax.Sha...]
    ppermute x0 -> x89, starting transfers between devices: none -> 105 us  [swap(): lax.ppermute(values, axis, [(i, i ^ mask) for i in range(lax.axis_size(ax...]
    unnamed x25 -> x0, waiting for transfers between devices: 66.3 us -> none
    all_to_all x7 -> x0, waiting for transfers between devices: 54.6 us -> none  [the longest x1 14.6 us: body(): lax.all_to_all(key_frames.reshape(frame_shape), 'seq', split_axis=2, conc...]
  transfers between devices with their start and end apart: 30 -> 89, of which waited for: 23 -> 24; matrix products, arithmetic and copies ran while one was open for 17% -> 29% of each run, Pallas kernels for 0% -> 11%
where the time goes in v1:
time: 822 us; the launch traced here: 812 us
  waiting for transfers between devices  309 us (38%)
  Pallas kernels  131 us (16%)
  local copies, waits for them, and re-layouts  106 us (13%)
  other arithmetic  106 us (13%)
  starting transfers between devices  105 us (13%)
  matrix products  51.8 us (6%)
    ppermute x89, waiting for transfers between devices, swap(): lax.ppermute(values, axis, [(i, i ^ mask) for i in range(lax.axis_size(ax...  309 us
    ppermute x89, starting transfers between devices, swap(): lax.ppermute(values, axis, [(i, i ^ mask) for i in range(lax.axis_size(ax...  105 us
    pallas_call x1, Pallas kernels, mlp(): pl.pallas_call(mlp_kernel, grid=(blocks * per_block,), out_shape=(jax.Sha...  33 us
    dynamic_slice x18, local copies, waits for them, and re-layouts, pick(): return lax.dynamic_index_in_dim(values, index, axis, keepdims=False)  32.9 us
    unnamed x225, local copies, waits for them, and re-layouts  31.4 us
    pallas_call x1, Pallas kernels, attend_back(): pl.pallas_call(functools.partial(attend_back_kernel, heads, width, scale)...  30.7 us
    another operation x18, other arithmetic, gather_steps(): held = jnp.stack([held] + [swap(held, axis, mask) for mask in masks])  28.1 us
    pallas_call x5, Pallas kernels, fetch(): pl.pallas_call(functools.partial(assemble_kernel, steps, rows, columns, r...  27.6 us
  transfers between devices with their start and end apart: 89, of which 24 were waited for; matrix products, arithmetic and copies ran while one was open for 29% of the time, Pallas kernels for 11%

profile of v1, /device:TPU:0, one launch (start us, length us, event | category | flops | bytes accessed | tf_op | source)
XLA Modules:
  0.0 812.0 jit_solution(4143188365213364858)
XLA Ops:
  2.3 5.0 collective-permute-start.8
  8.0 3.8 collective-permute-start.2
  45.3 8.9 %collective-permute-start.42 = (bf16[128,1024]{1,0:T(8,128)(2,1)S(1)}, bf16[128,1024]{1,0:T(8,128)(2,1)S(1)}, u32[]{:S(2)}, u32[]{:S(2)}) collective-permute-start(bf16[128,1024]{1,0:T(8,128)(2,1)S(1)} %bitcast.766), channel_id=1, source_target_pairs={{0,8},{4,12},{8,0},{12,4},{16,24},{20,28},{24,16},{28,20},{1,9},{5... | collective-permute-start | bytes 786440 | tf_op jit(solution)/shard_map/ppermute | solution.py:35
  54.2 16.3 %collective-permute-done.37 = bf16[128,1024]{1,0:T(8,128)(2,1)S(1)} collective-permute-done((bf16[128,1024]{1,0:T(8,128)(2,1)S(1)}, bf16[128,1024]{1,0:T(8,128)(2,1)S(1)}, u32[]{:S(2)}, u32[]{:S(2)}) %collective-permute-start.37) | collective-permute-done | bytes 262176 | tf_op jit(solution)/shard_map/ppermute | solution.py:35
  74.4 11.6 %collective-permute-done.43 = bf16[128,1024]{1,0:T(8,128)(2,1)S(1)} collective-permute-done((bf16[128,1024]{1,0:T(8,128)(2,1)S(1)}, bf16[128,1024]{1,0:T(8,128)(2,1)S(1)}, u32[]{:S(2)}, u32[]{:S(2)}) %collective-permute-start.43) | collective-permute-done | bytes 262176 | tf_op jit(solution)/shard_map/ppermute | solution.py:35
  88.7 3.4 collective-permute-done.13
  99.0 5.4 collective-permute-done.19
  110.5 29.7 %collective-permute-done.16 = f32[6,1536]{1,0:T(8,128)S(1)} collective-permute-done((f32[6,1536]{1,0:T(8,128)S(1)}, f32[6,1536]{1,0:T(8,128)S(1)}, u32[]{:S(2)}, u32[]{:S(2)}) %collective-permute-start.16) | collective-permute-done | bytes 36896 | tf_op jit(solution)/shard_map/ppermute | solution.py:35
  146.7 3.6 fusion.127
  158.3 32.7 %collective-permute-done.40 = bf16[2,4,128,1024]{3,2,1,0:T(8,128)(2,1)} collective-permute-done((bf16[2,4,128,1024]{3,2,1,0:T(8,128)(2,1)}, bf16[2,4,128,1024]{3,2,1,0:T(8,128)(2,1)}, u32[]{:S(2)}, u32[]{:S(2)}) %collective-permute-start.40) | collective-permute-done | bytes 2097184 | tf_op jit(solution)/shard_map/ppermute | solution.py:35
  191.0 4.1 pad_maximum_fusion.mine_ref
  195.6 4.0 pad_maximum_fusion.1.mine_ref
  199.6 5.3 assemble.5
  204.9 5.2 fusion.148
  218.0 6.8 collective-permute-done.34
  239.1 3.3 assemble.6.w_ref
  242.4 3.6 project.4.rest_0_
  246.0 3.6 project.5.rest_0_
  249.6 24.3 %collective-permute-done.22.x_ref = bf16[2,256,1024]{2,1,0:T(8,128)(2,1)} collective-permute-done((bf16[2,256,1024]{2,1,0:T(8,128)(2,1)}, bf16[2,256,1024]{2,1,0:T(8,128)(2,1)}, u32[]{:S(2)}, u32[]{:S(2)}) %collective-permute-start.22) | collective-permute-done | bytes 1048608 | tf_op jit(solution)/shard_map/ppermute | solution.py:35
  273.8 3.6 project.6.rest_0_
  277.4 3.6 project.7.qkv_ref
  281.0 25.3 %attend.1 = (bf16[4,2,256,256]{3,2,1,0:T(8,128)(2,1)}, f32[2,4,4,256]{3,2,1,0:T(4,128)}) custom-call(bf16[4,2,256,768]{3,2,1,0:T(8,128)(2,1)} %project.7.qkv_ref, s32[2,1024,1]{2,1,0:T(8,128)} %reshape.634.seg_col_ref, s32[2,4,1,256]{3,2,1,0:T(1,128)} %reshape.557.seg_row_ref), custom_call_target="tpu_custom_call" | custom-call | flops 8589934592 | bytes 4194304 | tf_op jit(solution)/shard_map/attend/pallas_call | solution.py:244
  311.9 3.8 assemble.7
  321.4 4.5 fusion.134
  326.3 4.9 fusion.20.normed_ref
  331.2 7.6 assemble.8.up_ref
  338.8 7.6 assemble.9.down_ref
  346.4 33.0 %mlp.1 = (f32[512,1024]{1,0:T(8,128)}, f32[512,1024]{1,0:T(8,128)}, bf16[4,1024,1024]{2,1,0:T(8,128)(2,1)}, bf16[4,1024,1024]{2,1,0:T(8,128)(2,1)}) custom-call(bf16[512,1024]{1,0:T(8,128)(2,1)} %fusion.20.normed_ref, bf16[512,1024]{1,0:T(8,128)(2,1)} %get-tuple-element.175.grad_ref, bf16[4,1024,1024]{2,1,0:T(8,128)(2,1)} %assemble.8.up_ref, ...), custom_call_target="tpu_custom_call" | custom-call | flops 25769803776 | bytes 39845888 | tf_op jit(solution)/shard_map/mlp/pallas_call | solution.py:398
  379.3 3.4 fusion.132
  382.8 5.7 fusion.133
  393.1 3.6 convolution_convert_fusion.2
  419.6 4.0 fusion.137
  429.0 3.2 fusion.136
  451.8 3.1 fusion.103
  456.3 3.6 pad_maximum_fusion.2
  466.0 30.7 %attend_back.1 = bf16[4,2,256,768]{3,2,1,0:T(8,128)(2,1)} custom-call(bf16[4,2,256,768]{3,2,1,0:T(8,128)(2,1)} %project.7.qkv_ref, s32[2,1024,1]{2,1,0:T(8,128)} %reshape.634.seg_col_ref, s32[2,4,1,256]{3,2,1,0:T(1,128)} %reshape.557.seg_row_ref, bf16[4,2,256,256]{3,2,1,0:T(8,128)(2,1)} %get-tuple-element.15.out_ref, ...), custom_call_target="tpu_custom_call" | custom-call | flops 21474836480 | bytes 8388608 | tf_op jit(solution)/shard_map/attend_back/pallas_call | solution.py:338
  496.6 3.7 fusion.139
  500.4 5.8 fusion.47
  510.2 3.8 convolution_convert_fusion.3
  549.7 5.7 collective-permute-done.62
  558.2 4.6 collective-permute-done.52
  562.8 4.9 fusion.50
  623.7 28.1 %collective-permute-done.71 = bf16[2,4,128,1024]{3,2,1,0:T(8,128)(2,1)} collective-permute-done((bf16[2,4,128,1024]{3,2,1,0:T(8,128)(2,1)}, bf16[2,4,128,1024]{3,2,1,0:T(8,128)(2,1)}, u32[]{:S(2)}, u32[]{:S(2)}) %collective-permute-start.71) | collective-permute-done | bytes 2097184 | tf_op jit(solution)/shard_map/ppermute | solution.py:35
  654.2 63.5 %collective-permute-done.55 = bf16[2,4,256,256]{3,2,1,0:T(8,128)(2,1)} collective-permute-done((bf16[2,4,256,256]{3,2,1,0:T(8,128)(2,1)}, bf16[2,4,256,256]{3,2,1,0:T(8,128)(2,1)}, u32[]{:S(2)}, u32[]{:S(2)}) %collective-permute-start.55) | collective-permute-done | bytes 1048608 | tf_op jit(solution)/shard_map/ppermute | solution.py:35
  724.7 30.3 %collective-permute-done.56 = bf16[4,256,256]{2,1,0:T(8,128)(2,1)S(1)} collective-permute-done((bf16[4,256,256]{2,1,0:T(8,128)(2,1)S(1)}, bf16[4,256,256]{2,1,0:T(8,128)(2,1)S(1)}, u32[]{:S(2)}, u32[]{:S(2)}) %collective-permute-start.56) | collective-permute-done | bytes 524320 | tf_op jit(solution)/shard_map/ppermute | solution.py:35
  765.3 9.6 %collective-permute-done.78 = bf16[4,128,1024]{1,2,0:T(8,128)(2,1)S(1)} collective-permute-done((bf16[4,128,1024]{1,2,0:T(8,128)(2,1)S(1)}, bf16[4,128,1024]{1,2,0:T(8,128)(2,1)S(1)}, u32[]{:S(2)}, u32[]{:S(2)}) %collective-permute-start.78) | collective-permute-done | bytes 1048608 | tf_op jit(solution)/shard_map/ppermute | solution.py:35
  784.6 14.9 %collective-permute-done.74 = bf16[128,1024]{1,0:T(8,128)(2,1)S(1)} collective-permute-done((bf16[128,1024]{1,0:T(8,128)(2,1)S(1)}, bf16[128,1024]{1,0:T(8,128)(2,1)S(1)}, u32[]{:S(2)}, u32[]{:S(2)}) %collective-permute-start.74) | collective-permute-done | bytes 262176 | tf_op jit(solution)/shard_map/ppermute | solution.py:35
  800.4 10.2 %collective-permute-done.80 = bf16[128,1024]{0,1:T(8,128)(2,1)S(1)} collective-permute-done((bf16[128,1024]{0,1:T(8,128)(2,1)S(1)}, bf16[128,1024]{0,1:T(8,128)(2,1)S(1)}, u32[]{:S(2)}, u32[]{:S(2)}) %collective-permute-start.80) | collective-permute-done | bytes 262176 | tf_op jit(solution)/shard_map/ppermute | solution.py:35
  (552 shorter events, 291.9 us)
Async XLA Ops:
  8.0 27.3 %collective-permute-start.2 = (bf16[256,256]{1,0:T(8,128)(2,1)}, bf16[256,256]{1,0:T(8,128)(2,1)S(1)}, u32[]{:S(2)}, u32[]{:S(2)}) collective-permute-start(bf16[256,256]{1,0:T(8,128)(2,1)} %param.19), channel_id=1, source_target_pairs={{0,24},{4,28},{8,16},{12,20},{16,8},{20,12},{24,0},{28,4},{1,25},{... | collective-permute-start | bytes 393224 | tf_op jit(solution)/shard_map/ppermute | solution.py:35
  11.7 25.7 %collective-permute-start.1 = (bf16[256,256]{1,0:T(8,128)(2,1)}, bf16[256,256]{1,0:T(8,128)(2,1)S(1)}, u32[]{:S(2)}, u32[]{:S(2)}) collective-permute-start(bf16[256,256]{1,0:T(8,128)(2,1)} %param.19), channel_id=1, source_target_pairs={{0,16},{4,20},{8,24},{12,28},{16,0},{20,4},{24,8},{28,12},{1,17},{... | collective-permute-start | bytes 393224 | tf_op jit(solution)/shard_map/ppermute | solution.py:35
  35.2 35.3 %collective-permute-start.37 = (bf16[128,1024]{1,0:T(8,128)(2,1)S(1)}, bf16[128,1024]{1,0:T(8,128)(2,1)S(1)}, u32[]{:S(2)}, u32[]{:S(2)}) collective-permute-start(bf16[128,1024]{1,0:T(8,128)(2,1)S(1)} %copy-done.59), channel_id=1, source_target_pairs={{0,16},{4,20},{8,24},{12,28},{16,0},{20,4},{24,8},{28,12},{1,17},{... | collective-permute-start | bytes 786440 | tf_op jit(solution)/shard_map/ppermute | solution.py:35
  35.2 36.8 %collective-permute-start.36 = (bf16[128,1024]{1,0:T(8,128)(2,1)S(1)}, bf16[128,1024]{1,0:T(8,128)(2,1)S(1)}, u32[]{:S(2)}, u32[]{:S(2)}) collective-permute-start(bf16[128,1024]{1,0:T(8,128)(2,1)S(1)} %copy-done.59), channel_id=1, source_target_pairs={{0,8},{4,12},{8,0},{12,4},{16,24},{20,28},{24,16},{28,20},{1,9},{5... | collective-permute-start | bytes 786440 | tf_op jit(solution)/shard_map/ppermute | solution.py:35
  38.8 34.0 %collective-permute-start.44 = (bf16[128,1024]{1,0:T(8,128)(2,1)S(1)}, bf16[128,1024]{1,0:T(8,128)(2,1)S(1)}, u32[]{:S(2)}, u32[]{:S(2)}) collective-permute-start(bf16[128,1024]{1,0:T(8,128)(2,1)S(1)} %bitcast.764), channel_id=1, source_target_pairs={{0,24},{4,28},{8,16},{12,20},{16,8},{20,12},{24,0},{28,4},{1,25},{... | collective-permute-start | bytes 786440 | tf_op jit(solution)/shard_map/ppermute | solution.py:35
  42.8 43.2 %collective-permute-start.43 = (bf16[128,1024]{1,0:T(8,128)(2,1)S(1)}, bf16[128,1024]{1,0:T(8,128)(2,1)S(1)}, u32[]{:S(2)}, u32[]{:S(2)}) collective-permute-start(bf16[128,1024]{1,0:T(8,128)(2,1)S(1)} %bitcast.765), channel_id=1, source_target_pairs={{0,16},{4,20},{8,24},{12,28},{16,0},{20,4},{24,8},{28,12},{1,17},{... | collective-permute-start | bytes 786440 | tf_op jit(solution)/shard_map/ppermute | solution.py:35
  45.3 42.2 %collective-permute-start.42 = (bf16[128,1024]{1,0:T(8,128)(2,1)S(1)}, bf16[128,1024]{1,0:T(8,128)(2,1)S(1)}, u32[]{:S(2)}, u32[]{:S(2)}) collective-permute-start(bf16[128,1024]{1,0:T(8,128)(2,1)S(1)} %bitcast.766), channel_id=1, source_target_pairs={{0,8},{4,12},{8,0},{12,4},{16,24},{20,28},{24,16},{28,20},{1,9},{5... | collective-permute-start | bytes 786440 | tf_op jit(solution)/shard_map/ppermute | solution.py:35
  72.3 35.1 %collective-permute-start.39 = (bf16[4,128,1024]{2,1,0:T(8,128)(2,1)S(1)}, bf16[4,128,1024]{2,1,0:T(8,128)(2,1)S(1)}, u32[]{:S(2)}, u32[]{:S(2)}) collective-permute-start(bf16[4,128,1024]{2,1,0:T(8,128)(2,1)S(1)} %get-tuple-element.110), channel_id=1, source_target_pairs={{0,2},{1,3},{2,0},{3,1},{4,6},{5,7},{6,4},{7,5},{8,10},{9,11},{10,... | collective-permute-start | bytes 3145736 | tf_op jit(solution)/shard_map/ppermute | solution.py:35
  72.9 25.6 %collective-permute-start.20 = (bf16[128,768]{1,0:T(8,128)(2,1)S(1)}, bf16[128,768]{1,0:T(8,128)(2,1)S(1)}, u32[]{:S(2)}, u32[]{:S(2)}) collective-permute-start(bf16[128,768]{1,0:T(8,128)(2,1)S(1)} %copy-done.60), channel_id=1, source_target_pairs={{0,24},{4,28},{8,16},{12,20},{16,8},{20,12},{24,0},{28,4},{1,25},{... | collective-permute-start | bytes 589832 | tf_op jit(solution)/shard_map/ppermute | solution.py:35
  92.0 54.6 %collective-permute-start.45 = (bf16[4,128,1024]{2,1,0:T(8,128)(2,1)}, bf16[4,128,1024]{2,1,0:T(8,128)(2,1)}, u32[]{:S(2)}, u32[]{:S(2)}) collective-permute-start(bf16[4,128,1024]{2,1,0:T(8,128)(2,1)} %get-tuple-element.108), channel_id=1, source_target_pairs={{0,1},{1,0},{2,3},{3,2},{4,5},{5,4},{6,7},{7,6},{8,9},{9,8},{10,11... | collective-permute-start | bytes 3145736 | tf_op jit(solution)/shard_map/ppermute | solution.py:35
  98.4 53.4 %collective-permute-start.4 = (bf16[2,4,256,256]{3,2,1,0:T(8,128)(2,1)}, bf16[2,4,256,256]{3,2,1,0:T(8,128)(2,1)}, u32[]{:S(2)}, u32[]{:S(2)}) collective-permute-start(bf16[2,4,256,256]{3,2,1,0:T(8,128)(2,1)} %get-tuple-element.116), channel_id=1, source_target_pairs={{0,1},{1,0},{2,3},{3,2},{4,5},{5,4},{6,7},{7,6},{8,9},{9,8},{10,11... | collective-permute-start | bytes 3145736 | tf_op jit(solution)/shard_map/ppermute | solution.py:35
  104.4 35.8 %collective-permute-start.16 = (f32[6,1536]{1,0:T(8,128)S(1)}, f32[6,1536]{1,0:T(8,128)S(1)}, u32[]{:S(2)}, u32[]{:S(2)}) collective-permute-start(f32[6,1536]{1,0:T(8,128)S(1)} %fusion.97), channel_id=1, source_target_pairs={{0,3},{1,2},{2,1},{3,0},{4,7},{5,6},{6,5},{7,4},{8,11},{9,10},{10,... | collective-permute-start | bytes 110600 | tf_op jit(solution)/shard_map/ppermute | solution.py:35
  105.9 35.8 %collective-permute-start.15 = (f32[6,1536]{1,0:T(8,128)S(1)}, f32[6,1536]{1,0:T(8,128)S(1)}, u32[]{:S(2)}, u32[]{:S(2)}) collective-permute-start(f32[6,1536]{1,0:T(8,128)S(1)} %fusion.97), channel_id=1, source_target_pairs={{0,2},{1,3},{2,0},{3,1},{4,6},{5,7},{6,4},{7,5},{8,10},{9,11},{10,... | collective-permute-start | bytes 110600 | tf_op jit(solution)/shard_map/ppermute | solution.py:35
  107.4 34.8 %collective-permute-start.14 = (f32[6,1536]{1,0:T(8,128)S(1)}, f32[6,1536]{1,0:T(8,128)S(1)}, u32[]{:S(2)}, u32[]{:S(2)}) collective-permute-start(f32[6,1536]{1,0:T(8,128)S(1)} %fusion.97), channel_id=1, source_target_pairs={{0,1},{1,0},{2,3},{3,2},{4,5},{5,4},{6,7},{7,6},{8,9},{9,8},{10,11... | collective-permute-start | bytes 110600 | tf_op jit(solution)/shard_map/ppermute | solution.py:35
  140.2 70.0 %collective-permute-start.26 = (s32[2,256]{1,0:T(2,128)S(1)}, s32[2,256]{1,0:T(2,128)}, u32[]{:S(2)}, u32[]{:S(2)}) collective-permute-start(s32[2,256]{1,0:T(2,128)S(1)} %copy-done.61), channel_id=1, source_target_pairs={{0,3},{1,2},{2,1},{3,0},{4,7},{5,6},{6,5},{7,4},{8,11},{9,10},{10,... | collective-permute-start | bytes 6152 | tf_op jit(solution)/shard_map/ppermute | solution.py:35
  142.2 48.8 %collective-permute-start.40 = (bf16[2,4,128,1024]{3,2,1,0:T(8,128)(2,1)}, bf16[2,4,128,1024]{3,2,1,0:T(8,128)(2,1)}, u32[]{:S(2)}, u32[]{:S(2)}) collective-permute-start(bf16[2,4,128,1024]{3,2,1,0:T(8,128)(2,1)} %get-tuple-element.88), channel_id=1, source_target_pairs={{0,1},{1,0},{2,3},{3,2},{4,5},{5,4},{6,7},{7,6},{8,9},{9,8},{10,11... | collective-permute-start | bytes 6291464 | tf_op jit(solution)/shard_map/ppermute | solution.py:35
  150.3 44.8 %collective-permute-start.46 = (bf16[2,4,128,1024]{3,2,1,0:T(8,128)(2,1)}, bf16[2,4,128,1024]{3,2,1,0:T(8,128)(2,1)}, u32[]{:S(2)}, u32[]{:S(2)}) collective-permute-start(bf16[2,4,128,1024]{3,2,1,0:T(8,128)(2,1)} %get-tuple-element.86), channel_id=1, source_target_pairs={{0,2},{1,3},{2,0},{3,1},{4,6},{5,7},{6,4},{7,5},{8,10},{9,11},{10,... | collective-permute-start | bytes 6291464 | tf_op jit(solution)/shard_map/ppermute | solution.py:35
  154.6 45.0 %collective-permute-start.5 = (bf16[2,2,4,256,256]{4,3,2,1,0:T(8,128)(2,1)}, bf16[2,2,4,256,256]{4,3,2,1,0:T(8,128)(2,1)}, u32[]{:S(2)}, u32[]{:S(2)}) collective-permute-start(bf16[2,2,4,256,256]{4,3,2,1,0:T(8,128)(2,1)} %pad_maximum_fusion.5.mine_ref), channel_id=1, source_target_pairs={{0,4},{4,0},{8,12},{12,8},{16,20},{20,16},{24,28},{28,24},{1,5},{5... | collective-permute-start | bytes 6291464 | tf_op jit(solution)/shard_map/ppermute | solution.py:35
  155.7 56.4 %collective-permute-start.25 = (s32[2,256]{1,0:T(2,128)S(1)}, s32[2,256]{1,0:T(2,128)S(1)}, u32[]{:S(2)}, u32[]{:S(2)}) collective-permute-start(s32[2,256]{1,0:T(2,128)S(1)} %copy-done.61), channel_id=1, source_target_pairs={{0,2},{1,3},{2,0},{3,1},{4,6},{5,7},{6,4},{7,5},{8,10},{9,11},{10,... | collective-permute-start | bytes 6152 | tf_op jit(solution)/shard_map/ppermute | solution.py:35
  191.0 35.8 %collective-permute-start.21 = (bf16[4,128,768]{2,1,0:T(8,128)(2,1)}, bf16[4,128,768]{2,1,0:T(8,128)(2,1)}, u32[]{:S(2)}, u32[]{:S(2)}) collective-permute-start(bf16[4,128,768]{2,1,0:T(8,128)(2,1)} %pad_maximum_fusion.19.mine_ref), channel_id=1, source_target_pairs={{0,4},{4,0},{8,12},{12,8},{16,20},{20,16},{24,28},{28,24},{1,5},{5... | collective-permute-start | bytes 2359304 | tf_op jit(solution)/shard_map/ppermute | solution.py:35
  195.1 136.1 %collective-permute-start.41 = (bf16[2,2,4,128,1024]{4,3,2,1,0:T(8,128)(2,1)}, bf16[2,2,4,128,1024]{4,3,2,1,0:T(8,128)(2,1)}, u32[]{:S(2)}, u32[]{:S(2)}) collective-permute-start(bf16[2,2,4,128,1024]{4,3,2,1,0:T(8,128)(2,1)} %pad_maximum_fusion.mine_ref), channel_id=1, source_target_pairs={{0,4},{4,0},{8,12},{12,8},{16,20},{20,16},{24,28},{28,24},{1,5},{5... | collective-permute-start | bytes 12582920 | tf_op jit(solution)/shard_map/ppermute | solution.py:35
  199.6 139.2 %collective-permute-start.47 = (bf16[2,2,4,128,1024]{4,3,2,1,0:T(8,128)(2,1)}, bf16[2,2,4,128,1024]{4,3,2,1,0:T(8,128)(2,1)}, u32[]{:S(2)}, u32[]{:S(2)}) collective-permute-start(bf16[2,2,4,128,1024]{4,3,2,1,0:T(8,128)(2,1)} %pad_maximum_fusion.1.mine_ref), channel_id=1, source_target_pairs={{0,4},{4,0},{8,12},{12,8},{16,20},{20,16},{24,28},{28,24},{1,5},{5... | collective-permute-start | bytes 12582920 | tf_op jit(solution)/shard_map/ppermute | solution.py:35
  216.8 29.2 %collective-permute-start.23 = (bf16[2,256,1024]{2,1,0:T(8,128)(2,1)}, bf16[2,256,1024]{2,1,0:T(8,128)(2,1)}, u32[]{:S(2)}, u32[]{:S(2)}) collective-permute-start(bf16[2,256,1024]{2,1,0:T(8,128)(2,1)} %bitcast.40.x_ref), channel_id=1, source_target_pairs={{0,1},{1,0},{2,3},{3,2},{4,5},{5,4},{6,7},{7,6},{8,9},{9,8},{10,11... | collective-permute-start | bytes 3145736 | tf_op jit(solution)/shard_map/ppermute | solution.py:35
  224.8 52.6 %collective-permute-start.17 = (bf16[2,256,1024]{2,1,0:T(8,128)(2,1)}, bf16[2,256,1024]{2,1,0:T(8,128)(2,1)}, u32[]{:S(2)}, u32[]{:S(2)}) collective-permute-start(bf16[2,256,1024]{2,1,0:T(8,128)(2,1)} %bitcast.40.x_ref), channel_id=1, source_target_pairs={{0,3},{1,2},{2,1},{3,0},{4,7},{5,6},{6,5},{7,4},{8,11},{9,10},{10,... | collective-permute-start | bytes 3145736 | tf_op jit(solution)/shard_map/ppermute | solution.py:35
  226.7 47.1 %collective-permute-start.22 = (bf16[2,256,1024]{2,1,0:T(8,128)(2,1)}, bf16[2,256,1024]{2,1,0:T(8,128)(2,1)}, u32[]{:S(2)}, u32[]{:S(2)}) collective-permute-start(bf16[2,256,1024]{2,1,0:T(8,128)(2,1)} %bitcast.40.x_ref), channel_id=1, source_target_pairs={{0,2},{1,3},{2,0},{3,1},{4,6},{5,7},{6,4},{7,5},{8,10},{9,11},{10,... | collective-permute-start | bytes 3145736 | tf_op jit(solution)/shard_map/ppermute | solution.py:35
  246.0 64.8 %collective-permute-start.35 = (bf16[2,2,4,128,256]{4,3,2,1,0:T(8,128)(2,1)}, bf16[2,2,4,128,256]{4,3,2,1,0:T(8,128)(2,1)}, u32[]{:S(2)}, u32[]{:S(2)}) collective-permute-start(bf16[2,2,4,128,256]{4,3,2,1,0:T(8,128)(2,1)} %pad_maximum_fusion.13.mine_ref), channel_id=1, source_target_pairs={{0,4},{4,0},{8,12},{12,8},{16,20},{20,16},{24,28},{28,24},{1,5},{5... | collective-permute-start | bytes 3145736 | tf_op jit(solution)/shard_map/ppermute | solution.py:35
  400.9 62.9 %collective-permute-start.50 = (bf16[2,256,256]{2,1,0:T(8,128)(2,1)}, bf16[2,256,256]{2,1,0:T(8,128)(2,1)}, u32[]{:S(2)}, u32[]{:S(2)}) collective-permute-start(bf16[2,256,256]{2,1,0:T(8,128)(2,1)} %bitcast.713), channel_id=1, source_target_pairs={{0,3},{1,2},{2,1},{3,0},{4,7},{5,6},{6,5},{7,4},{8,11},{9,10},{10,... | collective-permute-start | bytes 786440 | tf_op jit(solution)/shard_map/ppermute | solution.py:35
  403.0 60.8 %collective-permute-start.49 = (bf16[2,256,256]{2,1,0:T(8,128)(2,1)}, bf16[2,256,256]{2,1,0:T(8,128)(2,1)}, u32[]{:S(2)}, u32[]{:S(2)}) collective-permute-start(bf16[2,256,256]{2,1,0:T(8,128)(2,1)} %bitcast.714), channel_id=1, source_target_pairs={{0,2},{1,3},{2,0},{3,1},{4,6},{5,7},{6,4},{7,5},{8,10},{9,11},{10,... | collective-permute-start | bytes 786440 | tf_op jit(solution)/shard_map/ppermute | solution.py:35
  404.8 58.9 %collective-permute-start.48 = (bf16[2,256,256]{2,1,0:T(8,128)(2,1)}, bf16[2,256,256]{2,1,0:T(8,128)(2,1)}, u32[]{:S(2)}, u32[]{:S(2)}) collective-permute-start(bf16[2,256,256]{2,1,0:T(8,128)(2,1)} %bitcast.715), channel_id=1, source_target_pairs={{0,1},{1,0},{2,3},{3,2},{4,5},{5,4},{6,7},{7,6},{8,9},{9,8},{10,11... | collective-permute-start | bytes 786440 | tf_op jit(solution)/shard_map/ppermute | solution.py:35
  419.6 125.2 %collective-permute-start.64 = (bf16[4,4,128,256]{2,3,1,0:T(8,128)(2,1)}, bf16[4,4,128,256]{2,3,1,0:T(8,128)(2,1)}, u32[]{:S(2)}, u32[]{:S(2)}) collective-permute-start(bf16[4,4,128,256]{2,3,1,0:T(8,128)(2,1)} %pad_maximum_fusion.18), channel_id=1, source_target_pairs={{0,4},{4,0},{8,12},{12,8},{16,20},{20,16},{24,28},{28,24},{1,5},{5... | collective-permute-start | bytes 3145736 | tf_op jit(solution)/shard_map/ppermute | solution.py:35
  514.0 44.2 %collective-permute-start.53 = (bf16[512,1024]{1,0:T(8,128)(2,1)}, bf16[512,1024]{1,0:T(8,128)(2,1)}, u32[]{:S(2)}, u32[]{:S(2)}) collective-permute-start(bf16[512,1024]{1,0:T(8,128)(2,1)} %convolution_convert_fusion.3), channel_id=1, source_target_pairs={{0,3},{1,2},{2,1},{3,0},{4,7},{5,6},{6,5},{7,4},{8,11},{9,10},{10,... | collective-permute-start | bytes 3145736 | tf_op jit(solution)/shard_map/ppermute | solution.py:35
  517.4 45.4 %collective-permute-start.52 = (bf16[512,1024]{1,0:T(8,128)(2,1)}, bf16[512,1024]{1,0:T(8,128)(2,1)}, u32[]{:S(2)}, u32[]{:S(2)}) collective-permute-start(bf16[512,1024]{1,0:T(8,128)(2,1)} %convolution_convert_fusion.4), channel_id=1, source_target_pairs={{0,2},{1,3},{2,0},{3,1},{4,6},{5,7},{6,4},{7,5},{8,10},{9,11},{10,... | collective-permute-start | bytes 3145736 | tf_op jit(solution)/shard_map/ppermute | solution.py:35
  520.5 42.3 %collective-permute-start.51 = (bf16[512,1024]{1,0:T(8,128)(2,1)}, bf16[512,1024]{1,0:T(8,128)(2,1)}, u32[]{:S(2)}, u32[]{:S(2)}) collective-permute-start(bf16[512,1024]{1,0:T(8,128)(2,1)} %convolution_convert_fusion.5), channel_id=1, source_target_pairs={{0,1},{1,0},{2,3},{3,2},{4,5},{5,4},{6,7},{7,6},{8,9},{9,8},{10,11... | collective-permute-start | bytes 3145736 | tf_op jit(solution)/shard_map/ppermute | solution.py:35
  555.5 40.5 %collective-permute-start.70 = (bf16[4,4,128,1024]{3,2,1,0:T(8,128)(2,1)}, bf16[4,4,128,1024]{3,2,1,0:T(8,128)(2,1)}, u32[]{:S(2)}, u32[]{:S(2)}) collective-permute-start(bf16[4,4,128,1024]{3,2,1,0:T(8,128)(2,1)} %pad_maximum_fusion.2), channel_id=1, source_target_pairs={{0,4},{4,0},{8,12},{12,8},{16,20},{20,16},{24,28},{28,24},{1,5},{5... | collective-permute-start | bytes 12582920 | tf_op jit(solution)/shard_map/ppermute | solution.py:35
  555.6 44.5 %collective-permute-start.76 = (bf16[4,4,128,1024]{2,3,1,0:T(8,128)(2,1)}, bf16[4,4,128,1024]{2,3,1,0:T(8,128)(2,1)}, u32[]{:S(2)}, u32[]{:S(2)}) collective-permute-start(bf16[4,4,128,1024]{2,3,1,0:T(8,128)(2,1)} %pad_maximum_fusion.3), channel_id=1, source_target_pairs={{0,4},{4,0},{8,12},{12,8},{16,20},{20,16},{24,28},{28,24},{1,5},{5... | collective-permute-start | bytes 12582920 | tf_op jit(solution)/shard_map/ppermute | solution.py:35
  587.7 23.7 %collective-permute-start.54 = (bf16[4,4,256,256]{3,2,1,0:T(8,128)(2,1)S(1)}, bf16[4,4,256,256]{3,2,1,0:T(8,128)(2,1)S(1)}, u32[]{:S(2)}, u32[]{:S(2)}) collective-permute-start(bf16[4,4,256,256]{3,2,1,0:T(8,128)(2,1)S(1)} %pad_maximum_fusion.8), channel_id=1, source_target_pairs={{0,4},{4,0},{8,12},{12,8},{16,20},{20,16},{24,28},{28,24},{1,5},{5... | collective-permute-start | bytes 6291464 | tf_op jit(solution)/shard_map/ppermute | solution.py:35
  600.1 51.7 %collective-permute-start.71 = (bf16[2,4,128,1024]{3,2,1,0:T(8,128)(2,1)}, bf16[2,4,128,1024]{3,2,1,0:T(8,128)(2,1)}, u32[]{:S(2)}, u32[]{:S(2)}) collective-permute-start(bf16[2,4,128,1024]{3,2,1,0:T(8,128)(2,1)} %pad_maximum_fusion.9), channel_id=1, source_target_pairs={{0,1},{1,0},{2,3},{3,2},{4,5},{5,4},{6,7},{7,6},{8,9},{9,8},{10,11... | collective-permute-start | bytes 6291464 | tf_op jit(solution)/shard_map/ppermute | solution.py:35
  607.3 112.6 %collective-permute-start.77 = (bf16[2,4,128,1024]{2,3,1,0:T(8,128)(2,1)}, bf16[2,4,128,1024]{2,3,1,0:T(8,128)(2,1)}, u32[]{:S(2)}, u32[]{:S(2)}) collective-permute-start(bf16[2,4,128,1024]{2,3,1,0:T(8,128)(2,1)} %pad_maximum_fusion.10), channel_id=1, source_target_pairs={{0,1},{1,0},{2,3},{3,2},{4,5},{5,4},{6,7},{7,6},{8,9},{9,8},{10,11... | collective-permute-start | bytes 6291464 | tf_op jit(solution)/shard_map/ppermute | solution.py:35
  613.0 104.7 %collective-permute-start.55 = (bf16[2,4,256,256]{3,2,1,0:T(8,128)(2,1)}, bf16[2,4,256,256]{3,2,1,0:T(8,128)(2,1)}, u32[]{:S(2)}, u32[]{:S(2)}) collective-permute-start(bf16[2,4,256,256]{3,2,1,0:T(8,128)(2,1)} %pad_maximum_fusion.17), channel_id=1, source_target_pairs={{0,1},{1,0},{2,3},{3,2},{4,5},{5,4},{6,7},{7,6},{8,9},{9,8},{10,11... | collective-permute-start | bytes 3145736 | tf_op jit(solution)/shard_map/ppermute | solution.py:35
  620.7 102.3 %collective-permute-start.69 = (bf16[128,256]{0,1:T(8,128)(2,1)S(1)}, bf16[128,256]{0,1:T(8,128)(2,1)S(1)}, u32[]{:S(2)}, u32[]{:S(2)}) collective-permute-start(bf16[128,256]{0,1:T(8,128)(2,1)S(1)} %get-tuple-element.118), channel_id=1, source_target_pairs={{0,24},{4,28},{8,16},{12,20},{16,8},{20,12},{24,0},{28,4},{1,25},{... | collective-permute-start | bytes 196616 | tf_op jit(solution)/shard_map/ppermute | solution.py:35
  622.8 101.2 %collective-permute-start.68 = (bf16[128,256]{0,1:T(8,128)(2,1)S(1)}, bf16[128,256]{0,1:T(8,128)(2,1)S(1)}, u32[]{:S(2)}, u32[]{:S(2)}) collective-permute-start(bf16[128,256]{0,1:T(8,128)(2,1)S(1)} %get-tuple-element.119), channel_id=1, source_target_pairs={{0,16},{4,20},{8,24},{12,28},{16,0},{20,4},{24,8},{28,12},{1,17},{... | collective-permute-start | bytes 196616 | tf_op jit(solution)/shard_map/ppermute | solution.py:35
  651.9 72.2 %collective-permute-start.67 = (bf16[128,256]{0,1:T(8,128)(2,1)S(1)}, bf16[128,256]{0,1:T(8,128)(2,1)S(1)}, u32[]{:S(2)}, u32[]{:S(2)}) collective-permute-start(bf16[128,256]{0,1:T(8,128)(2,1)S(1)} %get-tuple-element.117), channel_id=1, source_target_pairs={{0,8},{4,12},{8,0},{12,4},{16,24},{20,28},{24,16},{28,20},{1,9},{5... | collective-permute-start | bytes 196616 | tf_op jit(solution)/shard_map/ppermute | solution.py:35
  717.7 43.4 %collective-permute-start.72 = (bf16[4,128,1024]{2,1,0:T(8,128)(2,1)S(1)}, bf16[4,128,1024]{2,1,0:T(8,128)(2,1)S(1)}, u32[]{:S(2)}, u32[]{:S(2)}) collective-permute-start(bf16[4,128,1024]{2,1,0:T(8,128)(2,1)S(1)} %fusion.13), channel_id=1, source_target_pairs={{0,2},{1,3},{2,0},{3,1},{4,6},{5,7},{6,4},{7,5},{8,10},{9,11},{10,... | collective-permute-start | bytes 3145736 | tf_op jit(solution)/shard_map/ppermute | solution.py:35
  719.9 35.1 %collective-permute-start.56 = (bf16[4,256,256]{2,1,0:T(8,128)(2,1)S(1)}, bf16[4,256,256]{2,1,0:T(8,128)(2,1)S(1)}, u32[]{:S(2)}, u32[]{:S(2)}) collective-permute-start(bf16[4,256,256]{2,1,0:T(8,128)(2,1)S(1)} %fusion.59), channel_id=1, source_target_pairs={{0,2},{1,3},{2,0},{3,1},{4,6},{5,7},{6,4},{7,5},{8,10},{9,11},{10,... | collective-permute-start | bytes 1572872 | tf_op jit(solution)/shard_map/ppermute | solution.py:35
  723.0 51.9 %collective-permute-start.78 = (bf16[4,128,1024]{1,2,0:T(8,128)(2,1)S(1)}, bf16[4,128,1024]{1,2,0:T(8,128)(2,1)S(1)}, u32[]{:S(2)}, u32[]{:S(2)}) collective-permute-start(bf16[4,128,1024]{1,2,0:T(8,128)(2,1)S(1)} %fusion.9), channel_id=1, source_target_pairs={{0,2},{1,3},{2,0},{3,1},{4,6},{5,7},{6,4},{7,5},{8,10},{9,11},{10,... | collective-permute-start | bytes 3145736 | tf_op jit(solution)/shard_map/ppermute | solution.py:35
  774.9 24.6 %collective-permute-start.74 = (bf16[128,1024]{1,0:T(8,128)(2,1)S(1)}, bf16[128,1024]{1,0:T(8,128)(2,1)S(1)}, u32[]{:S(2)}, u32[]{:S(2)}) collective-permute-start(bf16[128,1024]{1,0:T(8,128)(2,1)S(1)} %get-tuple-element.76), channel_id=1, source_target_pairs={{0,16},{4,20},{8,24},{12,28},{16,0},{20,4},{24,8},{28,12},{1,17},{... | collective-permute-start | bytes 786440 | tf_op jit(solution)/shard_map/ppermute | solution.py:35
  781.6 29.0 %collective-permute-start.80 = (bf16[128,1024]{0,1:T(8,128)(2,1)S(1)}, bf16[128,1024]{0,1:T(8,128)(2,1)S(1)}, u32[]{:S(2)}, u32[]{:S(2)}) collective-permute-start(bf16[128,1024]{0,1:T(8,128)(2,1)S(1)} %get-tuple-element.65), channel_id=1, source_target_pairs={{0,16},{4,20},{8,24},{12,28},{16,0},{20,4},{24,8},{28,12},{1,17},{... | collective-permute-start | bytes 786440 | tf_op jit(solution)/shard_map/ppermute | solution.py:35
  781.6 29.0 %collective-permute-start.79 = (bf16[128,1024]{0,1:T(8,128)(2,1)S(1)}, bf16[128,1024]{0,1:T(8,128)(2,1)S(1)}, u32[]{:S(2)}, u32[]{:S(2)}) collective-permute-start(bf16[128,1024]{0,1:T(8,128)(2,1)S(1)} %get-tuple-element.63), channel_id=1, source_target_pairs={{0,8},{4,12},{8,0},{12,4},{16,24},{20,28},{24,16},{28,20},{1,9},{5... | collective-permute-start | bytes 786440 | tf_op jit(solution)/shard_map/ppermute | solution.py:35
  (137 other events, 1521.5 us)

commit v2 on v1

v2 whole, which is shorter than its diff:
```python
import functools
import math

import jax
import jax.numpy as jnp
from jax import lax
from jax.experimental import pallas as pl
from jax.experimental.pallas import tpu as pltpu
from jax.sharding import Mesh
from jax.sharding import PartitionSpec as P

HEADS = 16
AXES = {"dp": ("chip", "core"), "seq": ("slow", "fast"), "all": ("chip", "core", "slow", "fast")}
CORES = 2
EPSILON = 1e-06
MASKED = -1e30
VMEM_LIMIT = 60 * 1024 * 1024
F32 = jnp.float32
BF16 = jnp.bfloat16
NT = (((1,), (1,)), ((), ()))
TN = (((0,), (0,)), ((), ()))


def dot(left, right):
    return jnp.dot(left, right, preferred_element_type=F32)


def against(left, right):
    return lax.dot_general(left, right, NT, preferred_element_type=F32)


def over_rows(left, right):
    return lax.dot_general(left, right, TN, preferred_element_type=F32)


def axis_size(axis):
    return math.prod(lax.axis_size(name) for name in AXES[axis])


def swap(values, axis, mask):
    return lax.ppermute(values, AXES[axis], [(i, i ^ mask) for i in range(axis_size(axis))])


def chip_masks():
    return [CORES * k for k in range(1, axis_size("dp") // CORES)]


def bits(axis):
    found, mask = [], CORES if axis == "dp" else 1
    while mask < axis_size(axis):
        found.append(mask)
        mask *= 2
    return found


def seq_halves():
    fast, slow = lax.axis_size("fast"), lax.axis_size("slow")
    return [list(range(1, fast)), [fast * k for k in range(1, slow)]]


def gather_steps(shard, steps):
    held = shard
    for axis, masks in steps:
        held = jnp.stack([held] + [swap(held, axis, mask) for mask in masks])
    return held


SMEM_SPEC = pl.BlockSpec(memory_space=pltpu.SMEM)
ANY_SPEC = pl.BlockSpec(memory_space=pl.ANY)


def pass_kernel(*refs):
    del refs


def after(value, *earlier):
    return pl.pallas_call(
        pass_kernel,
        out_shape=jax.ShapeDtypeStruct(value.shape, value.dtype),
        in_specs=[ANY_SPEC] * (1 + len(earlier)),
        out_specs=ANY_SPEC,
        input_output_aliases={0: 0},
        name="after",
    )(value, *earlier)


class Pieces:
    def __init__(self, arrays, masks, rows, columns):
        self.arrays, self.masks, self.rows, self.columns = arrays, masks, rows, columns


def start_gather(shard):
    return Pieces([shard[None]], [[(0, 0)]], *shard.shape)


def gather_over(held, axis, masks):
    arrays, tables = list(held.arrays), list(held.masks)
    for mask in masks:
        for array, table in zip(held.arrays, held.masks):
            arrays.append(swap(array, axis, mask))
            tables.append([(d ^ mask, s) if axis == "dp" else (d, s ^ mask) for d, s in table])
    return Pieces(arrays, tables, held.rows, held.columns)


def pack(held):
    if len(held.arrays) == 1:
        return held
    return Pieces(
        [jnp.concatenate(held.arrays)], [[entry for table in held.masks for entry in table]], held.rows, held.columns
    )


def hold(held, *earlier):
    return Pieces([after(array, *earlier) for array in held.arrays], held.masks, held.rows, held.columns)


def gather_seq(held, masks):
    held = gather_over(held, "seq", masks)
    return pack(held) if axis_size("seq") > 4 else held


def whole_columns(shard, place, relative):
    held = lax.all_gather(lax.all_gather(shard, AXES["dp"], axis=0, tiled=True), AXES["seq"], axis=0)
    if relative:
        held = jnp.take(held, jnp.arange(held.shape[0]) ^ place[1], axis=0)
    full = jnp.moveaxis(held, 0, 1).reshape(held.shape[1], -1)
    return Pieces([full], None, *full.shape)


def narrow(shard):
    return shard.shape[1] % 128 != 0


class Bank:
    def __init__(self, array, start, columns):
        self.arrays, self.start, self.columns = [array], start, columns
        self.rows = array.shape[1]


def bank_copies(bank, ref, seq, first, columns, target, sems, column):
    seqs, found = axis_size("seq"), []
    for owner in range(bank.arrays[0].shape[0] // seqs):
        source = ref.at[owner * seqs + seq, :, pl.ds(bank.start + first, columns)]
        spot = target.at[pl.ds(owner * bank.rows, bank.rows), pl.ds(column, columns)]
        found.append(pltpu.make_async_copy(source, spot, sems.at[len(found)]))
    return found


def pack_kernel(*refs):
    *head, w_up_ref, w_down_ref, _, _, bank_ref = refs
    parts = [ref[...].T for ref in head] + [w_up_ref[...], w_down_ref[...].T]
    bank_ref[...] = jnp.concatenate(parts, 1)


def pack_bank(earlier, too, *weights):
    rows = weights[-2].shape[0]
    return pl.pallas_call(
        pack_kernel,
        out_shape=jax.ShapeDtypeStruct((rows, sum(weight.size for weight in weights) // rows), BF16),
        in_specs=[pl.BlockSpec(memory_space=pltpu.VMEM)] * len(weights) + [ANY_SPEC] * 2,
        compiler_params=pltpu.CompilerParams(vmem_limit_bytes=VMEM_LIMIT),
        name="pack_bank",
    )(*weights, earlier, too)


def unpack_kernel(chunk, sums_ref, up_ref, down_ref):
    for part in range(up_ref.shape[1] // chunk):
        start = 2 * part * chunk
        span = slice(part * chunk, (part + 1) * chunk)
        up_ref[:, span] = sums_ref[:, start : start + chunk].astype(F32)
        down_ref[span, :] = sums_ref[:, start + chunk : start + 2 * chunk].astype(F32).T


def unpack_sums(sums, units, chunk):
    rows = sums.shape[0]
    return pl.pallas_call(
        functools.partial(unpack_kernel, chunk),
        out_shape=tuple(jax.ShapeDtypeStruct(shape, F32) for shape in [(rows, units), (units, rows)]),
        compiler_params=pltpu.CompilerParams(vmem_limit_bytes=VMEM_LIMIT),
        name="unpack_sums",
    )(sums)


def weight_copies(pieces, refs, target, sems, place_ref, relative):
    if isinstance(pieces, Bank):
        copies, seqs = [], axis_size("seq")
        per_seq = pieces.arrays[0].shape[0] // seqs
        for seq in range(seqs):
            column = pl.multiple_of((place_ref[1] ^ seq) * pieces.columns, pieces.columns)
            part_sems = sems.at[pl.ds(seq * per_seq, per_seq)]
            copies += bank_copies(pieces, refs[0], seq, 0, pieces.columns, target, part_sems, column)
        return copies
    if pieces.masks is None:
        return [pltpu.make_async_copy(refs[0], target, sems.at[0])]
    copies, rows, columns = [], pieces.rows, pieces.columns
    for ref, table in zip(refs, pieces.masks):
        for entry, (dp_mask, seq_mask) in enumerate(table):
            row = pl.multiple_of((place_ref[0] ^ dp_mask) * rows, rows)
            target_rows = target.at[pl.ds(row, rows), :]
            if target.shape[1] != columns:
                if relative:
                    column = seq_mask * columns
                else:
                    column = pl.multiple_of((place_ref[1] ^ seq_mask) * columns, columns)
                target_rows = target.at[pl.ds(row, rows), pl.ds(column, columns)]
            copies.append(pltpu.make_async_copy(ref.at[entry], target_rows, sems.at[len(copies)]))
    return copies


def copy_count(pieces):
    if isinstance(pieces, Bank):
        return pieces.arrays[0].shape[0]
    return 1 if pieces.masks is None else sum(len(table) for table in pieces.masks)


def assemble_kernel(pieces, place_ref, *rest):
    refs, out_ref, sems = rest[:-2], rest[-2], rest[-1]
    copies = weight_copies(pieces, refs, out_ref, sems, place_ref, False)
    for copy in copies:
        copy.start()
    for copy in copies:
        copy.wait()


def assemble(pieces, place, shape):
    return pl.pallas_call(
        functools.partial(assemble_kernel, pieces),
        out_shape=jax.ShapeDtypeStruct(shape, BF16),
        in_specs=[SMEM_SPEC] + [ANY_SPEC] * len(pieces.arrays),
        out_specs=pl.BlockSpec(memory_space=pltpu.VMEM),
        scratch_shapes=[pltpu.SemaphoreType.DMA((copy_count(pieces),))],
        compiler_params=pltpu.CompilerParams(vmem_limit_bytes=VMEM_LIMIT),
        cost_estimate=pl.CostEstimate(flops=0, bytes_accessed=4 * math.prod(shape), transcendentals=0),
        name="assemble",
    )(place, *pieces.arrays)


def send_seq(held):
    total = held[0]
    for mask in range(1, held.shape[0]):
        total = total + swap(held[mask].astype(BF16), "seq", mask).astype(F32)
    return total


def send_chips(held):
    total = held[0]
    for mask in chip_masks():
        total = total + swap(held[mask // CORES].astype(BF16), "dp", mask).astype(F32)
    return total


def halve_chips(held):
    for mask in reversed(bits("dp")):
        count = held.shape[0] // 2
        held = held[:count] + swap(held[count:].astype(BF16), "dp", mask).astype(F32)
    return held[0]


def add_cores(keep, give):
    return keep.astype(F32) + swap(give, "dp", 1).astype(F32)


def split_rows(place_ref, source_ref, rows, chip, core, by_mask):
    owner = place_ref[0] ^ (chip * CORES + core) if by_mask else chip * CORES + (place_ref[0] % CORES ^ core)
    return source_ref[pl.ds(pl.multiple_of(owner * rows, rows), rows), :]


def weight_grad_kernel(count, seqs, by_mask, place_ref, *rest):
    x_refs, y_ref, (keep_ref, give_ref, xt_ref) = rest[:count], rest[count], rest[-3:]
    chip = pl.program_id(0)
    per_piece = len(y_ref.shape) == 3
    rows, columns = keep_ref.shape[-2:]
    wide = x_refs[0].shape[1]

    @pl.when(chip == 0)
    def _():
        for piece, ref in enumerate(x_refs):
            if per_piece:
                xt_ref[:, piece * ref.shape[0] : (piece + 1) * ref.shape[0]] = ref[...].T
            else:
                xt_ref[piece * wide : (piece + 1) * wide, :] = ref[...].T

    y = y_ref[...].reshape(-1, y_ref.shape[-1])
    for core, out_ref in ((0, keep_ref), (1, give_ref)):
        result = dot(split_rows(place_ref, xt_ref, rows, chip, core, by_mask), y).astype(BF16)
        for seq in range(seqs):
            out_ref[seq, 0] = result[:, seq * columns : (seq + 1) * columns]


def weight_grad(place, xs, y, rows, seqs, by_mask, *earlier):
    chips = axis_size("dp") // CORES
    tokens, wide = xs[0].shape
    columns = y.shape[-1] // seqs
    shape = (wide, len(xs) * tokens) if y.ndim == 3 else (len(xs) * wide, tokens)
    out = jax.ShapeDtypeStruct((seqs, chips, rows, columns), BF16)
    spec = pl.BlockSpec((seqs, 1, rows, columns), lambda i: (0, i, 0, 0))
    constant = lambda array: pl.BlockSpec(array.shape, lambda i: (0,) * array.ndim)
    return pl.pallas_call(
        functools.partial(weight_grad_kernel, len(xs), seqs, by_mask),
        grid=(chips,),
        out_shape=(out, out),
        in_specs=[SMEM_SPEC] + [constant(x) for x in xs] + [constant(y)] + [ANY_SPEC] * len(earlier),
        out_specs=(spec, spec),
        scratch_shapes=[pltpu.VMEM(shape, BF16)],
        compiler_params=pltpu.CompilerParams(vmem_limit_bytes=VMEM_LIMIT),
        cost_estimate=pl.CostEstimate(
            flops=2 * math.prod(shape) * columns * seqs,
            bytes_accessed=2 * (math.prod(shape) + y.size) + 2 * shape[0] * columns * seqs,
            transcendentals=0,
        ),
        name="weight_grad",
    )(place, *xs, y, *earlier)


def qkv_kernel(width, scale, x_ref, w_ref, cos_ref, sin_ref, *rest):
    out_ref = rest[-1]
    half = width // 2
    projected = dot(x_ref[0], w_ref[...])
    cosine, sine = cos_ref[0], sin_ref[0]
    for part, factor in ((0, scale), (1, 1.0)):
        low = projected[:, part * width : part * width + half]
        high = projected[:, part * width + half : (part + 1) * width]
        out_ref[0, 0, :, part * width : part * width + half] = ((low * cosine - high * sine) * factor).astype(BF16)
        out_ref[0, 0, :, part * width + half : (part + 1) * width] = ((high * cosine + low * sine) * factor).astype(BF16)
    out_ref[0, 0, :, 2 * width :] = projected[:, 2 * width :].astype(BF16)


def project_piece(piece, normed, weights, cos_table, sin_table, held, scale):
    rows, frames, model = normed.shape
    pieces = cos_table.shape[0]
    width = weights.shape[1] // 3
    in_specs = [
        pl.BlockSpec((1, frames, model), lambda r: (r, 0, 0)),
        pl.BlockSpec((model, 3 * width), lambda r: (0, 0)),
        pl.BlockSpec((1, frames, width // 2), lambda r: (piece, 0, 0)),
        pl.BlockSpec((1, frames, width // 2), lambda r: (piece, 0, 0)),
    ]
    arrays = [normed, weights, cos_table, sin_table]
    aliases = {}
    if held is not None:
        in_specs.append(pl.BlockSpec(memory_space=pl.ANY))
        arrays.append(held)
        aliases = {4: 0}
    return pl.pallas_call(
        functools.partial(qkv_kernel, width, scale),
        grid=(rows,),
        out_shape=jax.ShapeDtypeStruct((pieces, rows, frames, 3 * width), BF16),
        in_specs=in_specs,
        out_specs=pl.BlockSpec((1, 1, frames, 3 * width), lambda r: (piece, r, 0, 0)),
        input_output_aliases=aliases,
        compiler_params=pltpu.CompilerParams(vmem_limit_bytes=VMEM_LIMIT),
        cost_estimate=pl.CostEstimate(
            flops=2 * rows * frames * model * 3 * width, bytes_accessed=5 * rows * frames * model, transcendentals=0
        ),
        name="project",
    )(*arrays)


def spread_back_kernel(grad_ref, weight_ref, *out_refs):
    piece = pl.program_id(0)
    result = against(grad_ref[0, 0], weight_ref[...]).astype(BF16)
    for position, ref in enumerate(out_refs):

        @pl.when(piece == position)
        def _():
            ref[0] = result


def spread_back(grad_qkv, weights):
    pieces, rows, frames, triple = grad_qkv.shape
    model = weights.shape[0]

    def out_spec(position):
        return pl.BlockSpec(
            (1, frames, model),
            lambda m, r: (jnp.where(m < position, 0, jnp.where(m == position, r, rows - 1)), 0, 0),
        )

    return pl.pallas_call(
        spread_back_kernel,
        grid=(pieces - 1, rows),
        out_shape=(jax.ShapeDtypeStruct((rows, frames, model), BF16),) * (pieces - 1),
        in_specs=[
            pl.BlockSpec((1, 1, frames, triple), lambda m, r: (m + 1, r, 0, 0)),
            pl.BlockSpec(weights.shape, lambda m, r: (0, 0)),
        ],
        out_specs=tuple(out_spec(position) for position in range(pieces - 1)),
        compiler_params=pltpu.CompilerParams(vmem_limit_bytes=VMEM_LIMIT),
        cost_estimate=pl.CostEstimate(
            flops=2 * (pieces - 1) * rows * frames * triple * model,
            bytes_accessed=2 * pieces * rows * frames * (triple + model),
            transcendentals=0,
        ),
        name="spread_back",
    )(grad_qkv, weights)


def head_lanes(shape, heads, width, split):
    lane = lax.broadcasted_iota(jnp.int32, shape, 1)
    size = width // heads
    if split:
        return (lane % (width // 2)) // (size // 2)
    return lane // size


def spread_back_kernel(grad_ref, weight_ref, *out_refs):
    piece = pl.program_id(0)
    result = against(grad_ref[0, 0], weight_ref[...]).astype(BF16)
    for position, ref in enumerate(out_refs):

        @pl.when(piece == position)
        def _():
            ref[0] = result


def spread_back(grad_qkv, weights):
    pieces, rows, frames, triple = grad_qkv.shape
    model = weights.shape[0]

    def out_spec(position):
        return pl.BlockSpec(
            (1, frames, model),
            lambda m, r: (jnp.where(m < position, 0, jnp.where(m == position, r, rows - 1)), 0, 0),
        )

    return pl.pallas_call(
        spread_back_kernel,
        grid=(pieces - 1, rows),
        out_shape=(jax.ShapeDtypeStruct((rows, frames, model), BF16),) * (pieces - 1),
        in_specs=[
            pl.BlockSpec((1, 1, frames, triple), lambda m, r: (m + 1, r, 0, 0)),
            pl.BlockSpec(weights.shape, lambda m, r: (0, 0)),
        ],
        out_specs=tuple(out_spec(position) for position in range(pieces - 1)),
        compiler_params=pltpu.CompilerParams(vmem_limit_bytes=VMEM_LIMIT),
        cost_estimate=pl.CostEstimate(
            flops=2 * (pieces - 1) * rows * frames * triple * model,
            bytes_accessed=2 * pieces * rows * frames * (triple + model),
            transcendentals=0,
        ),
        name="spread_back",
    )(grad_qkv, weights)


def head_lanes(shape, heads, width, split):
    lane = lax.broadcasted_iota(jnp.int32, shape, 1)
    size = width // heads
    if split:
        return (lane % (width // 2)) // (size // 2)
    return lane // size


def column_of(row, lanes):
    return jnp.broadcast_to(row, (128, row.shape[1])).T[:, :lanes]


def attend_kernel(heads, width, qkv_ref, seg_ref, *rest):
    pieces, _, frames, _ = qkv_ref.shape
    out_refs, (lse_ref, vt_ref, ot_ref, seg_col_ref) = rest[:pieces], rest[pieces:]
    length = pieces * frames
    step = pl.program_id(1)
    size = width // heads
    keys = qkv_ref[:, 0, :, width : 2 * width].reshape(length, width)

    @pl.when(step == 0)
    def _():
        vt_ref[...] = qkv_ref[:, 0, :, 2 * width :].reshape(length, width).T
        for piece in range(pieces):
            seg_col_ref[piece * frames : (piece + 1) * frames, :] = column_of(seg_ref[0, piece : piece + 1, :], 128)

    queries = qkv_ref[step, 0, :, :width]
    owner = head_lanes((frames, width), heads, width, True)
    allowed = seg_col_ref[:, :1] == seg_ref[0, pl.ds(step, 1), :]
    for head in range(heads):
        masked = jnp.where(owner == head, queries, jnp.zeros_like(queries))
        scores = jnp.where(allowed, against(keys, masked), MASKED)
        highest = jnp.max(scores, 0, keepdims=True)
        raised = jnp.exp(scores - highest)
        total = jnp.sum(raised, 0, keepdims=True)
        lse_ref[0, 0, head : head + 1, :] = highest + jnp.log(total)
        result = dot(vt_ref[head * size : (head + 1) * size, :], raised.astype(BF16))
        ot_ref[head * size : (head + 1) * size, :] = result / total
    result = ot_ref[...].T.astype(BF16)
    for piece in range(pieces):

        @pl.when(step == piece)
        def _():
            out_refs[piece][0] = result


def attend(qkv, seg, heads):
    pieces, rows, frames, triple = qkv.shape
    width = triple // 3
    length = pieces * frames
    results = pl.pallas_call(
        functools.partial(attend_kernel, heads, width),
        grid=(rows, pieces),
        out_shape=(jax.ShapeDtypeStruct((rows, frames, width), BF16),) * pieces
        + (jax.ShapeDtypeStruct((rows, pieces, heads, frames), F32),),
        in_specs=[
            pl.BlockSpec((pieces, 1, frames, triple), lambda r, s: (0, r, 0, 0)),
            pl.BlockSpec((1, pieces, frames), lambda r, s: (r, 0, 0)),
        ],
        out_specs=(pl.BlockSpec((1, frames, width), lambda r, s: (r, 0, 0)),) * pieces
        + (pl.BlockSpec((1, 1, heads, frames), lambda r, s: (r, s, 0, 0)),),
        scratch_shapes=[
            pltpu.VMEM((width, length), BF16),
            pltpu.VMEM((width, frames), F32),
            pltpu.VMEM((length, 128), F32),
        ],
        compiler_params=pltpu.CompilerParams(vmem_limit_bytes=VMEM_LIMIT),
        cost_estimate=pl.CostEstimate(
            flops=4 * rows * length * length * 256 * heads,
            bytes_accessed=8 * rows * length * width,
            transcendentals=rows * heads * length * length,
        ),
        name="attend",
    )(qkv, seg)
    return results[:pieces], results[pieces]


def attend_back_kernel(heads, width, scale, qkv_ref, seg_ref, lse_ref, cos_ref, sin_ref, *rest):
    pieces, _, frames, _ = qkv_ref.shape
    out_refs, grad_refs = rest[:pieces], rest[pieces : 2 * pieces]
    result_ref, kt_ref, dk_ref, dv_ref, dqt_ref, seg_col_ref, out_ref, grad_ref = rest[2 * pieces :]
    length = pieces * frames
    step = pl.program_id(1)
    size, half = width // heads, width // 2
    keys = qkv_ref[:, 0, :, width : 2 * width].reshape(length, width)
    values = qkv_ref[:, 0, :, 2 * width :].reshape(length, width)

    @pl.when(step == 0)
    def _():
        kt_ref[...] = keys.T
        dk_ref[...] = jnp.zeros_like(dk_ref)
        dv_ref[...] = jnp.zeros_like(dv_ref)
        for piece in range(pieces):
            seg_col_ref[piece * frames : (piece + 1) * frames, :] = column_of(seg_ref[0, piece : piece + 1, :], 128)
            out_ref[piece] = out_refs[piece][0]
            grad_ref[piece] = grad_refs[piece][0]

    queries = qkv_ref[step, 0, :, :width]
    grad = grad_ref[step]
    query_owner = head_lanes((frames, width), heads, width, True)
    value_owner = head_lanes((frames, width), heads, width, False)
    allowed = seg_col_ref[:, :1] == seg_ref[0, pl.ds(step, 1), :]
    product = grad.astype(F32) * out_ref[step].astype(F32)
    picker = lax.broadcasted_iota(jnp.int32, (8, width), 1) // size == lax.broadcasted_iota(jnp.int32, (8, width), 0)
    inner = lax.dot_general(
        picker.astype(F32), product, NT, precision=lax.Precision.HIGHEST, preferred_element_type=F32
    )
    for head in range(heads):
        masked = jnp.where(query_owner == head, queries, jnp.zeros_like(queries))
        masked_grad = jnp.where(value_owner == head, grad, jnp.zeros_like(grad))
        scores = against(keys, masked)
        weights = jnp.where(allowed, jnp.exp(scores - lse_ref[0, 0, head : head + 1, :]), 0.0)
        grad_weights = against(values, masked_grad)
        grad_scores = (weights * (grad_weights - inner[head : head + 1, :])).astype(BF16)
        dv_ref[...] += dot(weights.astype(BF16), masked_grad)
        dk_ref[...] += dot(grad_scores, masked)
        low, high = head * size // 2, half + head * size // 2
        head_keys = jnp.concatenate([kt_ref[low : low + size // 2, :], kt_ref[high : high + size // 2, :]], 0)
        part = dot(head_keys, grad_scores)
        dqt_ref[low : low + size // 2, :] = part[: size // 2]
        dqt_ref[high : high + size // 2, :] = part[size // 2 :]

    def unrotate(values, cosine, sine):
        low, high = values[:, :half], values[:, half:]
        return (low * cosine + high * sine).astype(BF16), (high * cosine - low * sine).astype(BF16)

    low, high = unrotate(dqt_ref[...].T * scale, cos_ref[step], sin_ref[step])
    result_ref[step, 0, :, :half] = low
    result_ref[step, 0, :, half:width] = high

    @pl.when(step == pieces - 1)
    def _():
        for piece in range(pieces):
            span = slice(piece * frames, (piece + 1) * frames)
            low, high = unrotate(dk_ref[span, :], cos_ref[piece], sin_ref[piece])
            result_ref[piece, 0, :, width : width + half] = low
            result_ref[piece, 0, :, width + half : 2 * width] = high
            result_ref[piece, 0, :, 2 * width :] = dv_ref[span, :].astype(BF16)


def attend_back(qkv, seg, lse, cos_table, sin_table, outs, grads, heads, scale):
    pieces, rows, frames, triple = qkv.shape
    width = triple // 3
    length = pieces * frames
    whole = pl.BlockSpec((pieces, 1, frames, triple), lambda r, s: (0, r, 0, 0))
    table = pl.BlockSpec((pieces, frames, width // 2), lambda r, s: (0, 0, 0))
    block = pl.BlockSpec((1, frames, width), lambda r, s: (r, 0, 0))
    return pl.pallas_call(
        functools.partial(attend_back_kernel, heads, width, scale),
        grid=(rows, pieces),
        out_shape=jax.ShapeDtypeStruct(qkv.shape, BF16),
        in_specs=[
            whole,
            pl.BlockSpec((1, pieces, frames), lambda r, s: (r, 0, 0)),
            pl.BlockSpec((1, 1, heads, frames), lambda r, s: (r, s, 0, 0)),
            table,
            table,
        ]
        + [block] * (2 * pieces),
        out_specs=whole,
        scratch_shapes=[
            pltpu.VMEM((width, length), BF16),
            pltpu.VMEM((length, width), F32),
            pltpu.VMEM((length, width), F32),
            pltpu.VMEM((width, frames), F32),
            pltpu.VMEM((length, 128), F32),
            pltpu.VMEM((pieces, frames, width), BF16),
            pltpu.VMEM((pieces, frames, width), BF16),
        ],
        compiler_params=pltpu.CompilerParams(vmem_limit_bytes=VMEM_LIMIT),
        cost_estimate=pl.CostEstimate(
            flops=10 * rows * length * length * 256 * heads,
            bytes_accessed=16 * rows * length * width,
            transcendentals=rows * heads * length * length,
        ),
        name="attend_back",
    )(qkv, seg, lse, cos_table, sin_table, *outs, *grads)


def mlp_kernel(bank, chunk, place_ref, normed_ref, grad_ref, bank_ref, *rest):
    fed_ref, gn_ref, grads_ref, nt_ref, gt_ref, weight_ref, result_ref, sems = rest
    step, rows = pl.program_id(0), bank.rows
    units = bank.columns // 2
    per_place = units // chunk
    half = bank.arrays[0].shape[0] // axis_size("seq")

    def copies(block, slot):
        start = (block % per_place) * chunk
        target, found = weight_ref.at[slot], []
        for which in range(2):
            found += bank_copies(
                bank, bank_ref, block // per_place, which * units + start, chunk, target,
                sems.at[slot, pl.ds(which * half, half)], which * chunk,
            )
        return found

    @pl.when(step == 0)
    def _():
        for copy in copies(0, 0):
            copy.start()
        nt_ref[...] = normed_ref[...].T
        gt_ref[...] = grad_ref[...].T
        fed_ref[...] = jnp.zeros_like(fed_ref)
        gn_ref[...] = jnp.zeros_like(gn_ref)

    for block in range(1, axis_size("seq") * per_place):

        @pl.when(step + 1 == block)
        def _():
            for copy in copies(block, block % 2):
                copy.start()

    slot = step % 2
    for copy in copies(0, slot):
        copy.wait()
    up, down = weight_ref[slot, :, :chunk], weight_ref[slot, :, chunk:]
    before = dot(normed_ref[...], up)
    square = before * before
    factor = math.sqrt(2.0 / math.pi)
    bent = jnp.tanh(factor * (before + 0.044715 * (square * before)))
    activated = (0.5 * before * (1.0 + bent)).astype(BF16)
    slope = 0.5 * (1.0 + bent) + 0.5 * before * (1.0 - bent * bent) * (factor * (1.0 + 3 * 0.044715 * square))
    grad_before = (dot(grad_ref[...], down) * slope).astype(BF16)
    fed_ref[...] += against(activated, down)
    gn_ref[...] += against(grad_before, up)
    result_ref[:, :chunk] = dot(nt_ref[...], grad_before).astype(BF16)
    result_ref[:, chunk:] = dot(gt_ref[...], activated).astype(BF16)
    for chip in range(grads_ref.shape[2]):
        for core in range(CORES):
            owner = chip * CORES + core
            grads_ref[core, 0, chip] = result_ref[owner * rows : (owner + 1) * rows, :]


def mlp(place, normed, grad, bank):
    tokens, model = normed.shape
    seqs, chips = axis_size("seq"), axis_size("dp") // CORES
    units = bank.columns // 2
    chunk = min(512, units)
    per_place = units // chunk
    whole = pl.BlockSpec((tokens, model), lambda i: (0, 0))
    hidden = seqs * units
    return pl.pallas_call(
        functools.partial(mlp_kernel, bank, chunk),
        grid=(seqs * per_place,),
        out_shape=(jax.ShapeDtypeStruct((tokens, model), F32),) * 2
        + (jax.ShapeDtypeStruct((CORES, seqs, chips, bank.rows, 2 * units), BF16),),
        in_specs=[SMEM_SPEC, whole, whole, ANY_SPEC],
        out_specs=(
            whole,
            whole,
            pl.BlockSpec(
                (CORES, 1, chips, bank.rows, 2 * chunk), lambda i: (0, i // per_place, 0, 0, i % per_place)
            ),
        ),
        scratch_shapes=[
            pltpu.VMEM((model, tokens), BF16),
            pltpu.VMEM((model, tokens), BF16),
            pltpu.VMEM((2, model, 2 * chunk), BF16),
            pltpu.VMEM((model, 2 * chunk), BF16),
            pltpu.SemaphoreType.DMA((2, 2 * CORES * chips)),
        ],
        compiler_params=pltpu.CompilerParams(vmem_limit_bytes=VMEM_LIMIT),
        cost_estimate=pl.CostEstimate(
            flops=12 * tokens * model * hidden,
            bytes_accessed=8 * model * hidden + 12 * tokens * model,
            transcendentals=tokens * hidden,
        ),
        name="mlp",
    )(place, normed, grad, *bank.arrays)


def standardize(values):
    centre = values - jnp.mean(values, -1, keepdims=True)
    inverse = lax.rsqrt(jnp.mean(centre * centre, -1, keepdims=True) + EPSILON)
    return centre * inverse, inverse


def standardize_back(grad, standard, inverse):
    return inverse * (
        grad - jnp.mean(grad, -1, keepdims=True) - standard * jnp.mean(grad * standard, -1, keepdims=True)
    )


def utterance_of(seg_ref):
    return column_of(seg_ref[0], 1)


def by_frame(owner, mod_ref, part):
    count = mod_ref.shape[1]
    result = mod_ref[0, count - 1, part : part + 1, :]
    for position in range(count - 2, -1, -1):
        result = jnp.where(owner == float(position), mod_ref[0, position, part : part + 1, :], result)
    return result


def add_up(owner, values, out_ref, part, count):
    for position in range(count):
        out_ref[0, part, position : position + 1, :] = jnp.sum(
            jnp.where(owner == float(position), values, 0.0), 0, keepdims=True
        )


def load_weight(pieces, refs, target, sems, place_ref, relative):
    @pl.when(pl.program_id(0) == 0)
    def _():
        copies = weight_copies(pieces, refs, target, sems, place_ref, relative)
        for copy in copies:
            copy.start()
        for copy in copies:
            copy.wait()


def row_call(kernel, name, place, rows, by_row, fixed, pieces, weight_shape, outs, flops, earlier=()):
    row_spec = lambda shape: pl.BlockSpec((1,) + tuple(shape[1:]), lambda r: (r,) + (0,) * (len(shape) - 1))
    fixed_specs = [pl.BlockSpec(array.shape, lambda r, n=array.ndim: (0,) * n) for array in fixed]
    scalars = [array for array in place]
    size = sum(array.size * array.dtype.itemsize for array in by_row) + 2 * math.prod(weight_shape)
    return pl.pallas_call(
        kernel,
        grid=(rows,),
        out_shape=tuple(outs),
        in_specs=[SMEM_SPEC] * len(scalars)
        + [row_spec(array.shape) for array in by_row]
        + fixed_specs
        + [ANY_SPEC] * (len(pieces.arrays) + len(earlier)),
        out_specs=tuple(row_spec(out.shape) for out in outs),
        scratch_shapes=[pltpu.VMEM(weight_shape, BF16), pltpu.SemaphoreType.DMA((copy_count(pieces),))],
        compiler_params=pltpu.CompilerParams(vmem_limit_bytes=VMEM_LIMIT),
        cost_estimate=pl.CostEstimate(flops=flops, bytes_accessed=2 * size, transcendentals=0),
        name=name,
    )(*scalars, *by_row, *fixed, *pieces.arrays, *earlier)


def enter_kernel(pieces, place_ref, coef_ref, frames_ref, skip_ref, cond_ref, seg_ref, mod_ref, *rest):
    refs, (hidden_ref, normed_ref, weight_ref, sems) = rest[:-4], rest[-4:]
    load_weight(pieces, refs, weight_ref, sems, place_ref, False)
    row, model = pl.program_id(0), frames_ref.shape[2]
    owner = utterance_of(seg_ref)
    count = mod_ref.shape[1]
    factor = coef_ref[row, count - 1]
    for position in range(count - 2, -1, -1):
        factor = jnp.where(owner == float(position), coef_ref[row, position], factor)
    hidden = dot(frames_ref[0], weight_ref[:model, :]) + dot(skip_ref[0], weight_ref[model:, :])
    hidden = hidden + factor * cond_ref[0].astype(F32)
    hidden_ref[0] = hidden
    standard, _ = standardize(hidden)
    normed_ref[0] = (standard * (1.0 + by_frame(owner, mod_ref, 1)) + by_frame(owner, mod_ref, 0)).astype(BF16)


def branch_kernel(pieces, count, place_ref, *rest):
    blocks, (hidden_ref, cot_ref, seg_ref, mod_ref) = rest[:count], rest[count : count + 4]
    refs = rest[count + 4 : -7]
    attn_ref, branch_ref, middle_ref, normed_ref, grad_ref, weight_ref, sems = rest[-7:]
    load_weight(pieces, refs, weight_ref, sems, place_ref, True)
    owner = utterance_of(seg_ref)
    attn = jnp.concatenate([block[0] for block in blocks], -1)
    attn_ref[0] = attn
    branch = against(attn, weight_ref[...])
    branch_ref[0] = branch
    middle = hidden_ref[0] + by_frame(owner, mod_ref, 2) * branch
    middle_ref[0] = middle
    standard, _ = standardize(middle)
    normed_ref[0] = (standard * (1.0 + by_frame(owner, mod_ref, 4)) + by_frame(owner, mod_ref, 3)).astype(BF16)
    grad_ref[0] = (by_frame(owner, mod_ref, 5) * cot_ref[0].astype(F32)).astype(BF16)


def middle_back_kernel(pieces, seqs, place_ref, middle_ref, fed_ref, gn_ref, cot_ref, branch_ref, seg_ref, mod_ref, *rest):
    refs = rest[: len(pieces.arrays)]
    output_ref, grad_ref, grad_branch_ref, sums_ref = rest[len(refs) : len(refs) + 4]
    block_refs, (weight_ref, sems) = rest[len(refs) + 4 : -2], rest[-2:]
    load_weight(pieces, refs, weight_ref, sems, place_ref, True)
    owner, count = utterance_of(seg_ref), mod_ref.shape[1]
    middle, fed, grad_norm, grad_out = middle_ref[0], fed_ref[0], gn_ref[0], cot_ref[0].astype(F32)
    output_ref[0] = (middle + by_frame(owner, mod_ref, 5) * fed).astype(BF16)
    standard, inverse = standardize(middle)
    grad_middle = grad_out + standardize_back(grad_norm * (1.0 + by_frame(owner, mod_ref, 4)), standard, inverse)
    grad_ref[0] = grad_middle
    grad_branch = (by_frame(owner, mod_ref, 2) * grad_middle).astype(BF16)
    grad_branch_ref[0] = grad_branch
    grad_attn = dot(grad_branch, weight_ref[...]).astype(BF16)
    width = grad_attn.shape[1] // seqs
    for seq in range(seqs):
        block_refs[seq][0] = grad_attn[:, seq * width : (seq + 1) * width]
    add_up(owner, grad_middle * branch_ref[0], sums_ref, 0, count)
    add_up(owner, grad_norm, sums_ref, 1, count)
    add_up(owner, grad_norm * standard, sums_ref, 2, count)
    add_up(owner, grad_out * fed, sums_ref, 3, count)


def leave_kernel(pieces, seqs, place_ref, hidden_ref, grad_middle_ref, own_ref, *rest):
    got = rest[: seqs - 1]
    seg_ref, mod_ref, qkv_ref = rest[seqs - 1 : seqs + 2]
    refs = rest[seqs + 2 : seqs + 2 + len(pieces.arrays)]
    columns_ref, frames_ref, skip_ref, sums_ref, weight_ref, sems = rest[-6:]
    load_weight(pieces, refs, weight_ref, sems, place_ref, False)
    owner, count = utterance_of(seg_ref), mod_ref.shape[1]
    grad_norm = against(own_ref[0], qkv_ref[...])
    for ref in got:
        grad_norm = grad_norm + ref[0].astype(F32)
    standard, inverse = standardize(hidden_ref[0])
    grad = standardize_back(grad_norm * (1.0 + by_frame(owner, mod_ref, 1)), standard, inverse)
    grad_hidden = (grad_middle_ref[0] + grad).astype(BF16)
    model = grad_hidden.shape[1]
    frames_ref[0] = against(grad_hidden, weight_ref[:model, :]).astype(BF16)
    skip_ref[0] = against(grad_hidden, weight_ref[model:, :]).astype(BF16)
    add_up(owner, grad_norm, sums_ref, 0, count)
    add_up(owner, grad_norm * standard, sums_ref, 1, count)
    width = model // seqs
    turned = grad_hidden.astype(F32)
    bit = 1
    while bit < seqs:
        parts = [turned[:, (s ^ bit) * width : ((s ^ bit) + 1) * width] for s in range(seqs)]
        turned = jnp.where((place_ref[1] // bit) % 2 == 1, jnp.concatenate(parts, -1), turned)
        bit *= 2
    columns_ref[0] = turned.astype(BF16)


def time_embed(flow_values, model_width):
    half_dim = model_width // 2
    frequency = jnp.exp(jnp.arange(half_dim, dtype=F32) * (-math.log(10000.0) / half_dim))
    angles = 1000.0 * flow_values[..., None] * frequency
    return jnp.concatenate([jnp.sin(angles), jnp.cos(angles)], -1)


def body(
    frames, skip_in, cond, seg_ids, drop_flags, flow_times, w_skip, w_qkv, w_out, w_up, w_down, w_mod, cotangent
):
    row_count, frame_count, model = frames.shape
    seq_size, dp_size = axis_size("seq"), axis_size("dp")
    chips = dp_size // CORES
    dp, seq = lax.axis_index(AXES["dp"]), lax.axis_index(AXES["seq"])
    place = jnp.stack([dp, seq]).astype(jnp.int32)
    head_dim = model // HEADS
    heads = HEADS // seq_size
    width = heads * head_dim
    half = head_dim // 2
    scale = head_dim ** (-0.5)
    tokens = row_count * frame_count
    segs = drop_flags.shape[1]
    frame_shape = (row_count, frame_count, model)
    partners = range(1, seq_size)
    fast, slow = seq_halves()
    rows = w_up.shape[0]
    shape_of = jax.ShapeDtypeStruct

    by_head = w_qkv.reshape(w_qkv.shape[0], heads, 3, 2, half)
    qkv_shard = jnp.concatenate(
        [
            by_head[:, :, 0].swapaxes(1, 2).reshape(-1, width),
            by_head[:, :, 1].swapaxes(1, 2).reshape(-1, width),
            by_head[:, :, 2].reshape(-1, width),
        ],
        1,
    )
    skip_parts = pack(gather_over(start_gather(w_skip), "dp", chip_masks()))

    skip_near = skip_parts.arrays[0]

    small = jnp.concatenate([flow_times, drop_flags.astype(F32)], 1)
    small = gather_steps(small, [("dp", [mask]) for mask in bits("dp") + [1]])
    small = small.reshape((CORES, chips) + small.shape[-2:])
    dropped = jnp.sum(small[..., segs:])
    slots = float(row_count * segs * dp_size)
    cond_scale = slots / jnp.maximum(slots - dropped, 1.0)
    utterances = row_count * segs
    activity = jax.nn.silu(time_embed(small[..., :segs], model)).astype(BF16).reshape(dp_size * utterances, model)
    mod_rows, mod_columns = w_mod.shape
    activity = lax.dynamic_slice_in_dim(activity, dp * mod_rows, mod_rows, 1)
    coefficients = (1.0 - drop_flags.astype(F32)) * cond_scale

    if narrow(w_skip):
        skip_parts = whole_columns(w_skip, place, False)
        arrived = skip_parts.arrays[0]
    else:
        skip_parts = gather_over(skip_parts, "seq", partners)
        arrived = skip_parts.arrays[-1]
        skip_parts = gather_over(skip_parts, "dp", [1])

    partial = dot(activity, w_mod).reshape(CORES, chips, utterances, mod_columns)
    modulation = partial[0] + swap(partial[1], "dp", 1)
    for mask in reversed(bits("dp")):
        count = modulation.shape[0] // 2
        modulation = modulation[:count] + swap(modulation[count:], "dp", mask)
    modulation = modulation[0]
    extra = -(-tokens // mod_columns)
    numbers = jnp.pad(seg_ids.astype(F32).reshape(-1), (0, extra * mod_columns - tokens)).reshape(extra, mod_columns)
    own_mod = jnp.concatenate([modulation, numbers])
    all_mod = jnp.stack([own_mod] + [swap(own_mod, "seq", mask) for mask in partners])
    segments = all_mod[:, utterances:].reshape(seq_size, -1)[:, :tokens].reshape(seq_size, row_count, frame_count)
    segments = segments.swapaxes(0, 1)
    modulation = jnp.take(all_mod[:, :utterances], jnp.arange(seq_size) ^ seq, axis=0)
    modulation = modulation.swapaxes(0, 1).reshape(row_count, segs, 6, model)
    seg_here = segments[:, :1]

    units = w_up.shape[1]
    if narrow(w_out.T):
        out_parts = whole_columns(w_out.T, place, True)
        bank = pack_bank(arrived, all_mod, w_up, w_down)
    else:
        bank = pack_bank(arrived, all_mod, w_out, w_up, w_down)
    bank = lax.all_gather(bank, AXES["all"], axis=0)
    lead = bank.shape[2] - 2 * units
    if lead:
        out_parts = Bank(bank, 0, lead)
    bank = Bank(bank, lead, 2 * units)

    qkv_full = assemble(
        gather_over(pack(gather_over(start_gather(after(qkv_shard, arrived)), "dp", chip_masks())), "dp", [1]),
        place,
        (dp_size * rows, 3 * width),
    )
    hidden, normed = row_call(
        functools.partial(enter_kernel, skip_parts),
        "enter",
        [place, coefficients],
        row_count,
        [frames, skip_in, cond, seg_here, modulation],
        [],
        skip_parts,
        (2 * model, model),
        [shape_of(frame_shape, F32), shape_of(frame_shape, BF16)],
        4 * tokens * model * model,
    )

    positions = (jnp.arange(seq_size) ^ seq)[:, None] * frame_count + jnp.arange(frame_count)
    frequency = jnp.exp((jnp.arange(width // 2) % half).astype(F32) * (-2.0 * math.log(10000.0) / head_dim))
    angles = positions.astype(F32)[..., None] * frequency
    cos_table, sin_table = jnp.cos(angles), jnp.sin(angles)

    pieces = [normed] + [swap(normed, "seq", mask) for mask in partners]
    qkv = None
    for position, piece in enumerate(pieces):
        qkv = project_piece(position, piece, qkv_full, cos_table, sin_table, qkv, scale)

    attended, lse = attend(qkv, segments, heads)
    blocks = [attended[0]] + [swap(attended[mask], "seq", mask) for mask in partners]
    attn, branch, middle, normed_two, grad_fed = row_call(
        functools.partial(branch_kernel, out_parts, seq_size),
        "branch",
        [place],
        row_count,
        blocks + [hidden, cotangent, seg_here, modulation],
        [],
        out_parts,
        (model, model),
        [
            shape_of(frame_shape, BF16),
            shape_of(frame_shape, F32),
            shape_of(frame_shape, F32),
            shape_of(frame_shape, BF16),
            shape_of(frame_shape, BF16),
        ],
        2 * tokens * model * model,
    )
    fed, grad_norm_two, grad_bank = mlp(
        place, normed_two.reshape(tokens, model), grad_fed.reshape(tokens, model), bank
    )
    sum_bank = lax.psum_scatter(
        grad_bank.reshape((CORES * seq_size,) + grad_bank.shape[2:]),
        ("core",) + AXES["seq"],
        scatter_dimension=0,
        tiled=True,
    )[0]
    results = row_call(
        functools.partial(middle_back_kernel, out_parts, seq_size),
        "middle_back",
        [place],
        row_count,
        [middle, fed.reshape(frame_shape), grad_norm_two.reshape(frame_shape), cotangent, branch, seg_here, modulation],
        [],
        out_parts,
        (model, model),
        [
            shape_of(frame_shape, BF16),
            shape_of(frame_shape, F32),
            shape_of(frame_shape, BF16),
            shape_of((row_count, 4, 8, model), F32),
        ]
        + [shape_of((row_count, frame_count, width), BF16)] * seq_size,
        2 * tokens * model * model,
    )
    output, grad_middle, grad_branch, sums_two = results[:4]
    grad_heads = [results[4]] + [swap(results[4 + mask], "seq", mask) for mask in partners]
    keep_out, give_out = weight_grad(
        place, [grad_branch.reshape(tokens, model)], attn.reshape(tokens, model), rows, seq_size, True
    )
    sum_out = add_cores(keep_out, give_out)

    grad_qkv = attend_back(
        qkv, segments, lse, cos_table, sin_table, attended, grad_heads, heads, scale
    )
    flat_grad = grad_qkv.reshape(seq_size, tokens, 3 * width)
    got = [
        swap(partial, "seq", mask) for mask, partial in zip(partners, spread_back(grad_qkv, qkv_full))
    ]
    keep_qkv, give_qkv = weight_grad(
        place, [piece.reshape(tokens, model) for piece in pieces], flat_grad, rows, 1, True, got[0]
    )
    sum_out = halve_chips(send_seq(sum_out)).T
    sum_qkv = halve_chips(add_cores(keep_qkv, give_qkv)[0])
    sum_qkv = jnp.stack(
        [
            sum_qkv[:, :width].reshape(rows, 2, heads, half).swapaxes(1, 2).reshape(rows, heads, head_dim),
            sum_qkv[:, width : 2 * width].reshape(rows, 2, heads, half).swapaxes(1, 2).reshape(rows, heads, head_dim),
            sum_qkv[:, 2 * width :].reshape(rows, heads, head_dim),
        ],
        2,
    ).reshape(rows, 3 * width)

    grad_columns, grad_frames, grad_skip, sums_one = row_call(
        functools.partial(leave_kernel, skip_parts, seq_size),
        "leave",
        [place],
        row_count,
        [hidden, grad_middle, flat_grad[0].reshape(row_count, frame_count, 3 * width)]
        + got
        + [seg_here, modulation],
        [qkv_full],
        skip_parts,
        (2 * model, model),
        [
            shape_of(frame_shape, BF16),
            shape_of(frame_shape, BF16),
            shape_of(frame_shape, BF16),
            shape_of((row_count, 2, 8, model), F32),
        ],
        6 * tokens * model * model,
        [keep_qkv],
    )
    sum_bank = lax.psum_scatter(after(sum_bank, grad_columns), "chip", scatter_dimension=0, tiled=True)[0]
    sum_up, sum_down = unpack_sums(sum_bank, units, min(512, units))
    keep_skip, give_skip = weight_grad(
        place,
        [frames.reshape(tokens, model), skip_in.reshape(tokens, model)],
        grad_columns.reshape(tokens, model),
        w_skip.shape[0],
        seq_size,
        True,
    )
    sum_skip = send_chips(send_seq(add_cores(keep_skip, give_skip)))

    grad_modulation = jnp.concatenate([sums_one, sums_two], 1)[:, :, :segs]
    grad_modulation = grad_modulation.swapaxes(1, 2).reshape(utterances, 6 * model)
    own = grad_modulation
    for mask in reversed(bits("seq")):
        count = own.shape[1] // 2
        mine = (seq // mask) % 2
        keep_mod = lax.dynamic_slice_in_dim(own, mine * count, count, 1)
        own = keep_mod + swap(lax.dynamic_slice_in_dim(own, (1 - mine) * count, count, 1), "seq", mask)
    own = gather_steps(own, [("dp", [mask]) for mask in bits("dp") + [1]]).reshape(dp_size * utterances, mod_columns)
    sum_mod = jnp.dot(activity.astype(F32).T, own, precision=lax.Precision.HIGHEST)
    return (
        output,
        grad_frames,
        grad_skip,
        sum_skip,
        sum_qkv,
        sum_out,
        sum_up,
        sum_down,
        sum_mod,
    )


def solution(mesh):
    chips, seqs = mesh.shape["dp"] // CORES, mesh.shape["seq"]
    fast = 1
    while fast * fast < seqs:
        fast *= 2
    cut = Mesh(mesh.devices.reshape(chips, CORES, seqs // fast, fast), ("chip", "core", "slow", "fast"))
    dp, seq = AXES["dp"], AXES["seq"]
    tokens, rows, both, turned = P(dp, seq, None), P(dp, None), P(dp, seq), P(seq, dp)
    in_specs = (tokens, tokens, tokens, both, rows, rows, both, both, turned, both, turned, both, tokens)
    out_specs = (tokens, tokens, tokens, both, both, turned, both, turned, both)
    return jax.shard_map(body, mesh=cut, in_specs=in_specs, out_specs=out_specs, check_vma=False)
```

time: 822 us -> 538 us (0.65)
  local copies, waits for them, and re-layouts: 106 us -> 12.9 us
  other arithmetic: 106 us -> 17.4 us
  waiting for transfers between devices: 309 us -> 235 us
  Pallas kernels: 131 us -> 185 us
  matrix products: 51.8 us -> 1.62 us
  starting transfers between devices: 105 us -> 62.7 us
  between operations: 3.46 us -> 15.7 us
    ppermute x89 -> x56, waiting for transfers between devices: 309 us -> 230 us  [swap(): lax.ppermute(values, AXES[axis], [(i, i ^ mask) for i in range(axis_size(...]
    pallas_call x6 -> x14, Pallas kernels: 60.5 us -> 114 us  [the longest x4 42.1 us: row_call(): pl.pallas_call(kernel, grid=(rows,), out_shape=tuple(outs), in_specs=[SME...]
    ppermute x89 -> x56, starting transfers between devices: 105 us -> 62.4 us  [swap(): lax.ppermute(values, AXES[axis], [(i, i ^ mask) for i in range(axis_size(...]
    dot_general x15 -> x0, matrix products: 41.7 us -> none  [the longest x6 19.5 us: against(): return lax.dot_general(left, right, NT, preferred_element_type=F32)]
    dynamic_slice x20 -> x2, local copies, waits for them, and re-layouts: 33 us -> 0.03 us  [body(): lax.dynamic_slice_in_dim(own, (1 - mine) * count, count, 1)]
    another operation x18 -> x6, other arithmetic: 28.1 us -> 0.85 us  [gather_steps(): held = jnp.stack([held] + [swap(held, axis, mask) for mask in masks])]
    unnamed x225 -> x60, local copies, waits for them, and re-layouts: 31.4 us -> 6.71 us
    another operation x14 -> x4, other arithmetic: 23 us -> 2.89 us  [the longest x4 8.48 us: reduce_weight(): jnp.stack([pick(block, 1 - core, 1).astype(BF16) for block in shaped])]
  transfers between devices with their start and end apart: 89 -> 59, of which waited for: 24 -> 30; matrix products, arithmetic and copies ran while one was open for 29% -> 5% of each run, Pallas kernels for 11% -> 26%
where the time goes in v2:
time: 538 us; the launch traced here: 530 us
  waiting for transfers between devices  235 us (44%)
  Pallas kernels  185 us (34%)
  starting transfers between devices  62.7 us (12%)
  other arithmetic  17.4 us (3%)
  between operations  15.7 us (3%)
  local copies, waits for them, and re-layouts  12.9 us (2%)
    ppermute x56, waiting for transfers between devices, swap(): lax.ppermute(values, AXES[axis], [(i, i ^ mask) for i in range(axis_size(...  230 us
    ppermute x56, starting transfers between devices, swap(): lax.ppermute(values, AXES[axis], [(i, i ^ mask) for i in range(axis_size(...  62.4 us
    pallas_call x4, Pallas kernels, row_call(): pl.pallas_call(kernel, grid=(rows,), out_shape=tuple(outs), in_specs=[SME...  42.1 us
    pallas_call x1, Pallas kernels, mlp(): pl.pallas_call(functools.partial(mlp_kernel, bank, chunk), grid=(seqs * p...  35 us
    pallas_call x1, Pallas kernels, attend_back(): pl.pallas_call(functools.partial(attend_back_kernel, heads, width, scale)...  31.1 us
    pallas_call x1, Pallas kernels, attend(): pl.pallas_call(functools.partial(attend_kernel, heads, width), grid=(rows...  25.8 us
    pallas_call x3, Pallas kernels, weight_grad(): pl.pallas_call(functools.partial(weight_grad_kernel, len(xs), seqs, by_ma...  21 us
    pallas_call x4, Pallas kernels, project_piece(): pl.pallas_call(functools.partial(qkv_kernel, width, scale), grid=(rows,),...  14.3 us
  transfers between devices with their start and end apart: 59, of which 30 were waited for; matrix products, arithmetic and copies ran while one was open for 5% of the time, Pallas kernels for 26%

profile of v2, /device:TPU:0, one launch (start us, length us, event | category | flops | bytes accessed | tf_op | source)
XLA Modules:
  0.0 529.7 jit_solution(14534583932869525329)
XLA Ops:
  8.7 3.0 collective-permute-start
  13.3 3.0 collective-permute-start.1
  20.8 2.9 collective-permute-start.10
  25.4 2.9 collective-permute-start.4
  28.3 12.1 %collective-permute-done.4 = f32[2,6,1536]{2,1,0:T(8,128)S(1)} collective-permute-done((f32[2,6,1536]{2,1,0:T(8,128)S(1)}, f32[2,6,1536]{2,1,0:T(8,128)S(1)}, u32[]{:S(2)}, u32[]{:S(2)}) %collective-permute-start.4) | collective-permute-done | bytes 73760 | tf_op jit(solution)/shard_map/ppermute | solution.py:41
  41.4 2.5 collective-permute-start.14
  48.2 9.4 %collective-permute-done.6 = f32[7,1536]{1,0:T(8,128)S(1)} collective-permute-done((f32[7,1536]{1,0:T(8,128)S(1)}, f32[7,1536]{1,0:T(8,128)S(1)}, u32[]{:S(2)}, u32[]{:S(2)}) %collective-permute-start.6) | collective-permute-done | bytes 43040 | tf_op jit(solution)/shard_map/ppermute | solution.py:41
  68.1 10.9 %collective-permute-done.12.rest_1_.rest_7_ = bf16[4,256,256]{2,1,0:T(8,128)(2,1)S(1)} collective-permute-done((bf16[4,256,256]{2,1,0:T(8,128)(2,1)S(1)}, bf16[4,256,256]{2,1,0:T(8,128)(2,1)S(1)}, u32[]{:S(2)}, u32[]{:S(2)}) %collective-permute-start.12) | collective-permute-done | bytes 524320 | tf_op jit(solution)/shard_map/ppermute | solution.py:41
  79.0 2.2 collective-permute-done.13.rest_2_.rest_8_
  84.3 3.3 collective-permute-start.21
  88.9 8.2 %enter.1 = (f32[2,256,1024]{2,1,0:T(8,128)}, bf16[2,256,1024]{2,1,0:T(8,128)(2,1)}) custom-call(s32[2]{0:T(128)} %pad_add_fusion.place_ref, f32[2,3]{1,0:T(2,128)} %subtract_multiply_fusion.coef_ref, bf16[2,256,1024]{2,1,0:T(8,128)(2,1)} %frames_ref.1, bf16[2,256,1024]{2,1,0:T(8,128)(2,1)} %skip_ref.1, bf16[2,256,1024]{2,1,0:T(8,128)(2,1)} %cond_ref.1, ...), custom_call_target="tpu_custom_call" | custom-call | flops 2147483648 | bytes 14979072 | tf_op jit(solution)/shard_map/enter/pallas_call | solution.py:762
  100.7 4.6 collective-permute-done.22
  105.6 3.0 multiply_sine_fusion
  108.6 3.4 assemble.1.w_ref.weight_ref.rest_5_
  112.0 3.6 project.4.rest_0_
  115.5 24.1 %collective-permute-done.25.x_ref = bf16[2,256,1024]{2,1,0:T(8,128)(2,1)S(1)} collective-permute-done((bf16[2,256,1024]{2,1,0:T(8,128)(2,1)}, bf16[2,256,1024]{2,1,0:T(8,128)(2,1)S(1)}, u32[]{:S(2)}, u32[]{:S(2)}) %collective-permute-start.25) | collective-permute-done | bytes 1048608 | tf_op jit(solution)/shard_map/ppermute | solution.py:41
  140.6 3.6 project.5.rest_0_
  145.1 3.6 project.6.rest_0_
  148.7 23.6 %collective-permute-done.19.x_ref = bf16[2,256,1024]{2,1,0:T(8,128)(2,1)} collective-permute-done((bf16[2,256,1024]{2,1,0:T(8,128)(2,1)}, bf16[2,256,1024]{2,1,0:T(8,128)(2,1)}, u32[]{:S(2)}, u32[]{:S(2)}) %collective-permute-start.19) | collective-permute-done | bytes 1048608 | tf_op jit(solution)/shard_map/ppermute | solution.py:41
  172.3 3.6 project.7.qkv_ref
  175.9 25.8 %attend.1 = (bf16[2,256,256]{2,1,0:T(8,128)(2,1)}, bf16[2,256,256]{2,1,0:T(8,128)(2,1)}, bf16[2,256,256]{2,1,0:T(8,128)(2,1)}, bf16[2,256,256]{2,1,0:T(8,128)(2,1)}, f32[2,4,4,256]{3,2,1,0:T(4,128)}) custom-call(bf16[4,2,256,768]{3,2,1,0:T(8,128)(2,1)} %project.7.qkv_ref, f32[2,4,256]{2,1,0:T(4,128)} %bitcast.192), custom_call_target="tpu_custom_call" | custom-call | flops 8589934592 | bytes 4194304 | tf_op jit(solution)/shard_map/attend/pallas_call | solution.py:495
  203.0 2.2 collective-permute-start.28
  205.3 6.0 %collective-permute-done.26.rest_1_ = bf16[2,256,256]{2,1,0:T(8,128)(2,1)S(1)} collective-permute-done((bf16[2,256,256]{2,1,0:T(8,128)(2,1)}, bf16[2,256,256]{2,1,0:T(8,128)(2,1)S(1)}, u32[]{:S(2)}, u32[]{:S(2)}) %collective-permute-start.26) | collective-permute-done | bytes 262176 | tf_op jit(solution)/shard_map/ppermute | solution.py:41
  211.3 3.7 collective-permute-done.27.rest_2_
  214.9 4.2 all-gather.3.cloned.1.call-done
  219.2 8.2 %branch.1 = (bf16[2,256,1024]{2,1,0:T(8,128)(2,1)}, f32[2,256,1024]{2,1,0:T(8,128)}, f32[2,256,1024]{2,1,0:T(8,128)}, bf16[2,256,1024]{2,1,0:T(8,128)(2,1)}, bf16[2,256,1024]{2,1,0:T(8,128)(2,1)}) custom-call(s32[2]{0:T(128)} %pad_add_fusion.place_ref, bf16[2,256,256]{2,1,0:T(8,128)(2,1)} %get-tuple-element.48.rest_0_, bf16[2,256,256]{2,1,0:T(8,128)(2,1)} %copy-done.15, ...), custom_call_target="tpu_custom_call" | custom-call | flops 1073741824 | bytes 12881920 | tf_op jit(solution)/shard_map/branch/pallas_call | solution.py:762
  227.4 35.0 %mlp.1 = (f32[512,1024]{1,0:T(8,128)}, f32[512,1024]{1,0:T(8,128)}, bf16[2,4,4,128,2048]{4,3,2,1,0:T(8,128)(2,1)}) custom-call(s32[2]{0:T(128)} %pad_add_fusion.place_ref, bf16[512,1024]{1,0:T(8,128)(2,1)} %bitcast.202, bf16[512,1024]{1,0:T(8,128)(2,1)} %bitcast.203, bf16[32,128,2304]{2,1,0:T(8,128)(2,1)} %bitcast.148), custom_call_target="tpu_custom_call" | custom-call | flops 25769803776 | bytes 39845888 | tf_op jit(solution)/shard_map/mlp/pallas_call | solution.py:686
  262.4 12.6 %middle_back.1 = (bf16[2,256,1024]{2,1,0:T(8,128)(2,1)}, f32[2,256,1024]{2,1,0:T(8,128)}, bf16[2,256,1024]{2,1,0:T(8,128)(2,1)}, f32[2,4,8,1024]{3,2,1,0:T(8,128...) custom-call(s32[2]{0:T(128)} %pad_add_fusion.place_ref, ...), custom_call_target="tpu_custom_call" | custom-call | flops 1073741824 | bytes 23367680 | tf_op jit(solution)/shard_map/middle_back/pallas_call | solution.py:762
  275.7 2.8 collective-permute-start.31
  278.5 5.2 weight_grad.5
  284.5 5.0 collective-permute-done.31.rest_7_
  290.2 31.1 %attend_back.1.grad_ref = bf16[4,2,256,768]{3,2,1,0:T(8,128)(2,1)} custom-call(bf16[4,2,256,768]{3,2,1,0:T(8,128)(2,1)} %project.7.qkv_ref, f32[2,4,256]{2,1,0:T(4,128)} %bitcast.193, f32[2,4,4,256]{3,2,1,0:T(4,128)} %get-tuple-element.61.lse_ref, f32[4,256,128]{2,1,0:T(8,128)} %get-tuple-element.133.cos_ref, f32[4,256,128]{2,1,0:T(8,128)} %get-tuple-element.132.sin_ref, ...), custom_call_target="tpu_custom_call" | custom-call | flops 21474836480 | bytes 8388608 | tf_op jit(solution)/shard_map/attend_back/pallas_call | solution.py:592
  321.3 8.0 %spread_back.1 = (bf16[2,256,1024]{2,1,0:T(8,128)(2,1)}, bf16[2,256,1024]{2,1,0:T(8,128)(2,1)}, bf16[2,256,1024]{2,1,0:T(8,128)(2,1)}) custom-call(bf16[4,2,256,768]{3,2,1,0:T(8,128)(2,1)} %attend_back.1.grad_ref, bf16[1024,768]{1,0:T(8,128)(2,1)} %assemble.1.w_ref.weight_ref.rest_5_), custom_call_target="tpu_custom_call" | custom-call | flops 2415919104 | bytes 7340032 | tf_op jit(solution)/shard_map/spread_back/pallas_call | solution.py:426
  337.7 29.2 %collective-permute-done.32.rest_5_.rest_0_ = bf16[2,256,1024]{2,1,0:T(8,128)(2,1)} collective-permute-done((bf16[2,256,1024]{2,1,0:T(8,128)(2,1)}, bf16[2,256,1024]{2,1,0:T(8,128)(2,1)}, u32[]{:S(2)}, u32[]{:S(2)}) %collective-permute-start.32) | collective-permute-done | bytes 1048608 | tf_op jit(solution)/shard_map/ppermute | solution.py:41
  366.8 9.2 %weight_grad.3 = (bf16[1,4,128,768]{3,2,1,0:T(8,128)(2,1)}, bf16[1,4,128,768]{3,2,1,0:T(8,128)(2,1)}) custom-call(s32[2]{0:T(128)} %pad_add_fusion.place_ref, bf16[512,1024]{1,0:T(8,128)(2,1)} %bitcast.163, bf16[512,1024]{1,0:T(8,128)(2,1)} %bitcast.160, bf16[512,1024]{1,0:T(8,128)(2,1)} %bitcast.161, bf16[512,1024]{1,0:T(8,128)(2,1)} %bitcast.37.rest_3_, ...), custom_call_target="tpu_custom_call" | custom-call | flops 3221225472 | bytes 8912896 | tf_op jit(solution)/shard_map/weight_grad/pallas_call | solution.py:298
  376.0 35.5 %collective-permute-done.34.rest_2_ = bf16[2,256,1024]{2,1,0:T(8,128)(2,1)} collective-permute-done((bf16[2,256,1024]{2,1,0:T(8,128)(2,1)}, bf16[2,256,1024]{2,1,0:T(8,128)(2,1)}, u32[]{:S(2)}, u32[]{:S(2)}) %collective-permute-start.34) | collective-permute-done | bytes 1048608 | tf_op jit(solution)/shard_map/ppermute | solution.py:41
  411.5 13.1 %leave.1 = (bf16[2,256,1024]{2,1,0:T(8,128)(2,1)}, bf16[2,256,1024]{2,1,0:T(8,128)(2,1)}, bf16[2,256,1024]{2,1,0:T(8,128)(2,1)}, f32[2,2,8,1024]{3,2,1,0:T(8,128)}) custom-call(s32[2]{0:T(128)} %pad_add_fusion.place_ref, f32[2,256,1024]{2,1,0:T(8,128)} %get-tuple-element.52.rest_4_.hidden_ref, f32[2,256,1024]{2,1,0:T(8,128)} %get-tuple-element.60.grad_middle_ref, ...), custom_call_target="tpu_custom_call" | custom-call | flops 3221225472 | bytes 24940544 | tf_op jit(solution)/shard_map/leave/pallas_call | solution.py:762
  432.3 6.6 %weight_grad.4 = (bf16[4,4,256,256]{3,2,1,0:T(8,128)(2,1)}, bf16[4,4,256,256]{3,2,1,0:T(8,128)(2,1)}) custom-call(s32[2]{0:T(128)} %pad_add_fusion.place_ref, bf16[512,1024]{1,0:T(8,128)(2,1)} %bitcast.198, bf16[512,1024]{1,0:T(8,128)(2,1)} %bitcast.199, bf16[512,1024]{1,0:T(8,128)(2,1)} %bitcast.162), custom_call_target="tpu_custom_call" | custom-call | flops 2147483648 | bytes 7340032 | tf_op jit(solution)/shard_map/weight_grad/pallas_call | solution.py:298
  442.3 2.5 collective-permute-start.49
  445.1 2.2 collective-permute-start.54
  447.3 5.9 %collective-permute-done.49 = bf16[2,128,256]{2,1,0:T(8,128)(2,1)S(1)} collective-permute-done((bf16[2,128,256]{2,1,0:T(8,128)(2,1)S(1)}, bf16[2,128,256]{2,1,0:T(8,128)(2,1)S(1)}, u32[]{:S(2)}, u32[]{:S(2)}) %collective-permute-start.49) | collective-permute-done | bytes 131104 | tf_op jit(solution)/shard_map/ppermute | solution.py:41
  454.5 5.5 %collective-permute-done.50 = bf16[1,128,256]{2,1,0:T(8,128)(2,1)S(1)} collective-permute-done((bf16[1,128,256]{2,1,0:T(8,128)(2,1)S(1)}, bf16[1,128,256]{2,1,0:T(8,128)(2,1)S(1)}, u32[]{:S(2)}, u32[]{:S(2)}) %collective-permute-start.50) | collective-permute-done | bytes 65568 | tf_op jit(solution)/shard_map/ppermute | solution.py:41
  462.7 2.3 convert_add_fusion
  468.6 33.8 %collective-permute-done.43 = bf16[2,128,768]{2,1,0:T(8,128)(2,1)S(1)} collective-permute-done((bf16[2,128,768]{2,1,0:T(8,128)(2,1)S(1)}, bf16[2,128,768]{2,1,0:T(8,128)(2,1)S(1)}, u32[]{:S(2)}, u32[]{:S(2)}) %collective-permute-start.43) | collective-permute-done | bytes 393248 | tf_op jit(solution)/shard_map/ppermute | solution.py:41
  504.0 4.2 collective-permute-done.44
  508.8 2.2 collective-permute-start.40
  511.0 2.1 collective-permute-start.41
  515.9 4.0 collective-permute-done.40
  (238 shorter events, 72.5 us)
Async XLA Ops:
  7.2 212.0 %all-gather.3.cloned.1.call-start = ((), (), s32[]{:S(2)}) async-start(), calls=%async_computation.4 | async-start | bytes 19464192 | tf_op jit(solution)/shard_map/all_gather | solution.py:945
  20.8 20.5 %collective-permute-start.10 = (bf16[1,256,256]{2,1,0:T(8,128)(2,1)S(1)}, bf16[1,256,256]{2,1,0:T(8,128)(2,1)S(1)}, u32[]{:S(2)}, u32[]{:S(2)}) collective-permute-start(bf16[1,256,256]{2,1,0:T(8,128)(2,1)S(1)} %bitcast.180), channel_id=1, source_target_pairs={{0,16},{4,20},{8,24},{12,28},{16,0},{20,4},{24,8},{28,12},{1,17},{... | collective-permute-start | bytes 393224 | tf_op jit(solution)/shard_map/ppermute | solution.py:41
  23.7 17.5 %collective-permute-start.11 = (bf16[1,256,256]{2,1,0:T(8,128)(2,1)S(1)}, bf16[1,256,256]{2,1,0:T(8,128)(2,1)S(1)}, u32[]{:S(2)}, u32[]{:S(2)}) collective-permute-start(bf16[1,256,256]{2,1,0:T(8,128)(2,1)S(1)} %bitcast.181), channel_id=1, source_target_pairs={{0,24},{4,28},{8,16},{12,20},{16,8},{20,12},{24,0},{28,4},{1,25},{... | collective-permute-start | bytes 393224 | tf_op jit(solution)/shard_map/ppermute | solution.py:41
  25.1 16.2 %collective-permute-start.9 = (bf16[1,256,256]{2,1,0:T(8,128)(2,1)S(1)}, bf16[1,256,256]{2,1,0:T(8,128)(2,1)S(1)}, u32[]{:S(2)}, u32[]{:S(2)}) collective-permute-start(bf16[1,256,256]{2,1,0:T(8,128)(2,1)S(1)} %bitcast.182), channel_id=1, source_target_pairs={{0,8},{4,12},{8,0},{12,4},{16,24},{20,28},{24,16},{28,20},{1,9},{5... | collective-permute-start | bytes 393224 | tf_op jit(solution)/shard_map/ppermute | solution.py:41
  25.4 15.0 %collective-permute-start.4 = (f32[2,6,1536]{2,1,0:T(8,128)S(1)}, f32[2,6,1536]{2,1,0:T(8,128)S(1)}, u32[]{:S(2)}, u32[]{:S(2)}) collective-permute-start(f32[2,6,1536]{2,1,0:T(8,128)S(1)} %slice.188), channel_id=1, source_target_pairs={{0,16},{4,20},{8,24},{12,28},{16,0},{20,4},{24,8},{28,12},{1,17},{... | collective-permute-start | bytes 221192 | tf_op jit(solution)/shard_map/ppermute | solution.py:41
  41.4 17.4 %collective-permute-start.14 = (bf16[4,256,256]{2,1,0:T(8,128)(2,1)S(1)}, bf16[4,256,256]{2,1,0:T(8,128)(2,1)S(1)}, u32[]{:S(2)}, u32[]{:S(2)}) collective-permute-start(bf16[4,256,256]{2,1,0:T(8,128)(2,1)S(1)} %pad_maximum_fusion.1.rest_0_.rest_6_), channel_id=1, source_target_pairs={{0,3},{1,2},{2,1},{3,0},{4,7},{5,6},{6,5},{7,4},{8,11},{9,10},{10,... | collective-permute-start | bytes 1572872 | tf_op jit(solution)/shard_map/ppermute | solution.py:41
  44.6 13.0 %collective-permute-start.6 = (f32[7,1536]{1,0:T(8,128)S(1)}, f32[7,1536]{1,0:T(8,128)S(1)}, u32[]{:S(2)}, u32[]{:S(2)}) collective-permute-start(f32[7,1536]{1,0:T(8,128)S(1)} %pad_maximum_fusion.9), channel_id=1, source_target_pairs={{0,1},{1,0},{2,3},{3,2},{4,5},{5,4},{6,7},{7,6},{8,9},{9,8},{10,11... | collective-permute-start | bytes 129032 | tf_op jit(solution)/shard_map/ppermute | solution.py:41
  46.2 11.4 %collective-permute-start.7 = (f32[7,1536]{1,0:T(8,128)S(1)}, f32[7,1536]{1,0:T(8,128)S(1)}, u32[]{:S(2)}, u32[]{:S(2)}) collective-permute-start(f32[7,1536]{1,0:T(8,128)S(1)} %pad_maximum_fusion.9), channel_id=1, source_target_pairs={{0,2},{1,3},{2,0},{3,1},{4,6},{5,7},{6,4},{7,5},{8,10},{9,11},{10,... | collective-permute-start | bytes 129032 | tf_op jit(solution)/shard_map/ppermute | solution.py:41
  47.8 10.3 %collective-permute-start.8 = (f32[7,1536]{1,0:T(8,128)S(1)}, f32[7,1536]{1,0:T(8,128)S(1)}, u32[]{:S(2)}, u32[]{:S(2)}) collective-permute-start(f32[7,1536]{1,0:T(8,128)S(1)} %pad_maximum_fusion.9), channel_id=1, source_target_pairs={{0,3},{1,2},{2,1},{3,0},{4,7},{5,6},{6,5},{7,4},{8,11},{9,10},{10,... | collective-permute-start | bytes 129032 | tf_op jit(solution)/shard_map/ppermute | solution.py:41
  61.6 385.7 %reduce-scatter.3.cloned.1.call-start = ((), (), s32[]{:S(2)}) async-start(), calls=%async_computation.2 | async-start | bytes 18874368 | tf_op jit(solution)/shard_map/reduce_scatter | solution.py:1002
  62.4 16.6 %collective-permute-start.12 = (bf16[4,256,256]{2,1,0:T(8,128)(2,1)S(1)}, bf16[4,256,256]{2,1,0:T(8,128)(2,1)S(1)}, u32[]{:S(2)}, u32[]{:S(2)}) collective-permute-start(bf16[4,256,256]{2,1,0:T(8,128)(2,1)S(1)} %pad_maximum_fusion.1.rest_0_.rest_6_), channel_id=1, source_target_pairs={{0,1},{1,0},{2,3},{3,2},{4,5},{5,4},{6,7},{7,6},{8,9},{9,8},{10,11... | collective-permute-start | bytes 1572872 | tf_op jit(solution)/shard_map/ppermute | solution.py:41
  64.0 17.2 %collective-permute-start.13 = (bf16[4,256,256]{2,1,0:T(8,128)(2,1)S(1)}, bf16[4,256,256]{2,1,0:T(8,128)(2,1)S(1)}, u32[]{:S(2)}, u32[]{:S(2)}) collective-permute-start(bf16[4,256,256]{2,1,0:T(8,128)(2,1)S(1)} %pad_maximum_fusion.1.rest_0_.rest_6_), channel_id=1, source_target_pairs={{0,2},{1,3},{2,0},{3,1},{4,6},{5,7},{6,4},{7,5},{8,10},{9,11},{10,... | collective-permute-start | bytes 1572872 | tf_op jit(solution)/shard_map/ppermute | solution.py:41
  67.6 16.8 %collective-permute-start.15 = (bf16[4,256,256]{2,1,0:T(8,128)(2,1)S(1)}, bf16[4,256,256]{2,1,0:T(8,128)(2,1)}, u32[]{:S(2)}, u32[]{:S(2)}) collective-permute-start(bf16[4,256,256]{2,1,0:T(8,128)(2,1)S(1)} %pad_maximum_fusion.1.rest_0_.rest_6_), channel_id=1, source_target_pairs={{0,4},{4,0},{8,12},{12,8},{16,20},{20,16},{24,28},{28,24},{1,5},{5... | collective-permute-start | bytes 1572872 | tf_op jit(solution)/shard_map/ppermute | solution.py:41
  67.6 20.0 %collective-permute-start.18 = (bf16[4,256,256]{2,1,0:T(8,128)(2,1)S(1)}, bf16[4,256,256]{2,1,0:T(8,128)(2,1)}, u32[]{:S(2)}, u32[]{:S(2)}) collective-permute-start(bf16[4,256,256]{2,1,0:T(8,128)(2,1)S(1)} %copy-done.3), channel_id=1, source_target_pairs={{0,4},{4,0},{8,12},{12,8},{16,20},{20,16},{24,28},{28,24},{1,5},{5... | collective-permute-start | bytes 1572872 | tf_op jit(solution)/shard_map/ppermute | solution.py:41
  79.0 9.9 %collective-permute-start.16 = (bf16[4,256,256]{2,1,0:T(8,128)(2,1)S(1)}, bf16[4,256,256]{2,1,0:T(8,128)(2,1)}, u32[]{:S(2)}, u32[]{:S(2)}) collective-permute-start(bf16[4,256,256]{2,1,0:T(8,128)(2,1)S(1)} %collective-permute-done.12.rest_1_.rest_7_), channel_id=1, source_target_pairs={{0,4},{4,0},{8,12},{12,8},{16,20},{20,16},{24,28},{28,24},{1,5},{5... | collective-permute-start | bytes 1572872 | tf_op jit(solution)/shard_map/ppermute | solution.py:41
  81.2 7.7 %collective-permute-start.17 = (bf16[4,256,256]{2,1,0:T(8,128)(2,1)S(1)}, bf16[4,256,256]{2,1,0:T(8,128)(2,1)}, u32[]{:S(2)}, u32[]{:S(2)}) collective-permute-start(bf16[4,256,256]{2,1,0:T(8,128)(2,1)S(1)} %collective-permute-done.13.rest_2_.rest_8_), channel_id=1, source_target_pairs={{0,4},{4,0},{8,12},{12,8},{16,20},{20,16},{24,28},{28,24},{1,5},{5... | collective-permute-start | bytes 1572872 | tf_op jit(solution)/shard_map/ppermute | solution.py:41
  83.9 15.5 %collective-permute-start.20 = (bf16[1,128,768]{2,1,0:T(8,128)(2,1)}, bf16[1,128,768]{2,1,0:T(8,128)(2,1)S(1)}, u32[]{:S(2)}, u32[]{:S(2)}) collective-permute-start(bf16[1,128,768]{2,1,0:T(8,128)(2,1)} %bitcast.155), channel_id=1, source_target_pairs={{0,8},{4,12},{8,0},{12,4},{16,24},{20,28},{24,16},{28,20},{1,9},{5... | collective-permute-start | bytes 589832 | tf_op jit(solution)/shard_map/ppermute | solution.py:41
  84.3 16.4 %collective-permute-start.21 = (bf16[1,128,768]{2,1,0:T(8,128)(2,1)}, bf16[1,128,768]{2,1,0:T(8,128)(2,1)S(1)}, u32[]{:S(2)}, u32[]{:S(2)}) collective-permute-start(bf16[1,128,768]{2,1,0:T(8,128)(2,1)} %bitcast.156), channel_id=1, source_target_pairs={{0,16},{4,20},{8,24},{12,28},{16,0},{20,4},{24,8},{28,12},{1,17},{... | collective-permute-start | bytes 589832 | tf_op jit(solution)/shard_map/ppermute | solution.py:41
  87.6 17.7 %collective-permute-start.22 = (bf16[1,128,768]{2,1,0:T(8,128)(2,1)}, bf16[1,128,768]{2,1,0:T(8,128)(2,1)S(1)}, u32[]{:S(2)}, u32[]{:S(2)}) collective-permute-start(bf16[1,128,768]{2,1,0:T(8,128)(2,1)} %bitcast.157), channel_id=1, source_target_pairs={{0,24},{4,28},{8,16},{12,20},{16,8},{20,12},{24,0},{28,4},{1,25},{... | collective-permute-start | bytes 589832 | tf_op jit(solution)/shard_map/ppermute | solution.py:41
  97.1 42.5 %collective-permute-start.25 = (bf16[2,256,1024]{2,1,0:T(8,128)(2,1)}, bf16[2,256,1024]{2,1,0:T(8,128)(2,1)S(1)}, u32[]{:S(2)}, u32[]{:S(2)}) collective-permute-start(bf16[2,256,1024]{2,1,0:T(8,128)(2,1)} %get-tuple-element.47.x_ref), channel_id=1, source_target_pairs={{0,1},{1,0},{2,3},{3,2},{4,5},{5,4},{6,7},{7,6},{8,9},{9,8},{10,11... | collective-permute-start | bytes 3145736 | tf_op jit(solution)/shard_map/ppermute | solution.py:41
  97.9 46.3 %collective-permute-start.24 = (bf16[2,256,1024]{2,1,0:T(8,128)(2,1)}, bf16[2,256,1024]{2,1,0:T(8,128)(2,1)S(1)}, u32[]{:S(2)}, u32[]{:S(2)}) collective-permute-start(bf16[2,256,1024]{2,1,0:T(8,128)(2,1)} %get-tuple-element.47.x_ref), channel_id=1, source_target_pairs={{0,2},{1,3},{2,0},{3,1},{4,6},{5,7},{6,4},{7,5},{8,10},{9,11},{10,... | collective-permute-start | bytes 3145736 | tf_op jit(solution)/shard_map/ppermute | solution.py:41
  99.4 72.9 %collective-permute-start.19 = (bf16[2,256,1024]{2,1,0:T(8,128)(2,1)}, bf16[2,256,1024]{2,1,0:T(8,128)(2,1)}, u32[]{:S(2)}, u32[]{:S(2)}) collective-permute-start(bf16[2,256,1024]{2,1,0:T(8,128)(2,1)} %get-tuple-element.47.x_ref), channel_id=1, source_target_pairs={{0,3},{1,2},{2,1},{3,0},{4,7},{5,6},{6,5},{7,4},{8,11},{9,10},{10,... | collective-permute-start | bytes 3145736 | tf_op jit(solution)/shard_map/ppermute | solution.py:41
  201.8 9.5 %collective-permute-start.26 = (bf16[2,256,256]{2,1,0:T(8,128)(2,1)}, bf16[2,256,256]{2,1,0:T(8,128)(2,1)S(1)}, u32[]{:S(2)}, u32[]{:S(2)}) collective-permute-start(bf16[2,256,256]{2,1,0:T(8,128)(2,1)} %get-tuple-element.49.rest_1_), channel_id=1, source_target_pairs={{0,1},{1,0},{2,3},{3,2},{4,5},{5,4},{6,7},{7,6},{8,9},{9,8},{10,11... | collective-permute-start | bytes 786440 | tf_op jit(solution)/shard_map/ppermute | solution.py:41
  202.4 12.5 %collective-permute-start.27 = (bf16[2,256,256]{2,1,0:T(8,128)(2,1)}, bf16[2,256,256]{2,1,0:T(8,128)(2,1)S(1)}, u32[]{:S(2)}, u32[]{:S(2)}) collective-permute-start(bf16[2,256,256]{2,1,0:T(8,128)(2,1)} %get-tuple-element.50.rest_2_), channel_id=1, source_target_pairs={{0,2},{1,3},{2,0},{3,1},{4,6},{5,7},{6,4},{7,5},{8,10},{9,11},{10,... | collective-permute-start | bytes 786440 | tf_op jit(solution)/shard_map/ppermute | solution.py:41
  203.0 11.9 %collective-permute-start.28 = (bf16[2,256,256]{2,1,0:T(8,128)(2,1)}, bf16[2,256,256]{2,1,0:T(8,128)(2,1)S(1)}, u32[]{:S(2)}, u32[]{:S(2)}) collective-permute-start(bf16[2,256,256]{2,1,0:T(8,128)(2,1)} %get-tuple-element.51.rest_3_), channel_id=1, source_target_pairs={{0,3},{1,2},{2,1},{3,0},{4,7},{5,6},{6,5},{7,4},{8,11},{9,10},{10,... | collective-permute-start | bytes 786440 | tf_op jit(solution)/shard_map/ppermute | solution.py:41
  262.4 258.2 %reduce-scatter.5.cloned.1.call-start = ((), (), s32[]{:S(2)}) async-start(), calls=%async_computation.3 | async-start | bytes 2621440 | tf_op jit(solution)/shard_map/reduce_scatter | solution.py:1074
  275.0 9.4 %collective-permute-start.29 = (bf16[2,256,256]{2,1,0:T(8,128)(2,1)}, bf16[2,256,256]{2,1,0:T(8,128)(2,1)S(1)}, u32[]{:S(2)}, u32[]{:S(2)}) collective-permute-start(bf16[2,256,256]{2,1,0:T(8,128)(2,1)} %get-tuple-element.63), channel_id=1, source_target_pairs={{0,1},{1,0},{2,3},{3,2},{4,5},{5,4},{6,7},{7,6},{8,9},{9,8},{10,11... | collective-permute-start | bytes 786440 | tf_op jit(solution)/shard_map/ppermute | solution.py:41
  275.4 9.0 %collective-permute-start.30 = (bf16[2,256,256]{2,1,0:T(8,128)(2,1)}, bf16[2,256,256]{2,1,0:T(8,128)(2,1)S(1)}, u32[]{:S(2)}, u32[]{:S(2)}) collective-permute-start(bf16[2,256,256]{2,1,0:T(8,128)(2,1)} %get-tuple-element.64), channel_id=1, source_target_pairs={{0,2},{1,3},{2,0},{3,1},{4,6},{5,7},{6,4},{7,5},{8,10},{9,11},{10,... | collective-permute-start | bytes 786440 | tf_op jit(solution)/shard_map/ppermute | solution.py:41
  275.7 13.8 %collective-permute-start.31 = (bf16[2,256,256]{2,1,0:T(8,128)(2,1)}, bf16[2,256,256]{2,1,0:T(8,128)(2,1)S(1)}, u32[]{:S(2)}, u32[]{:S(2)}) collective-permute-start(bf16[2,256,256]{2,1,0:T(8,128)(2,1)} %get-tuple-element.65), channel_id=1, source_target_pairs={{0,3},{1,2},{2,1},{3,0},{4,7},{5,6},{6,5},{7,4},{8,11},{9,10},{10,... | collective-permute-start | bytes 786440 | tf_op jit(solution)/shard_map/ppermute | solution.py:41
  283.8 51.0 %collective-permute-start.45 = (bf16[4,4,128,256]{3,2,1,0:T(8,128)(2,1)}, bf16[4,4,128,256]{3,2,1,0:T(8,128)(2,1)S(1)}, u32[]{:S(2)}, u32[]{:S(2)}) collective-permute-start(bf16[4,4,128,256]{3,2,1,0:T(8,128)(2,1)} %get-tuple-element.79), channel_id=1, source_target_pairs={{0,4},{4,0},{8,12},{12,8},{16,20},{20,16},{24,28},{28,24},{1,5},{5... | collective-permute-start | bytes 3145736 | tf_op jit(solution)/shard_map/ppermute | solution.py:41
  329.3 37.6 %collective-permute-start.32 = (bf16[2,256,1024]{2,1,0:T(8,128)(2,1)}, bf16[2,256,1024]{2,1,0:T(8,128)(2,1)}, u32[]{:S(2)}, u32[]{:S(2)}) collective-permute-start(bf16[2,256,1024]{2,1,0:T(8,128)(2,1)} %get-tuple-element.66), channel_id=1, source_target_pairs={{0,1},{1,0},{2,3},{3,2},{4,5},{5,4},{6,7},{7,6},{8,9},{9,8},{10,11... | collective-permute-start | bytes 3145736 | tf_op jit(solution)/shard_map/ppermute | solution.py:41
  331.0 45.0 %collective-permute-start.33 = (bf16[2,256,1024]{2,1,0:T(8,128)(2,1)}, bf16[2,256,1024]{2,1,0:T(8,128)(2,1)}, u32[]{:S(2)}, u32[]{:S(2)}) collective-permute-start(bf16[2,256,1024]{2,1,0:T(8,128)(2,1)} %get-tuple-element.67), channel_id=1, source_target_pairs={{0,2},{1,3},{2,0},{3,1},{4,6},{5,7},{6,4},{7,5},{8,10},{9,11},{10,... | collective-permute-start | bytes 3145736 | tf_op jit(solution)/shard_map/ppermute | solution.py:41
  331.6 79.9 %collective-permute-start.34 = (bf16[2,256,1024]{2,1,0:T(8,128)(2,1)}, bf16[2,256,1024]{2,1,0:T(8,128)(2,1)}, u32[]{:S(2)}, u32[]{:S(2)}) collective-permute-start(bf16[2,256,1024]{2,1,0:T(8,128)(2,1)} %get-tuple-element.68), channel_id=1, source_target_pairs={{0,3},{1,2},{2,1},{3,0},{4,7},{5,6},{6,5},{7,4},{8,11},{9,10},{10,... | collective-permute-start | bytes 3145736 | tf_op jit(solution)/shard_map/ppermute | solution.py:41
  427.3 14.8 %collective-permute-start.46 = (bf16[4,128,256]{2,1,0:T(8,128)(2,1)}, bf16[4,128,256]{2,1,0:T(8,128)(2,1)S(1)}, u32[]{:S(2)}, u32[]{:S(2)}) collective-permute-start(bf16[4,128,256]{2,1,0:T(8,128)(2,1)} %get-tuple-element.112), channel_id=1, source_target_pairs={{0,1},{1,0},{2,3},{3,2},{4,5},{5,4},{6,7},{7,6},{8,9},{9,8},{10,11... | collective-permute-start | bytes 786440 | tf_op jit(solution)/shard_map/ppermute | solution.py:41
  427.8 14.4 %collective-permute-start.47 = (bf16[4,128,256]{2,1,0:T(8,128)(2,1)}, bf16[4,128,256]{2,1,0:T(8,128)(2,1)S(1)}, u32[]{:S(2)}, u32[]{:S(2)}) collective-permute-start(bf16[4,128,256]{2,1,0:T(8,128)(2,1)} %get-tuple-element.114), channel_id=1, source_target_pairs={{0,2},{1,3},{2,0},{3,1},{4,6},{5,7},{6,4},{7,5},{8,10},{9,11},{10,... | collective-permute-start | bytes 786440 | tf_op jit(solution)/shard_map/ppermute | solution.py:41
  429.5 12.7 %collective-permute-start.48 = (bf16[4,128,256]{2,1,0:T(8,128)(2,1)}, bf16[4,128,256]{2,1,0:T(8,128)(2,1)S(1)}, u32[]{:S(2)}, u32[]{:S(2)}) collective-permute-start(bf16[4,128,256]{2,1,0:T(8,128)(2,1)} %get-tuple-element.113), channel_id=1, source_target_pairs={{0,3},{1,2},{2,1},{3,0},{4,7},{5,6},{6,5},{7,4},{8,11},{9,10},{10,... | collective-permute-start | bytes 786440 | tf_op jit(solution)/shard_map/ppermute | solution.py:41
  431.6 9.2 %collective-permute-start.52 = (f32[6,1536]{1,0:T(8,128)S(1)}, f32[6,1536]{1,0:T(8,128)S(1)}, u32[]{:S(2)}, u32[]{:S(2)}) collective-permute-start(f32[6,1536]{1,0:T(8,128)S(1)} %constant_dynamic-slice_fusion), channel_id=1, source_target_pairs={{0,1},{1,0},{2,3},{3,2},{4,5},{5,4},{6,7},{7,6},{8,9},{9,8},{10,11... | collective-permute-start | bytes 110600 | tf_op jit(solution)/shard_map/ppermute | solution.py:41
  438.9 23.5 %collective-permute-start.35 = (bf16[4,4,256,256]{3,2,1,0:T(8,128)(2,1)}, bf16[4,4,256,256]{3,2,1,0:T(8,128)(2,1)}, u32[]{:S(2)}, u32[]{:S(2)}) collective-permute-start(bf16[4,4,256,256]{3,2,1,0:T(8,128)(2,1)} %get-tuple-element.74), channel_id=1, source_target_pairs={{0,4},{4,0},{8,12},{12,8},{16,20},{20,16},{24,28},{28,24},{1,5},{5... | collective-permute-start | bytes 6291464 | tf_op jit(solution)/shard_map/ppermute | solution.py:41
  442.3 10.9 %collective-permute-start.49 = (bf16[2,128,256]{2,1,0:T(8,128)(2,1)S(1)}, bf16[2,128,256]{2,1,0:T(8,128)(2,1)S(1)}, u32[]{:S(2)}, u32[]{:S(2)}) collective-permute-start(bf16[2,128,256]{2,1,0:T(8,128)(2,1)S(1)} %slice.278), channel_id=1, source_target_pairs={{0,16},{4,20},{8,24},{12,28},{16,0},{20,4},{24,8},{28,12},{1,17},{... | collective-permute-start | bytes 393224 | tf_op jit(solution)/shard_map/ppermute | solution.py:41
  444.8 16.0 %collective-permute-start.42 = (bf16[1,4,128,768]{3,2,1,0:T(8,128)(2,1)}, bf16[1,4,128,768]{3,2,1,0:T(8,128)(2,1)}, u32[]{:S(2)}, u32[]{:S(2)}) collective-permute-start(bf16[1,4,128,768]{3,2,1,0:T(8,128)(2,1)} %get-tuple-element.75), channel_id=1, source_target_pairs={{0,4},{4,0},{8,12},{12,8},{16,20},{20,16},{24,28},{28,24},{1,5},{5... | collective-permute-start | bytes 2359304 | tf_op jit(solution)/shard_map/ppermute | solution.py:41
  445.1 9.2 %collective-permute-start.54 = (f32[2,6,1536]{2,1,0:T(8,128)S(1)}, f32[2,6,1536]{2,1,0:T(8,128)S(1)}, u32[]{:S(2)}, u32[]{:S(2)}) collective-permute-start(f32[2,6,1536]{2,1,0:T(8,128)S(1)} %get-tuple-element.129), channel_id=1, source_target_pairs={{0,16},{4,20},{8,24},{12,28},{16,0},{20,4},{24,8},{28,12},{1,17},{... | collective-permute-start | bytes 221192 | tf_op jit(solution)/shard_map/ppermute | solution.py:41
  462.3 40.1 %collective-permute-start.43 = (bf16[2,128,768]{2,1,0:T(8,128)(2,1)S(1)}, bf16[2,128,768]{2,1,0:T(8,128)(2,1)S(1)}, u32[]{:S(2)}, u32[]{:S(2)}) collective-permute-start(bf16[2,128,768]{2,1,0:T(8,128)(2,1)S(1)} %fusion.7), channel_id=1, source_target_pairs={{0,16},{4,20},{8,24},{12,28},{16,0},{20,4},{24,8},{28,12},{1,17},{... | collective-permute-start | bytes 1179656 | tf_op jit(solution)/shard_map/ppermute | solution.py:41
  465.1 43.3 %collective-permute-start.36 = (bf16[4,256,256]{2,1,0:T(8,128)(2,1)S(1)}, bf16[4,256,256]{2,1,0:T(8,128)(2,1)S(1)}, u32[]{:S(2)}, u32[]{:S(2)}) collective-permute-start(bf16[4,256,256]{2,1,0:T(8,128)(2,1)S(1)} %get-tuple-element.109), channel_id=1, source_target_pairs={{0,1},{1,0},{2,3},{3,2},{4,5},{5,4},{6,7},{7,6},{8,9},{9,8},{10,11... | collective-permute-start | bytes 1572872 | tf_op jit(solution)/shard_map/ppermute | solution.py:41
  466.8 41.6 %collective-permute-start.37 = (bf16[4,256,256]{2,1,0:T(8,128)(2,1)S(1)}, bf16[4,256,256]{2,1,0:T(8,128)(2,1)S(1)}, u32[]{:S(2)}, u32[]{:S(2)}) collective-permute-start(bf16[4,256,256]{2,1,0:T(8,128)(2,1)S(1)} %get-tuple-element.111), channel_id=1, source_target_pairs={{0,2},{1,3},{2,0},{3,1},{4,6},{5,7},{6,4},{7,5},{8,10},{9,11},{10,... | collective-permute-start | bytes 1572872 | tf_op jit(solution)/shard_map/ppermute | solution.py:41
  467.6 40.8 %collective-permute-start.38 = (bf16[4,256,256]{2,1,0:T(8,128)(2,1)S(1)}, bf16[4,256,256]{2,1,0:T(8,128)(2,1)S(1)}, u32[]{:S(2)}, u32[]{:S(2)}) collective-permute-start(bf16[4,256,256]{2,1,0:T(8,128)(2,1)S(1)} %get-tuple-element.110), channel_id=1, source_target_pairs={{0,3},{1,2},{2,1},{3,0},{4,7},{5,6},{6,5},{7,4},{8,11},{9,10},{10,... | collective-permute-start | bytes 1572872 | tf_op jit(solution)/shard_map/ppermute | solution.py:41
  508.7 7.2 %collective-permute-start.39 = (bf16[256,256]{1,0:T(8,128)(2,1)S(1)}, bf16[256,256]{1,0:T(8,128)(2,1)S(1)}, u32[]{:S(2)}, u32[]{:S(2)}) collective-permute-start(bf16[256,256]{1,0:T(8,128)(2,1)S(1)} %get-tuple-element.115), channel_id=1, source_target_pairs={{0,8},{4,12},{8,0},{12,4},{16,24},{20,28},{24,16},{28,20},{1,9},{5... | collective-permute-start | bytes 393224 | tf_op jit(solution)/shard_map/ppermute | solution.py:41
  508.8 11.1 %collective-permute-start.40 = (bf16[256,256]{1,0:T(8,128)(2,1)S(1)}, bf16[256,256]{1,0:T(8,128)(2,1)S(1)}, u32[]{:S(2)}, u32[]{:S(2)}) collective-permute-start(bf16[256,256]{1,0:T(8,128)(2,1)S(1)} %get-tuple-element.117), channel_id=1, source_target_pairs={{0,16},{4,20},{8,24},{12,28},{16,0},{20,4},{24,8},{28,12},{1,17},{... | collective-permute-start | bytes 393224 | tf_op jit(solution)/shard_map/ppermute | solution.py:41
  511.0 8.9 %collective-permute-start.41 = (bf16[256,256]{1,0:T(8,128)(2,1)S(1)}, bf16[256,256]{1,0:T(8,128)(2,1)S(1)}, u32[]{:S(2)}, u32[]{:S(2)}) collective-permute-start(bf16[256,256]{1,0:T(8,128)(2,1)S(1)} %get-tuple-element.116), channel_id=1, source_target_pairs={{0,24},{4,28},{8,16},{12,20},{16,8},{20,12},{24,0},{28,4},{1,25},{... | collective-permute-start | bytes 393224 | tf_op jit(solution)/shard_map/ppermute | solution.py:41
  (38 other events, 323.1 us)
Sparse Core Ops, SparseCore 0:
  61.7 157.4 all-gather.2
  262.5 150.7 reduce-scatter.2
  447.4 55.7 reduce-scatter.4

commit v3 on v2

--- a/solution.py
+++ b/solution.py
@@ -134,41 +134,42 @@
 class Bank:
     def __init__(self, array, start, columns):
         self.arrays, self.start, self.columns = [array], start, columns
-        self.rows = array.shape[1]
+        self.rows = array.shape[2]
 
 
 def bank_copies(bank, ref, seq, first, columns, target, sems, column):
-    seqs, found = axis_size("seq"), []
-    for owner in range(bank.arrays[0].shape[0] // seqs):
-        source = ref.at[owner * seqs + seq, :, pl.ds(bank.start + first, columns)]
+    found = []
+    for owner in range(bank.arrays[0].shape[0]):
+        source = ref.at[owner, seq, :, pl.ds(bank.start + first, columns)]
         spot = target.at[pl.ds(owner * bank.rows, bank.rows), pl.ds(column, columns)]
         found.append(pltpu.make_async_copy(source, spot, sems.at[len(found)]))
     return found
 
 
-def pack_kernel(*refs):
-    *head, w_up_ref, w_down_ref, _, _, bank_ref = refs
+def pack_kernel(count, *refs):
+    *head, w_up_ref, w_down_ref = refs[:count]
+    bank_ref = refs[-1]
     parts = [ref[...].T for ref in head] + [w_up_ref[...], w_down_ref[...].T]
     bank_ref[...] = jnp.concatenate(parts, 1)
 
 
-def pack_bank(earlier, too, *weights):
+def pack_bank(earlier, *weights):
     rows = weights[-2].shape[0]
     return pl.pallas_call(
-        pack_kernel,
+        functools.partial(pack_kernel, len(weights)),
         out_shape=jax.ShapeDtypeStruct((rows, sum(weight.size for weight in weights) // rows), BF16),
-        in_specs=[pl.BlockSpec(memory_space=pltpu.VMEM)] * len(weights) + [ANY_SPEC] * 2,
+        in_specs=[pl.BlockSpec(memory_space=pltpu.VMEM)] * len(weights) + [ANY_SPEC] * len(earlier),
         compiler_params=pltpu.CompilerParams(vmem_limit_bytes=VMEM_LIMIT),
         name="pack_bank",
-    )(*weights, earlier, too)
+    )(*weights, *earlier)
 
 
 def unpack_kernel(chunk, sums_ref, up_ref, down_ref):
     for part in range(up_ref.shape[1] // chunk):
         start = 2 * part * chunk
         span = slice(part * chunk, (part + 1) * chunk)
-        up_ref[:, span] = sums_ref[:, start : start + chunk].astype(F32)
-        down_ref[span, :] = sums_ref[:, start + chunk : start + 2 * chunk].astype(F32).T
+        up_ref[:, span] = sums_ref[:, start : start + chunk]
+        down_ref[span, :] = sums_ref[:, start + chunk : start + 2 * chunk].T
 
 
 def unpack_sums(sums, units, chunk):
@@ -183,11 +184,10 @@
 
 def weight_copies(pieces, refs, target, sems, place_ref, relative):
     if isinstance(pieces, Bank):
-        copies, seqs = [], axis_size("seq")
-        per_seq = pieces.arrays[0].shape[0] // seqs
-        for seq in range(seqs):
+        copies, owners = [], pieces.arrays[0].shape[0]
+        for seq in range(axis_size("seq")):
+            part_sems = sems.at[pl.ds(seq * owners, owners)]
             column = pl.multiple_of((place_ref[1] ^ seq) * pieces.columns, pieces.columns)
-            part_sems = sems.at[pl.ds(seq * per_seq, per_seq)]
             copies += bank_copies(pieces, refs[0], seq, 0, pieces.columns, target, part_sems, column)
         return copies
     if pieces.masks is None:
@@ -209,7 +209,7 @@
 
 def copy_count(pieces):
     if isinstance(pieces, Bank):
-        return pieces.arrays[0].shape[0]
+        return axis_size("seq") * pieces.arrays[0].shape[0]
     return 1 if pieces.masks is None else sum(len(table) for table in pieces.masks)
 
 
@@ -235,24 +235,29 @@
     )(place, *pieces.arrays)
 
 
+def pick(values, index, axis):
+    return lax.dynamic_index_in_dim(values, index, axis, keepdims=False)
+
+
 def send_seq(held):
-    total = held[0]
+    total, sent = held[0], []
     for mask in range(1, held.shape[0]):
-        total = total + swap(held[mask].astype(BF16), "seq", mask).astype(F32)
-    return total
-
-
-def send_chips(held):
+        sent.append(held[mask].astype(BF16))
+        total = total + swap(sent[-1], "seq", mask).astype(F32)
+    return total, sent
+
+
+def send_chips(held, dtype=BF16):
     total = held[0]
     for mask in chip_masks():
-        total = total + swap(held[mask // CORES].astype(BF16), "dp", mask).astype(F32)
+        total = total + swap(held[mask // CORES].astype(dtype), "dp", mask).astype(F32)
     return total
 
 
-def halve_chips(held):
-    for mask in reversed(bits("dp")):
+def halve(held, axis):
+    for mask in reversed(bits(axis)):
         count = held.shape[0] // 2
-        held = held[:count] + swap(held[count:].astype(BF16), "dp", mask).astype(F32)
+        held = held[:count].astype(F32) + swap(held[count:].astype(BF16), axis, mask).astype(F32)
     return held[0]
 
 
@@ -265,57 +270,63 @@
     return source_ref[pl.ds(pl.multiple_of(owner * rows, rows), rows), :]
 
 
-def weight_grad_kernel(count, seqs, by_mask, place_ref, *rest):
-    x_refs, y_ref, (keep_ref, give_ref, xt_ref) = rest[:count], rest[count], rest[-3:]
+def weight_grad_kernel(count, y_count, by_token, seqs, by_mask, place_ref, *rest):
+    x_refs, y_refs, (keep_ref, give_ref, xt_ref) = rest[:count], rest[count : count + y_count], rest[-3:]
     chip = pl.program_id(0)
-    per_piece = len(y_ref.shape) == 3
     rows, columns = keep_ref.shape[-2:]
-    wide = x_refs[0].shape[1]
+    tokens, wide = x_refs[0].shape
 
     @pl.when(chip == 0)
     def _():
         for piece, ref in enumerate(x_refs):
-            if per_piece:
-                xt_ref[:, piece * ref.shape[0] : (piece + 1) * ref.shape[0]] = ref[...].T
+            if by_token:
+                xt_ref[:, piece * tokens : (piece + 1) * tokens] = ref[...].T
             else:
                 xt_ref[piece * wide : (piece + 1) * wide, :] = ref[...].T
 
-    y = y_ref[...].reshape(-1, y_ref.shape[-1])
+    parts = [ref[...].reshape(-1, ref.shape[-1]) for ref in y_refs]
+    y = parts[0] if y_count == 1 else jnp.concatenate(parts)
     for core, out_ref in ((0, keep_ref), (1, give_ref)):
         result = dot(split_rows(place_ref, xt_ref, rows, chip, core, by_mask), y).astype(BF16)
         for seq in range(seqs):
             out_ref[seq, 0] = result[:, seq * columns : (seq + 1) * columns]
 
 
-def weight_grad(place, xs, y, rows, seqs, by_mask, *earlier):
+def weight_grad(place, xs, ys, by_token, rows, seqs, by_mask, *earlier):
     chips = axis_size("dp") // CORES
     tokens, wide = xs[0].shape
-    columns = y.shape[-1] // seqs
-    shape = (wide, len(xs) * tokens) if y.ndim == 3 else (len(xs) * wide, tokens)
+    columns = ys[0].shape[-1] // seqs
+    shape = (wide, len(xs) * tokens) if by_token else (len(xs) * wide, tokens)
     out = jax.ShapeDtypeStruct((seqs, chips, rows, columns), BF16)
     spec = pl.BlockSpec((seqs, 1, rows, columns), lambda i: (0, i, 0, 0))
     constant = lambda array: pl.BlockSpec(array.shape, lambda i: (0,) * array.ndim)
     return pl.pallas_call(
-        functools.partial(weight_grad_kernel, len(xs), seqs, by_mask),
+        functools.partial(weight_grad_kernel, len(xs), len(ys), by_token, seqs, by_mask),
         grid=(chips,),
         out_shape=(out, out),
-        in_specs=[SMEM_SPEC] + [constant(x) for x in xs] + [constant(y)] + [ANY_SPEC] * len(earlier),
+        in_specs=[SMEM_SPEC] + [constant(array) for array in list(xs) + list(ys)] + [ANY_SPEC] * len(earlier),
         out_specs=(spec, spec),
         scratch_shapes=[pltpu.VMEM(shape, BF16)],
         compiler_params=pltpu.CompilerParams(vmem_limit_bytes=VMEM_LIMIT),
         cost_estimate=pl.CostEstimate(
             flops=2 * math.prod(shape) * columns * seqs,
-            bytes_accessed=2 * (math.prod(shape) + y.size) + 2 * shape[0] * columns * seqs,
+            bytes_accessed=2 * math.prod(shape) + 4 * shape[0] * columns * seqs,
             transcendentals=0,
         ),
         name="weight_grad",
-    )(place, *xs, y, *earlier)
-
-
-def qkv_kernel(width, scale, x_ref, w_ref, cos_ref, sin_ref, *rest):
-    out_ref = rest[-1]
+    )(place, *xs, *ys, *earlier)
+
+
+def project_kernel(pieces, width, scale, w_ref, cos_ref, sin_ref, *rest):
+    x_refs, (out_ref, x_ref) = rest[:pieces], rest[pieces:]
     half = width // 2
-    projected = dot(x_ref[0], w_ref[...])
+    for piece in range(pieces):
+
+        @pl.when(pl.program_id(0) == piece)
+        def _():
+            x_ref[...] = x_refs[piece][0]
+
+    projected = dot(x_ref[...], w_ref[...])
     cosine, sine = cos_ref[0], sin_ref[0]
     for part, factor in ((0, scale), (1, 1.0)):
         low = projected[:, part * width : part * width + half]
@@ -325,38 +336,31 @@
     out_ref[0, 0, :, 2 * width :] = projected[:, 2 * width :].astype(BF16)
 
 
-def project_piece(piece, normed, weights, cos_table, sin_table, held, scale):
-    rows, frames, model = normed.shape
-    pieces = cos_table.shape[0]
+def project(normed, weights, cos_table, sin_table, scale):
+    pieces = len(normed)
+    _, frames, model = normed[0].shape
     width = weights.shape[1] // 3
-    in_specs = [
-        pl.BlockSpec((1, frames, model), lambda r: (r, 0, 0)),
-        pl.BlockSpec((model, 3 * width), lambda r: (0, 0)),
-        pl.BlockSpec((1, frames, width // 2), lambda r: (piece, 0, 0)),
-        pl.BlockSpec((1, frames, width // 2), lambda r: (piece, 0, 0)),
-    ]
-    arrays = [normed, weights, cos_table, sin_table]
-    aliases = {}
-    if held is not None:
-        in_specs.append(pl.BlockSpec(memory_space=pl.ANY))
-        arrays.append(held)
-        aliases = {4: 0}
+    table = pl.BlockSpec((1, frames, width // 2), lambda s: (s, 0, 0))
     return pl.pallas_call(
-        functools.partial(qkv_kernel, width, scale),
-        grid=(rows,),
-        out_shape=jax.ShapeDtypeStruct((pieces, rows, frames, 3 * width), BF16),
-        in_specs=in_specs,
-        out_specs=pl.BlockSpec((1, 1, frames, 3 * width), lambda r: (piece, r, 0, 0)),
-        input_output_aliases=aliases,
+        functools.partial(project_kernel, pieces, width, scale),
+        grid=(pieces,),
+        out_shape=jax.ShapeDtypeStruct((pieces, 1, frames, 3 * width), BF16),
+        in_specs=[pl.BlockSpec((model, 3 * width), lambda s: (0, 0)), table, table]
+        + [pl.BlockSpec((1, frames, model), lambda s: (0, 0, 0))] * pieces,
+        out_specs=pl.BlockSpec((1, 1, frames, 3 * width), lambda s: (s, 0, 0, 0)),
+        scratch_shapes=[pltpu.VMEM((frames, model), BF16)],
         compiler_params=pltpu.CompilerParams(vmem_limit_bytes=VMEM_LIMIT),
         cost_estimate=pl.CostEstimate(
-            flops=2 * rows * frames * model * 3 * width, bytes_accessed=5 * rows * frames * model, transcendentals=0
+            flops=2 * pieces * frames * model * 3 * width,
+            bytes_accessed=2 * pieces * frames * (model + 3 * width),
+            transcendentals=0,
         ),
         name="project",
-    )(*arrays)
-
-
-def spread_back_kernel(grad_ref, weight_ref, *out_refs):
+    )(weights, cos_table, sin_table, *normed)
+
+
+def spread_back_kernel(count, grad_ref, weight_ref, *rest):
+    out_refs = rest[-count:]
     piece = pl.program_id(0)
     result = against(grad_ref[0, 0], weight_ref[...]).astype(BF16)
     for position, ref in enumerate(out_refs):
@@ -366,7 +370,7 @@
             ref[0] = result
 
 
-def spread_back(grad_qkv, weights):
+def spread_back(grad_qkv, weights, *earlier):
     pieces, rows, frames, triple = grad_qkv.shape
     model = weights.shape[0]
 
@@ -377,13 +381,14 @@
         )
 
     return pl.pallas_call(
-        spread_back_kernel,
+        functools.partial(spread_back_kernel, pieces - 1),
         grid=(pieces - 1, rows),
         out_shape=(jax.ShapeDtypeStruct((rows, frames, model), BF16),) * (pieces - 1),
         in_specs=[
             pl.BlockSpec((1, 1, frames, triple), lambda m, r: (m + 1, r, 0, 0)),
             pl.BlockSpec(weights.shape, lambda m, r: (0, 0)),
-        ],
+        ]
+        + [ANY_SPEC] * len(earlier),
         out_specs=tuple(out_spec(position) for position in range(pieces - 1)),
         compiler_params=pltpu.CompilerParams(vmem_limit_bytes=VMEM_LIMIT),
         cost_estimate=pl.CostEstimate(
@@ -392,7 +397,7 @@
             transcendentals=0,
         ),
         name="spread_back",
-    )(grad_qkv, weights)
+    )(grad_qkv, weights, *earlier)
 
 
 def head_lanes(shape, heads, width, split):
@@ -403,7 +408,8 @@
     return lane // size
 
 
-def spread_back_kernel(grad_ref, weight_ref, *out_refs):
+def spread_back_kernel(count, grad_ref, weight_ref, *rest):
+    out_refs = rest[-count:]
     piece = pl.program_id(0)
     result = against(grad_ref[0, 0], weight_ref[...]).astype(BF16)
     for position, ref in enumerate(out_refs):
@@ -413,7 +419,7 @@
             ref[0] = result
 
 
-def spread_back(grad_qkv, weights):
+def spread_back(grad_qkv, weights, *earlier):
     pieces, rows, frames, triple = grad_qkv.shape
     model = weights.shape[0]
 
@@ -424,13 +430,14 @@
         )
 
     return pl.pallas_call(
-        spread_back_kernel,
+        functools.partial(spread_back_kernel, pieces - 1),
         grid=(pieces - 1, rows),
         out_shape=(jax.ShapeDtypeStruct((rows, frames, model), BF16),) * (pieces - 1),
         in_specs=[
             pl.BlockSpec((1, 1, frames, triple), lambda m, r: (m + 1, r, 0, 0)),
             pl.BlockSpec(weights.shape, lambda m, r: (0, 0)),
-        ],
+        ]
+        + [ANY_SPEC] * len(earlier),
         out_specs=tuple(out_spec(position) for position in range(pieces - 1)),
         compiler_params=pltpu.CompilerParams(vmem_limit_bytes=VMEM_LIMIT),
         cost_estimate=pl.CostEstimate(
@@ -439,7 +446,7 @@
             transcendentals=0,
         ),
         name="spread_back",
-    )(grad_qkv, weights)
+    )(grad_qkv, weights, *earlier)
 
 
 def head_lanes(shape, heads, width, split):
@@ -488,7 +495,7 @@
             out_refs[piece][0] = result
 
 
-def attend(qkv, seg, heads):
+def attend(qkv, seg, row, heads):
     pieces, rows, frames, triple = qkv.shape
     width = triple // 3
     length = pieces * frames
@@ -499,7 +506,7 @@
         + (jax.ShapeDtypeStruct((rows, pieces, heads, frames), F32),),
         in_specs=[
             pl.BlockSpec((pieces, 1, frames, triple), lambda r, s: (0, r, 0, 0)),
-            pl.BlockSpec((1, pieces, frames), lambda r, s: (r, 0, 0)),
+            pl.BlockSpec((1, pieces, frames), lambda r, s: (row, 0, 0)),
         ],
         out_specs=(pl.BlockSpec((1, frames, width), lambda r, s: (r, 0, 0)),) * pieces
         + (pl.BlockSpec((1, 1, heads, frames), lambda r, s: (r, s, 0, 0)),),
@@ -522,7 +529,7 @@
 def attend_back_kernel(heads, width, scale, qkv_ref, seg_ref, lse_ref, cos_ref, sin_ref, *rest):
     pieces, _, frames, _ = qkv_ref.shape
     out_refs, grad_refs = rest[:pieces], rest[pieces : 2 * pieces]
-    result_ref, kt_ref, dk_ref, dv_ref, dqt_ref, seg_col_ref, out_ref, grad_ref = rest[2 * pieces :]
+    result_ref, kt_ref, dk_ref, dv_ref, dqt_ref, seg_col_ref, out_ref, grad_ref = rest[-8:]
     length = pieces * frames
     step = pl.program_id(1)
     size, half = width // heads, width // 2
@@ -582,7 +589,7 @@
             result_ref[piece, 0, :, 2 * width :] = dv_ref[span, :].astype(BF16)
 
 
-def attend_back(qkv, seg, lse, cos_table, sin_table, outs, grads, heads, scale):
+def attend_back(qkv, seg, row, lse, cos_table, sin_table, outs, grads, heads, scale, earlier):
     pieces, rows, frames, triple = qkv.shape
     width = triple // 3
     length = pieces * frames
@@ -595,12 +602,13 @@
         out_shape=jax.ShapeDtypeStruct(qkv.shape, BF16),
         in_specs=[
             whole,
-            pl.BlockSpec((1, pieces, frames), lambda r, s: (r, 0, 0)),
+            pl.BlockSpec((1, pieces, frames), lambda r, s: (row, 0, 0)),
             pl.BlockSpec((1, 1, heads, frames), lambda r, s: (r, s, 0, 0)),
             table,
             table,
         ]
-        + [block] * (2 * pieces),
+        + [block] * (2 * pieces)
+        + [ANY_SPEC] * len(earlier),
         out_specs=whole,
         scratch_shapes=[
             pltpu.VMEM((width, length), BF16),
@@ -618,7 +626,7 @@
             transcendentals=rows * heads * length * length,
         ),
         name="attend_back",
-    )(qkv, seg, lse, cos_table, sin_table, *outs, *grads)
+    )(qkv, seg, lse, cos_table, sin_table, *outs, *grads, *earlier)
 
 
 def mlp_kernel(bank, chunk, place_ref, normed_ref, grad_ref, bank_ref, *rest):
@@ -626,7 +634,7 @@
     step, rows = pl.program_id(0), bank.rows
     units = bank.columns // 2
     per_place = units // chunk
-    half = bank.arrays[0].shape[0] // axis_size("seq")
+    half = bank.arrays[0].shape[0]
 
     def copies(block, slot):
         start = (block % per_place) * chunk
@@ -669,15 +677,13 @@
     gn_ref[...] += against(grad_before, up)
     result_ref[:, :chunk] = dot(nt_ref[...], grad_before).astype(BF16)
     result_ref[:, chunk:] = dot(gt_ref[...], activated).astype(BF16)
-    for chip in range(grads_ref.shape[2]):
-        for core in range(CORES):
-            owner = chip * CORES + core
-            grads_ref[core, 0, chip] = result_ref[owner * rows : (owner + 1) * rows, :]
+    for owner in range(grads_ref.shape[0]):
+        grads_ref[owner, 0] = result_ref[owner * rows : (owner + 1) * rows, :]
 
 
 def mlp(place, normed, grad, bank):
     tokens, model = normed.shape
-    seqs, chips = axis_size("seq"), axis_size("dp") // CORES
+    seqs, owners = axis_size("seq"), axis_size("dp")
     units = bank.columns // 2
     chunk = min(512, units)
     per_place = units // chunk
@@ -687,21 +693,19 @@
         functools.partial(mlp_kernel, bank, chunk),
         grid=(seqs * per_place,),
         out_shape=(jax.ShapeDtypeStruct((tokens, model), F32),) * 2
-        + (jax.ShapeDtypeStruct((CORES, seqs, chips, bank.rows, 2 * units), BF16),),
+        + (jax.ShapeDtypeStruct((owners, seqs, bank.rows, 2 * units), BF16),),
         in_specs=[SMEM_SPEC, whole, whole, ANY_SPEC],
         out_specs=(
             whole,
             whole,
-            pl.BlockSpec(
-                (CORES, 1, chips, bank.rows, 2 * chunk), lambda i: (0, i // per_place, 0, 0, i % per_place)
-            ),
+            pl.BlockSpec((owners, 1, bank.rows, 2 * chunk), lambda i: (0, i // per_place, 0, i % per_place)),
         ),
         scratch_shapes=[
             pltpu.VMEM((model, tokens), BF16),
             pltpu.VMEM((model, tokens), BF16),
             pltpu.VMEM((2, model, 2 * chunk), BF16),
             pltpu.VMEM((model, 2 * chunk), BF16),
-            pltpu.SemaphoreType.DMA((2, 2 * CORES * chips)),
+            pltpu.SemaphoreType.DMA((2, 2 * owners)),
         ],
         compiler_params=pltpu.CompilerParams(vmem_limit_bytes=VMEM_LIMIT),
         cost_estimate=pl.CostEstimate(
@@ -744,46 +748,55 @@
         )
 
 
-def load_weight(pieces, refs, target, sems, place_ref, relative):
-    @pl.when(pl.program_id(0) == 0)
-    def _():
-        copies = weight_copies(pieces, refs, target, sems, place_ref, relative)
-        for copy in copies:
-            copy.start()
-        for copy in copies:
-            copy.wait()
-
-
-def row_call(kernel, name, place, rows, by_row, fixed, pieces, weight_shape, outs, flops, earlier=()):
-    row_spec = lambda shape: pl.BlockSpec((1,) + tuple(shape[1:]), lambda r: (r,) + (0,) * (len(shape) - 1))
-    fixed_specs = [pl.BlockSpec(array.shape, lambda r, n=array.ndim: (0,) * n) for array in fixed]
-    scalars = [array for array in place]
+def start_weight(pieces, refs, target, sems, place_ref, relative):
+    copies = weight_copies(pieces, refs, target, sems, place_ref, relative)
+    for copy in copies:
+        copy.start()
+    return copies
+
+
+def wait_all(copies):
+    for copy in copies:
+        copy.wait()
+
+
+def row_call(kernel, name, place, row, by_row, fixed, pieces, weight_shape, outs, held, flops, earlier=()):
+    row_spec = lambda shape: pl.BlockSpec(
+        (1,) + tuple(shape[1:]), lambda i: (row if shape[0] > 1 else 0,) + (0,) * (len(shape) - 1)
+    )
+    fixed_specs = [pl.BlockSpec(array.shape, lambda i, n=array.ndim: (0,) * n) for array in fixed]
     size = sum(array.size * array.dtype.itemsize for array in by_row) + 2 * math.prod(weight_shape)
+    first = len(place) + len(by_row) + len(fixed) + len(pieces.arrays)
+    kept = [position for position, out in enumerate(outs) if held and out.shape[0] > 1]
+    held = [held[position] for position in kept]
+    aliases = {first + number: position for number, position in enumerate(kept)}
     return pl.pallas_call(
         kernel,
-        grid=(rows,),
+        grid=(1,),
         out_shape=tuple(outs),
-        in_specs=[SMEM_SPEC] * len(scalars)
+        in_specs=[SMEM_SPEC] * len(place)
         + [row_spec(array.shape) for array in by_row]
         + fixed_specs
-        + [ANY_SPEC] * (len(pieces.arrays) + len(earlier)),
+        + [ANY_SPEC] * (len(pieces.arrays) + len(held) + len(earlier)),
         out_specs=tuple(row_spec(out.shape) for out in outs),
+        input_output_aliases=aliases,
         scratch_shapes=[pltpu.VMEM(weight_shape, BF16), pltpu.SemaphoreType.DMA((copy_count(pieces),))],
         compiler_params=pltpu.CompilerParams(vmem_limit_bytes=VMEM_LIMIT),
-        cost_estimate=pl.CostEstimate(flops=flops, bytes_accessed=2 * size, transcendentals=0),
+        cost_estimate=pl.CostEstimate(flops=flops, bytes_accessed=size, transcendentals=0),
         name=name,
-    )(*scalars, *by_row, *fixed, *pieces.arrays, *earlier)
-
-
-def enter_kernel(pieces, place_ref, coef_ref, frames_ref, skip_ref, cond_ref, seg_ref, mod_ref, *rest):
-    refs, (hidden_ref, normed_ref, weight_ref, sems) = rest[:-4], rest[-4:]
-    load_weight(pieces, refs, weight_ref, sems, place_ref, False)
-    row, model = pl.program_id(0), frames_ref.shape[2]
+    )(*place, *by_row, *fixed, *pieces.arrays, *held, *earlier)
+
+
+def enter_kernel(pieces, row, place_ref, coef_ref, frames_ref, skip_ref, cond_ref, seg_ref, mod_ref, *rest):
+    refs, (hidden_ref, normed_ref, weight_ref, sems) = rest[: len(pieces.arrays)], rest[-4:]
+    copies = start_weight(pieces, refs, weight_ref, sems, place_ref, False)
+    model = frames_ref.shape[2]
     owner = utterance_of(seg_ref)
     count = mod_ref.shape[1]
     factor = coef_ref[row, count - 1]
     for position in range(count - 2, -1, -1):
         factor = jnp.where(owner == float(position), coef_ref[row, position], factor)
+    wait_all(copies)
     hidden = dot(frames_ref[0], weight_ref[:model, :]) + dot(skip_ref[0], weight_ref[model:, :])
     hidden = hidden + factor * cond_ref[0].astype(F32)
     hidden_ref[0] = hidden
@@ -793,12 +806,13 @@
 
 def branch_kernel(pieces, count, place_ref, *rest):
     blocks, (hidden_ref, cot_ref, seg_ref, mod_ref) = rest[:count], rest[count : count + 4]
-    refs = rest[count + 4 : -7]
+    refs = rest[count + 4 : count + 4 + len(pieces.arrays)]
     attn_ref, branch_ref, middle_ref, normed_ref, grad_ref, weight_ref, sems = rest[-7:]
-    load_weight(pieces, refs, weight_ref, sems, place_ref, True)
+    copies = start_weight(pieces, refs, weight_ref, sems, place_ref, True)
     owner = utterance_of(seg_ref)
     attn = jnp.concatenate([block[0] for block in blocks], -1)
     attn_ref[0] = attn
+    wait_all(copies)
     branch = against(attn, weight_ref[...])
     branch_ref[0] = branch
     middle = hidden_ref[0] + by_frame(owner, mod_ref, 2) * branch
@@ -810,9 +824,9 @@
 
 def middle_back_kernel(pieces, seqs, place_ref, middle_ref, fed_ref, gn_ref, cot_ref, branch_ref, seg_ref, mod_ref, *rest):
     refs = rest[: len(pieces.arrays)]
-    output_ref, grad_ref, grad_branch_ref, sums_ref = rest[len(refs) : len(refs) + 4]
-    block_refs, (weight_ref, sems) = rest[len(refs) + 4 : -2], rest[-2:]
-    load_weight(pieces, refs, weight_ref, sems, place_ref, True)
+    output_ref, grad_ref, grad_branch_ref, sums_ref = rest[-6 - seqs : -2 - seqs]
+    block_refs, (weight_ref, sems) = rest[-2 - seqs : -2], rest[-2:]
+    copies = start_weight(pieces, refs, weight_ref, sems, place_ref, True)
     owner, count = utterance_of(seg_ref), mod_ref.shape[1]
     middle, fed, grad_norm, grad_out = middle_ref[0], fed_ref[0], gn_ref[0], cot_ref[0].astype(F32)
     output_ref[0] = (middle + by_frame(owner, mod_ref, 5) * fed).astype(BF16)
@@ -821,6 +835,7 @@
     grad_ref[0] = grad_middle
     grad_branch = (by_frame(owner, mod_ref, 2) * grad_middle).astype(BF16)
     grad_branch_ref[0] = grad_branch
+    wait_all(copies)
     grad_attn = dot(grad_branch, weight_ref[...]).astype(BF16)
     width = grad_attn.shape[1] // seqs
     for seq in range(seqs):
@@ -836,7 +851,7 @@
     seg_ref, mod_ref, qkv_ref = rest[seqs - 1 : seqs + 2]
     refs = rest[seqs + 2 : seqs + 2 + len(pieces.arrays)]
     columns_ref, frames_ref, skip_ref, sums_ref, weight_ref, sems = rest[-6:]
-    load_weight(pieces, refs, weight_ref, sems, place_ref, False)
+    copies = start_weight(pieces, refs, weight_ref, sems, place_ref, False)
     owner, count = utterance_of(seg_ref), mod_ref.shape[1]
     grad_norm = against(own_ref[0], qkv_ref[...])
     for ref in got:
@@ -845,6 +860,7 @@
     grad = standardize_back(grad_norm * (1.0 + by_frame(owner, mod_ref, 1)), standard, inverse)
     grad_hidden = (grad_middle_ref[0] + grad).astype(BF16)
     model = grad_hidden.shape[1]
+    wait_all(copies)
     frames_ref[0] = against(grad_hidden, weight_ref[:model, :]).astype(BF16)
     skip_ref[0] = against(grad_hidden, weight_ref[model:, :]).astype(BF16)
     add_up(owner, grad_norm, sums_ref, 0, count)
@@ -901,15 +917,27 @@
     skip_near = skip_parts.arrays[0]
 
     small = jnp.concatenate([flow_times, drop_flags.astype(F32)], 1)
-    small = gather_steps(small, [("dp", [mask]) for mask in bits("dp") + [1]])
-    small = small.reshape((CORES, chips) + small.shape[-2:])
+    small = gather_steps(small, [("dp", chip_masks())])
+    mod_rows, mod_columns = w_mod.shape
+    mod_pair = swap(w_mod, "dp", 1)
+    utterances = row_count * segs
+
+    def activity_of(values, owner):
+        result = jax.nn.silu(time_embed(values, model)).astype(BF16).reshape(-1, model)
+        return lax.dynamic_slice_in_dim(result, owner * mod_rows, mod_rows, 1)
+
+    modulation = dot(activity_of(small[..., :segs], dp), w_mod)
+    modulation = modulation + dot(activity_of(small[..., :segs], dp ^ 1), mod_pair)
+    modulation = modulation.reshape(chips, utterances, mod_columns)
+    for mask in reversed(bits("dp")):
+        count = modulation.shape[0] // 2
+        modulation = modulation[:count] + swap(modulation[count:], "dp", mask)
+    modulation = modulation[0]
+
+    small = jnp.stack([small, swap(small, "dp", 1)])
     dropped = jnp.sum(small[..., segs:])
     slots = float(row_count * segs * dp_size)
     cond_scale = slots / jnp.maximum(slots - dropped, 1.0)
-    utterances = row_count * segs
-    activity = jax.nn.silu(time_embed(small[..., :segs], model)).astype(BF16).reshape(dp_size * utterances, model)
-    mod_rows, mod_columns = w_mod.shape
-    activity = lax.dynamic_slice_in_dim(activity, dp * mod_rows, mod_rows, 1)
     coefficients = (1.0 - drop_flags.astype(F32)) * cond_scale
 
     if narrow(w_skip):
@@ -920,12 +948,6 @@
         arrived = skip_parts.arrays[-1]
         skip_parts = gather_over(skip_parts, "dp", [1])
 
-    partial = dot(activity, w_mod).reshape(CORES, chips, utterances, mod_columns)
-    modulation = partial[0] + swap(partial[1], "dp", 1)
-    for mask in reversed(bits("dp")):
-        count = modulation.shape[0] // 2
-        modulation = modulation[:count] + swap(modulation[count:], "dp", mask)
-    modulation = modulation[0]
     extra = -(-tokens // mod_columns)
     numbers = jnp.pad(seg_ids.astype(F32).reshape(-1), (0, extra * mod_columns - tokens)).reshape(extra, mod_columns)
     own_mod = jnp.concatenate([modulation, numbers])
@@ -936,112 +958,172 @@
     modulation = modulation.swapaxes(0, 1).reshape(row_count, segs, 6, model)
     seg_here = segments[:, :1]
 
+    qkv_parts = start_gather(qkv_shard)
+    for mask in bits("dp"):
+        qkv_parts = pack(gather_over(qkv_parts, "dp", [mask]))
+    qkv_full = assemble(gather_over(qkv_parts, "dp", [1]), place, (dp_size * rows, 3 * width))
+
     units = w_up.shape[1]
-    if narrow(w_out.T):
-        out_parts = whole_columns(w_out.T, place, True)
-        bank = pack_bank(arrived, all_mod, w_up, w_down)
-    else:
-        bank = pack_bank(arrived, all_mod, w_out, w_up, w_down)
+    bank = pack_bank([arrived, all_mod, qkv_parts.arrays[0]], w_up, w_down)
     bank = lax.all_gather(bank, AXES["all"], axis=0)
-    lead = bank.shape[2] - 2 * units
-    if lead:
-        out_parts = Bank(bank, 0, lead)
-    bank = Bank(bank, lead, 2 * units)
-
-    qkv_full = assemble(
-        gather_over(pack(gather_over(start_gather(after(qkv_shard, arrived)), "dp", chip_masks())), "dp", [1]),
-        place,
-        (dp_size * rows, 3 * width),
-    )
-    hidden, normed = row_call(
-        functools.partial(enter_kernel, skip_parts),
-        "enter",
-        [place, coefficients],
-        row_count,
-        [frames, skip_in, cond, seg_here, modulation],
-        [],
-        skip_parts,
-        (2 * model, model),
-        [shape_of(frame_shape, F32), shape_of(frame_shape, BF16)],
-        4 * tokens * model * model,
-    )
+    bank = Bank(bank.reshape((dp_size, seq_size) + bank.shape[1:]), 0, 2 * units)
+
+    row_range = range(row_count)
+    one_row = (1,) + frame_shape[1:]
+    entered, normed = None, []
+    for row in row_range:
+        entered = row_call(
+            functools.partial(enter_kernel, skip_parts, row),
+            "enter",
+            [place, coefficients],
+            row,
+            [frames, skip_in, cond, seg_here, modulation],
+            [],
+            skip_parts,
+            (2 * model, model),
+            [shape_of(frame_shape, F32), shape_of(one_row, BF16)],
+            entered,
+            4 * frame_count * model * model,
+        )
+        normed.append(entered[1])
+    hidden = entered[0]
 
     positions = (jnp.arange(seq_size) ^ seq)[:, None] * frame_count + jnp.arange(frame_count)
     frequency = jnp.exp((jnp.arange(width // 2) % half).astype(F32) * (-2.0 * math.log(10000.0) / head_dim))
     angles = positions.astype(F32)[..., None] * frequency
     cos_table, sin_table = jnp.cos(angles), jnp.sin(angles)
 
-    pieces = [normed] + [swap(normed, "seq", mask) for mask in partners]
-    qkv = None
-    for position, piece in enumerate(pieces):
-        qkv = project_piece(position, piece, qkv_full, cos_table, sin_table, qkv, scale)
-
-    attended, lse = attend(qkv, segments, heads)
-    blocks = [attended[0]] + [swap(attended[mask], "seq", mask) for mask in partners]
-    attn, branch, middle, normed_two, grad_fed = row_call(
-        functools.partial(branch_kernel, out_parts, seq_size),
-        "branch",
-        [place],
-        row_count,
-        blocks + [hidden, cotangent, seg_here, modulation],
-        [],
-        out_parts,
-        (model, model),
-        [
-            shape_of(frame_shape, BF16),
-            shape_of(frame_shape, F32),
-            shape_of(frame_shape, F32),
-            shape_of(frame_shape, BF16),
-            shape_of(frame_shape, BF16),
-        ],
-        2 * tokens * model * model,
-    )
+    pieces = [[normed[row]] + [swap(normed[row], "seq", mask) for mask in partners] for row in row_range]
+    if narrow(w_out.T):
+        out_parts = whole_columns(w_out.T, place, True)
+    else:
+        out_parts = pack(gather_over(start_gather(after(w_out.T, pieces[0][-1])), "dp", chip_masks()))
+        out_parts = gather_over(gather_over(out_parts, "seq", partners), "dp", [1])
+    qkv, attended, lse, branched = [], [], [], None
+    for row in row_range:
+        qkv.append(project(pieces[row], qkv_full, cos_table, sin_table, scale))
+        result = attend(qkv[row], segments, row, heads)
+        attended.append(result[0])
+        lse.append(result[1])
+    for row in row_range:
+        blocks = [attended[row][0]] + [swap(attended[row][mask], "seq", mask) for mask in partners]
+        branched = row_call(
+            functools.partial(branch_kernel, out_parts, seq_size),
+            "branch",
+            [place],
+            row,
+            blocks + [hidden, cotangent, seg_here, modulation],
+            [],
+            out_parts,
+            (model, model),
+            [shape_of(frame_shape, dtype) for dtype in (BF16, F32, F32, BF16, BF16)],
+            branched,
+            2 * frame_count * model * model,
+        )
+    attn, branch, middle, normed_two, grad_fed = branched
     fed, grad_norm_two, grad_bank = mlp(
         place, normed_two.reshape(tokens, model), grad_fed.reshape(tokens, model), bank
     )
-    sum_bank = lax.psum_scatter(
-        grad_bank.reshape((CORES * seq_size,) + grad_bank.shape[2:]),
-        ("core",) + AXES["seq"],
-        scatter_dimension=0,
-        tiled=True,
-    )[0]
-    results = row_call(
-        functools.partial(middle_back_kernel, out_parts, seq_size),
-        "middle_back",
-        [place],
-        row_count,
-        [middle, fed.reshape(frame_shape), grad_norm_two.reshape(frame_shape), cotangent, branch, seg_here, modulation],
-        [],
-        out_parts,
-        (model, model),
-        [
-            shape_of(frame_shape, BF16),
-            shape_of(frame_shape, F32),
-            shape_of(frame_shape, BF16),
-            shape_of((row_count, 4, 8, model), F32),
-        ]
-        + [shape_of((row_count, frame_count, width), BF16)] * seq_size,
-        2 * tokens * model * model,
+    sum_bank = lax.psum_scatter(grad_bank, AXES["dp"], scatter_dimension=0, tiled=True)[0]
+    fed, grad_norm_two = fed.reshape(frame_shape), grad_norm_two.reshape(frame_shape)
+    returned, grad_heads, sums_two = None, [], []
+    for row in row_range:
+        returned = row_call(
+            functools.partial(middle_back_kernel, out_parts, seq_size),
+            "middle_back",
+            [place],
+            row,
+            [middle, fed, grad_norm_two, cotangent, branch, seg_here, modulation],
+            [],
+            out_parts,
+            (model, model),
+            [
+                shape_of(frame_shape, BF16),
+                shape_of(frame_shape, F32),
+                shape_of(frame_shape, BF16),
+                shape_of((1, 4, 8, model), F32),
+            ]
+            + [shape_of((1, frame_count, width), BF16)] * seq_size,
+            returned,
+            2 * frame_count * model * model,
+        )
+        sums_two.append(returned[3])
+        grad_heads.append([returned[4]] + [swap(returned[4 + mask], "seq", mask) for mask in partners])
+    output, grad_middle, grad_branch = returned[:3]
+    keep_out, give_out = weight_grad(
+        place, [grad_branch.reshape(tokens, model)], [attn.reshape(tokens, model)], True, rows, seq_size, False
     )
-    output, grad_middle, grad_branch, sums_two = results[:4]
-    grad_heads = [results[4]] + [swap(results[4 + mask], "seq", mask) for mask in partners]
-    keep_out, give_out = weight_grad(
-        place, [grad_branch.reshape(tokens, model)], attn.reshape(tokens, model), rows, seq_size, True
+    sum_out, _ = send_seq(add_cores(keep_out, give_out))
+
+    grad_qkv, got, partials = [], [], []
+    for row in row_range:
+        grad_qkv.append(
+            attend_back(
+                qkv[row], segments, row, lse[row], cos_table, sin_table, attended[row], grad_heads[row], heads, scale,
+                partials,
+            )
+        )
+        earlier = [sum_out] if row == row_count - 1 else []
+        partials = spread_back(grad_qkv[row], qkv_full, *earlier)
+        got.append([swap(partial, "seq", mask) for mask, partial in zip(partners, partials)])
+    keep_qkv, give_qkv = weight_grad(
+        place,
+        [piece.reshape(frame_count, model) for row_pieces in pieces for piece in row_pieces],
+        grad_qkv,
+        True,
+        rows,
+        1,
+        False,
+        got[0][-1],
     )
-    sum_out = add_cores(keep_out, give_out)
-
-    grad_qkv = attend_back(
-        qkv, segments, lse, cos_table, sin_table, attended, grad_heads, heads, scale
+    sum_pair = jnp.concatenate([sum_out, add_cores(keep_qkv, give_qkv)[0]], -1).astype(BF16)
+    sum_pair = after(sum_pair, sum_bank)
+    sum_pair = after(lax.psum_scatter(sum_pair, "chip", scatter_dimension=0, tiled=True)[0]).astype(F32)
+
+    left, sums_one = None, []
+    for row in row_range:
+        left = row_call(
+            functools.partial(leave_kernel, skip_parts, seq_size),
+            "leave",
+            [place],
+            row,
+            [hidden, grad_middle, grad_qkv[row][0]] + got[row] + [seg_here, modulation],
+            [qkv_full],
+            skip_parts,
+            (2 * model, model),
+            [shape_of(frame_shape, BF16)] * 3 + [shape_of((1, 2, 8, model), F32)],
+            left,
+            6 * frame_count * model * model,
+            [keep_qkv] if row == 0 else [],
+        )
+        sums_one.append(left[3])
+    grad_columns, grad_frames, grad_skip = left[:3]
+    sums_one, sums_two = jnp.concatenate(sums_one), jnp.concatenate(sums_two)
+    grad_modulation = jnp.concatenate([sums_one, sums_two], 1)[:, :, :segs]
+    grad_modulation = grad_modulation.swapaxes(1, 2).reshape(utterances, 6 * model)
+    own = lax.dynamic_slice_in_dim(grad_modulation, seq * mod_columns, mod_columns, 1)
+    for mask in partners:
+        own = own + swap(
+            lax.dynamic_slice_in_dim(grad_modulation, (seq ^ mask) * mod_columns, mod_columns, 1), "seq", mask
+        )
+    keep_skip, give_skip = weight_grad(
+        place,
+        [frames.reshape(tokens, model), skip_in.reshape(tokens, model)],
+        [grad_columns.reshape(tokens, model)],
+        False,
+        w_skip.shape[0],
+        seq_size,
+        True,
+        own,
     )
-    flat_grad = grad_qkv.reshape(seq_size, tokens, 3 * width)
-    got = [
-        swap(partial, "seq", mask) for mask, partial in zip(partners, spread_back(grad_qkv, qkv_full))
-    ]
-    keep_qkv, give_qkv = weight_grad(
-        place, [piece.reshape(tokens, model) for piece in pieces], flat_grad, rows, 1, True, got[0]
-    )
-    sum_out = halve_chips(send_seq(sum_out)).T
-    sum_qkv = halve_chips(add_cores(keep_qkv, give_qkv)[0])
+    sum_skip, _ = send_seq(add_cores(keep_skip, give_skip))
+
+    wide = pick(sum_bank, seq, 0).astype(F32)
+    for mask in partners:
+        wide = wide + swap(pick(sum_bank, seq ^ mask, 0), "seq", mask).astype(F32)
+    sum_up, sum_down = unpack_sums(wide, units, min(512, units))
+    skip_shard = send_chips(sum_skip)
+    sum_out, sum_qkv = sum_pair[:, :width].T, sum_pair[:, width:]
     sum_qkv = jnp.stack(
         [
             sum_qkv[:, :width].reshape(rows, 2, heads, half).swapaxes(1, 2).reshape(rows, heads, head_dim),
@@ -1051,53 +1133,14 @@
         2,
     ).reshape(rows, 3 * width)
 
-    grad_columns, grad_frames, grad_skip, sums_one = row_call(
-        functools.partial(leave_kernel, skip_parts, seq_size),
-        "leave",
-        [place],
-        row_count,
-        [hidden, grad_middle, flat_grad[0].reshape(row_count, frame_count, 3 * width)]
-        + got
-        + [seg_here, modulation],
-        [qkv_full],
-        skip_parts,
-        (2 * model, model),
-        [
-            shape_of(frame_shape, BF16),
-            shape_of(frame_shape, BF16),
-            shape_of(frame_shape, BF16),
-            shape_of((row_count, 2, 8, model), F32),
-        ],
-        6 * tokens * model * model,
-        [keep_qkv],
-    )
-    sum_bank = lax.psum_scatter(after(sum_bank, grad_columns), "chip", scatter_dimension=0, tiled=True)[0]
-    sum_up, sum_down = unpack_sums(sum_bank, units, min(512, units))
-    keep_skip, give_skip = weight_grad(
-        place,
-        [frames.reshape(tokens, model), skip_in.reshape(tokens, model)],
-        grad_columns.reshape(tokens, model),
-        w_skip.shape[0],
-        seq_size,
-        True,
-    )
-    sum_skip = send_chips(send_seq(add_cores(keep_skip, give_skip)))
-
-    grad_modulation = jnp.concatenate([sums_one, sums_two], 1)[:, :, :segs]
-    grad_modulation = grad_modulation.swapaxes(1, 2).reshape(utterances, 6 * model)
-    own = grad_modulation
-    for mask in reversed(bits("seq")):
-        count = own.shape[1] // 2
-        mine = (seq // mask) % 2
-        keep_mod = lax.dynamic_slice_in_dim(own, mine * count, count, 1)
-        own = keep_mod + swap(lax.dynamic_slice_in_dim(own, (1 - mine) * count, count, 1), "seq", mask)
-    own = gather_steps(own, [("dp", [mask]) for mask in bits("dp") + [1]]).reshape(dp_size * utterances, mod_columns)
+    own = gather_steps(own, [("dp", chip_masks()), ("dp", [1])]).reshape(dp_size * utterances, mod_columns)
+    activity = activity_of(small[..., :segs], dp)
     sum_mod = jnp.dot(activity.astype(F32).T, own, precision=lax.Precision.HIGHEST)
     return (
         output,
         grad_frames,
         grad_skip,
-        sum_skip,
+        skip_shard,
         sum_qkv,
         sum_out,
         sum_up,

time: 538 us -> 496 us (0.922)
  waiting for transfers between devices: 235 us -> 116 us
  starting transfers between devices: 62.7 us -> 93.9 us
  Pallas kernels: 185 us -> 204 us
  other arithmetic: 17.4 us -> 31.6 us
  local copies, waits for them, and re-layouts: 12.9 us -> 23.9 us
    ppermute x56 -> x79, waiting for transfers between devices: 230 us -> 110 us  [swap(): lax.ppermute(values, AXES[axis], [(i, i ^ mask) for i in range(axis_size(...]
    ppermute x56 -> x79, starting transfers between devices: 62.4 us -> 93.4 us  [swap(): lax.ppermute(values, AXES[axis], [(i, i ^ mask) for i in range(axis_size(...]
    pallas_call x13 -> x16, Pallas kernels: 87.4 us -> 102 us  [the longest x8 56.3 us: row_call(): pl.pallas_call(kernel, grid=(1,), out_shape=tuple(outs), in_specs=[SMEM_S...]
    reduce_scatter x2, waiting for transfers between devices: 0.01 us -> 6.53 us  [the longest x1 6.53 us: body(): lax.psum_scatter(grad_bank, AXES['dp'], scatter_dimension=0, tiled=True)[0]]
    unnamed x60 -> x115, local copies, waits for them, and re-layouts: 6.71 us -> 12.9 us
    pallas_call x1 -> x2, Pallas kernels: 31.1 us -> 33.9 us  [attend_back(): pl.pallas_call(functools.partial(attend_back_kernel, heads, width, scale)...]
    pallas_call x1 -> x2, Pallas kernels: 25.8 us -> 28 us  [attend(): pl.pallas_call(functools.partial(attend_kernel, heads, width), grid=(rows...]
  transfers between devices with their start and end apart: 59 -> 82, of which waited for: 30 -> 28; matrix products, arithmetic and copies ran while one was open for 5% -> 9% of each run, Pallas kernels for 26% -> 34%
where the time goes in v3:
time: 496 us; the launch traced here: 489 us
  Pallas kernels  204 us (41%)
  waiting for transfers between devices  116 us (23%)
  starting transfers between devices  93.9 us (19%)
  other arithmetic  31.6 us (6%)
  local copies, waits for them, and re-layouts  23.9 us (5%)
  between operations  15.8 us (3%)
    ppermute x79, waiting for transfers between devices, swap(): lax.ppermute(values, AXES[axis], [(i, i ^ mask) for i in range(axis_size(...  110 us
    ppermute x79, starting transfers between devices, swap(): lax.ppermute(values, AXES[axis], [(i, i ^ mask) for i in range(axis_size(...  93.4 us
    pallas_call x8, Pallas kernels, row_call(): pl.pallas_call(kernel, grid=(1,), out_shape=tuple(outs), in_specs=[SMEM_S...  56.3 us
    pallas_call x1, Pallas kernels, mlp(): pl.pallas_call(functools.partial(mlp_kernel, bank, chunk), grid=(seqs * p...  34.7 us
    pallas_call x2, Pallas kernels, attend_back(): pl.pallas_call(functools.partial(attend_back_kernel, heads, width, scale)...  33.9 us
    pallas_call x2, Pallas kernels, attend(): pl.pallas_call(functools.partial(attend_kernel, heads, width), grid=(rows...  28 us
    pallas_call x3, Pallas kernels, weight_grad(): pl.pallas_call(functools.partial(weight_grad_kernel, len(xs), len(ys), by...  21.5 us
    unnamed x115, local copies, waits for them, and re-layouts  12.9 us
  transfers between devices with their start and end apart: 82, of which 28 were waited for; matrix products, arithmetic and copies ran while one was open for 9% of the time, Pallas kernels for 34%

profile of v3, /device:TPU:0, one launch (start us, length us, event | category | flops | bytes accessed | tf_op | source)
XLA Modules:
  0.0 488.5 jit_solution(14760729485564423479)
XLA Ops:
  8.7 3.0 collective-permute-start.3
  11.8 2.6 collective-permute-start.4
  15.3 3.5 collective-permute-start.14
  23.3 3.1 collective-permute-start.8
  26.4 2.9 collective-permute-done.15
  29.4 2.5 collective-permute-start.18
  46.0 8.1 %collective-permute-done.1 = bf16[2,128,768]{2,1,0:T(8,128)(2,1)S(1)} collective-permute-done((bf16[2,128,768]{2,1,0:T(8,128)(2,1)S(1)}, bf16[2,128,768]{2,1,0:T(8,128)(2,1)S(1)}, u32[]{:S(2)}, u32[]{:S(2)}) %collective-permute-start.1) | collective-permute-done | bytes 393248 | tf_op jit(solution)/shard_map/ppermute | solution.py:41
  65.4 10.3 %collective-permute-done.16.rest_1_.rest_7_ = bf16[4,256,256]{2,1,0:T(8,128)(2,1)S(1)} collective-permute-done((bf16[4,256,256]{2,1,0:T(8,128)(2,1)S(1)}, bf16[4,256,256]{2,1,0:T(8,128)(2,1)S(1)}, u32[]{:S(2)}, u32[]{:S(2)}) %collective-permute-start.16) | collective-permute-done | bytes 524320 | tf_op jit(solution)/shard_map/ppermute | solution.py:41
  83.9 6.4 %enter.2 = (f32[2,256,1024]{2,1,0:T(8,128)}, bf16[1,256,1024]{2,1,0:T(8,128)(2,1)}) custom-call(s32[2]{0:T(128)} %pad_add_fusion.place_ref, f32[2,3]{1,0:T(2,128)} %subtract_multiply_fusion.coef_ref, bf16[2,256,1024]{2,1,0:T(8,128)(2,1)} %frames_ref.3, bf16[2,256,1024]{2,1,0:T(8,128)(2,1)} %skip_ref.3, bf16[2,256,1024]{2,1,0:T(8,128)(2,1)} %cond_ref.3, ...), custom_call_target="tpu_custom_call" | custom-call | flops 1073741824 | bytes 7489536 | tf_op jit(solution)/shard_map/enter/pallas_call | solution.py:773
  94.0 6.5 %enter.3 = (f32[2,256,1024]{2,1,0:T(8,128)}, bf16[1,256,1024]{2,1,0:T(8,128)(2,1)}) custom-call(s32[2]{0:T(128)} %pad_add_fusion.place_ref, f32[2,3]{1,0:T(2,128)} %subtract_multiply_fusion.coef_ref, bf16[2,256,1024]{2,1,0:T(8,128)(2,1)} %frames_ref.3, bf16[2,256,1024]{2,1,0:T(8,128)(2,1)} %skip_ref.3, ...), custom_call_target="tpu_custom_call", output_to_operand_aliasing={{0}: (15, {})} | custom-call | flops 1073741824 | bytes 7489536 | tf_op jit(solution)/shard_map/enter/pallas_call | solution.py:773
  101.8 15.3 %collective-permute-done.29.refs_1_.rest_3_ = bf16[1,256,1024]{2,1,0:T(8,128)(2,1)S(1)} collective-permute-done((bf16[1,256,1024]{2,1,0:T(8,128)(2,1)}, bf16[1,256,1024]{2,1,0:T(8,128)(2,1)S(1)}, u32[]{:S(2)}, u32[]{:S(2)}) %collective-permute-start.29) | collective-permute-done | bytes 524320 | tf_op jit(solution)/shard_map/ppermute | solution.py:41
  117.9 3.2 multiply_sine_fusion
  121.7 3.4 assemble.1.w_ref.weight_ref.rest_5_
  125.1 2.4 collective-permute-done.40.rest_1_
  132.5 6.1 %project.3.qkv_ref = bf16[4,1,256,768]{3,2,1,0:T(8,128)(2,1)} custom-call(bf16[1024,768]{1,0:T(8,128)(2,1)} %assemble.1.w_ref.weight_ref.rest_5_, f32[4,256,128]{2,1,0:T(8,128)} %get-tuple-element.193.cos_ref, f32[4,256,128]{2,1,0:T(8,128)} %get-tuple-element.192.sin_ref, bf16[1,256,1024]{2,1,0:T(8,128)(2,1)} %get-tuple-element.81.rest_0_, ...), custom_call_target="tpu_custom_call" | custom-call | flops 1610612736 | bytes 3670016 | tf_op jit(solution)/shard_map/project/pallas_call | solution.py:344
  142.3 13.9 %attend.3 = (bf16[1,256,256]{2,1,0:T(8,128)(2,1)}, bf16[1,256,256]{2,1,0:T(8,128)(2,1)}, bf16[1,256,256]{2,1,0:T(8,128)(2,1)}, bf16[1,256,256]{2,1,0:T(8,128)(2,1)}, f32[1,4,4,256]{3,2,1,0:T(4,128)}) custom-call(bf16[4,1,256,768]{3,2,1,0:T(8,128)(2,1)} %project.3.qkv_ref, f32[2,4,256]{2,1,0:T(4,128)} %bitcast.206), custom_call_target="tpu_custom_call" | custom-call | flops 4294967296 | bytes 2097152 | tf_op jit(solution)/shard_map/attend/pallas_call | solution.py:502
  157.7 6.0 %collective-permute-done.25.rest_3_ = bf16[1,256,1024]{2,1,0:T(8,128)(2,1)} collective-permute-done((bf16[1,256,1024]{2,1,0:T(8,128)(2,1)S(1)}, bf16[1,256,1024]{2,1,0:T(8,128)(2,1)}, u32[]{:S(2)}, u32[]{:S(2)}) %collective-permute-start.25) | collective-permute-done | bytes 524320 | tf_op jit(solution)/shard_map/ppermute | solution.py:41
  164.2 6.0 %project.2.qkv_ref = bf16[4,1,256,768]{3,2,1,0:T(8,128)(2,1)} custom-call(bf16[1024,768]{1,0:T(8,128)(2,1)} %assemble.1.w_ref.weight_ref.rest_5_, f32[4,256,128]{2,1,0:T(8,128)} %get-tuple-element.193.cos_ref, f32[4,256,128]{2,1,0:T(8,128)} %get-tuple-element.192.sin_ref, bf16[1,256,1024]{2,1,0:T(8,128)(2,1)} %get-tuple-element.75.rest_0_, ...), custom_call_target="tpu_custom_call" | custom-call | flops 1610612736 | bytes 3670016 | tf_op jit(solution)/shard_map/project/pallas_call | solution.py:344
  170.2 20.2 %collective-permute-done.42.rest_1_ = bf16[1,256,256]{2,1,0:T(8,128)(2,1)S(1)} collective-permute-done((bf16[1,256,256]{2,1,0:T(8,128)(2,1)}, bf16[1,256,256]{2,1,0:T(8,128)(2,1)S(1)}, u32[]{:S(2)}, u32[]{:S(2)}) %collective-permute-start.42) | collective-permute-done | bytes 131104 | tf_op jit(solution)/shard_map/ppermute | solution.py:41
  193.0 14.1 %attend.2 = (bf16[1,256,256]{2,1,0:T(8,128)(2,1)}, bf16[1,256,256]{2,1,0:T(8,128)(2,1)}, bf16[1,256,256]{2,1,0:T(8,128)(2,1)}, bf16[1,256,256]{2,1,0:T(8,128)(2,1)}, f32[1,4,4,256]{3,2,1,0:T(4,128)}) custom-call(bf16[4,1,256,768]{3,2,1,0:T(8,128)(2,1)} %project.2.qkv_ref, f32[2,4,256]{2,1,0:T(4,128)} %bitcast.207), custom_call_target="tpu_custom_call" | custom-call | flops 4294967296 | bytes 2097152 | tf_op jit(solution)/shard_map/attend/pallas_call | solution.py:502
  211.5 6.2 %branch.2 = (bf16[2,256,1024]{2,1,0:T(8,128)(2,1)}, f32[2,256,1024]{2,1,0:T(8,128)}, f32[2,256,1024]{2,1,0:T(8,128)}, bf16[2,256,1024]{2,1,0:T(8,128)(2,1)}, bf16[2,256,1024]{2,1,0:T(8,128)(2,1)}) custom-call(s32[2]{0:T(128)} %pad_add_fusion.place_ref, bf16[1,256,256]{2,1,0:T(8,128)(2,1)} %get-tuple-element.82.rest_0_, bf16[1,256,256]{2,1,0:T(8,128)(2,1)} %copy-done.39, ...), custom_call_target="tpu_custom_call" | custom-call | flops 536870912 | bytes 5916672 | tf_op jit(solution)/shard_map/branch/pallas_call | solution.py:773
  218.4 6.1 %branch.3 = (bf16[2,256,1024]{2,1,0:T(8,128)(2,1)}, f32[2,256,1024]{2,1,0:T(8,128)}, f32[2,256,1024]{2,1,0:T(8,128)}, bf16[2,256,1024]{2,1,0:T(8,128)(2,1)}, bf16[2,256,1024]{2,1,0:T(8,128)(2,1)}) custom-call(s32[2]{0:T(128)} %pad_add_fusion.place_ref, ...), custom_call_target="tpu_custom_call", output_to_operand_aliasing={{0}: (17, {}), {1}: (18, {}), {2}: (19, {}), {3}: (20, {}),... | custom-call | flops 536870912 | bytes 5916672 | tf_op jit(solution)/shard_map/branch/pallas_call | solution.py:773
  224.5 34.7 %mlp.1 = (f32[512,1024]{1,0:T(8,128)}, f32[512,1024]{1,0:T(8,128)}, bf16[8,4,128,2048]{3,2,1,0:T(8,128)(2,1)}) custom-call(s32[2]{0:T(128)} %pad_add_fusion.place_ref, bf16[512,1024]{1,0:T(8,128)(2,1)} %bitcast.169, bf16[512,1024]{1,0:T(8,128)(2,1)} %bitcast.170, bf16[8,4,128,2048]{3,2,1,0:T(8,128)(2,1)} %bitcast.220), custom_call_target="tpu_custom_call" | custom-call | flops 25769803776 | bytes 39845888 | tf_op jit(solution)/shard_map/mlp/pallas_call | solution.py:692
  259.7 7.7 %middle_back.2 = (bf16[2,256,1024]{2,1,0:T(8,128)(2,1)}, f32[2,256,1024]{2,1,0:T(8,128)}, bf16[2,256,1024]{2,1,0:T(8,128)(2,1)}, f32[1,4,8,1024]{3,2,1,0:T(8,128...) custom-call(s32[2]{0:T(128)} %pad_add_fusion.place_ref, ...), custom_call_target="tpu_custom_call" | custom-call | flops 536870912 | bytes 11683840 | tf_op jit(solution)/shard_map/middle_back/pallas_call | solution.py:773
  270.9 7.7 %middle_back.3 = (bf16[2,256,1024]{2,1,0:T(8,128)(2,1)}, f32[2,256,1024]{2,1,0:T(8,128)}, bf16[2,256,1024]{2,1,0:T(8,128)(2,1)}, f32[1,4,8,1024]{3,2,1,0:T(8,128...) custom-call(s32[2]{0:T(128)} %pad_add_fusion.place_ref, ...), custom_call_target="tpu_custom_call", output_to_operand_aliasing={{0}: (16, {}), {1}: (17, {}), {2}: (18, {})} | custom-call | flops 536870912 | bytes 11683840 | tf_op jit(solution)/shard_map/middle_back/pallas_call | solution.py:773
  280.8 5.1 %weight_grad.3 = (bf16[4,4,128,256]{3,2,1,0:T(8,128)(2,1)}, bf16[4,4,128,256]{3,2,1,0:T(8,128)(2,1)}) custom-call(s32[2]{0:T(128)} %pad_add_fusion.place_ref, bf16[512,1024]{1,0:T(8,128)(2,1)} %bitcast.167, bf16[512,1024]{1,0:T(8,128)(2,1)} %bitcast.168), custom_call_target="tpu_custom_call" | custom-call | flops 1073741824 | bytes 5242880 | tf_op jit(solution)/shard_map/weight_grad/pallas_call | solution.py:303
  288.0 16.9 %attend_back.2.grad_ref.rest_8_ = bf16[4,1,256,768]{3,2,1,0:T(8,128)(2,1)} custom-call(bf16[4,1,256,768]{3,2,1,0:T(8,128)(2,1)} %project.3.qkv_ref, f32[2,4,256]{2,1,0:T(4,128)} %bitcast.208, f32[1,4,4,256]{3,2,1,0:T(4,128)} %get-tuple-element.107.lse_ref, f32[4,256,128]{2,1,0:T(8,128)} %get-tuple-element.193.cos_ref, ...), custom_call_target="tpu_custom_call" | custom-call | flops 10737418240 | bytes 4194304 | tf_op jit(solution)/shard_map/attend_back/pallas_call | solution.py:599
  305.0 5.1 %spread_back.2 = (bf16[1,256,1024]{2,1,0:T(8,128)(2,1)}, bf16[1,256,1024]{2,1,0:T(8,128)(2,1)}, bf16[1,256,1024]{2,1,0:T(8,128)(2,1)}) custom-call(bf16[4,1,256,768]{3,2,1,0:T(8,128)(2,1)} %attend_back.2.grad_ref.rest_8_, bf16[1024,768]{1,0:T(8,128)(2,1)} %assemble.1.w_ref.weight_ref.rest_5_), custom_call_target="tpu_custom_call" | custom-call | flops 1207959552 | bytes 3670016 | tf_op jit(solution)/shard_map/spread_back/pallas_call | solution.py:432
  318.5 16.9 %attend_back.3.grad_ref.rest_9_ = bf16[4,1,256,768]{3,2,1,0:T(8,128)(2,1)} custom-call(bf16[4,1,256,768]{3,2,1,0:T(8,128)(2,1)} %project.2.qkv_ref, f32[2,4,256]{2,1,0:T(4,128)} %bitcast.209, f32[1,4,4,256]{3,2,1,0:T(4,128)} %get-tuple-element.102.lse_ref, f32[4,256,128]{2,1,0:T(8,128)} %get-tuple-element.193.cos_ref, ...), custom_call_target="tpu_custom_call" | custom-call | flops 10737418240 | bytes 4194304 | tf_op jit(solution)/shard_map/attend_back/pallas_call | solution.py:599
  337.2 4.8 collective-permute-done.52
  343.3 4.9 %collective-permute-done.54 = bf16[4,128,256]{2,1,0:T(8,128)(2,1)} collective-permute-done((bf16[4,128,256]{2,1,0:T(8,128)(2,1)S(1)}, bf16[4,128,256]{2,1,0:T(8,128)(2,1)}, u32[]{:S(2)}, u32[]{:S(2)}) %collective-permute-start.54) | collective-permute-done | bytes 262176 | tf_op jit(solution)/shard_map/ppermute | solution.py:41
  350.3 5.0 %spread_back.3 = (bf16[1,256,1024]{2,1,0:T(8,128)(2,1)}, bf16[1,256,1024]{2,1,0:T(8,128)(2,1)}, bf16[1,256,1024]{2,1,0:T(8,128)(2,1)}) custom-call(bf16[4,1,256,768]{3,2,1,0:T(8,128)(2,1)} %attend_back.3.grad_ref.rest_9_, bf16[1024,768]{1,0:T(8,128)(2,1)} %assemble.1.w_ref.weight_ref.rest_5_, f32[4,128,256]{2,1,0:T(8,128)} %get-tuple-element.158.rest_0_), custom_call_target="tpu_custom_call" | custom-call | flops 1207959552 | bytes 3670016 | tf_op jit(solution)/shard_map/spread_back/pallas_call | solution.py:432
  360.6 9.5 %weight_grad.4 = (bf16[1,4,128,768]{3,2,1,0:T(8,128)(2,1)}, bf16[1,4,128,768]{3,2,1,0:T(8,128)(2,1)}) custom-call(s32[2]{0:T(128)} %pad_add_fusion.place_ref, bf16[256,1024]{1,0:T(8,128)(2,1)} %bitcast.180, bf16[256,1024]{1,0:T(8,128)(2,1)} %bitcast.181, bf16[256,1024]{1,0:T(8,128)(2,1)} %bitcast.182, bf16[256,1024]{1,0:T(8,128)(2,1)} %bitcast.163, ...), custom_call_target="tpu_custom_call" | custom-call | flops 3221225472 | bytes 7340032 | tf_op jit(solution)/shard_map/weight_grad/pallas_call | solution.py:303
  370.9 8.0 %leave.2 = (bf16[2,256,1024]{2,1,0:T(8,128)(2,1)}, bf16[2,256,1024]{2,1,0:T(8,128)(2,1)}, bf16[2,256,1024]{2,1,0:T(8,128)(2,1)}, f32[1,2,8,1024]{3,2,1,0:T(8,128)}) custom-call(s32[2]{0:T(128)} %pad_add_fusion.place_ref, f32[2,256,1024]{2,1,0:T(8,128)} %get-tuple-element.80.rest_4_.hidden_ref, f32[2,256,1024]{2,1,0:T(8,128)} %get-tuple-element.101.grad_middle_ref, ...), custom_call_target="tpu_custom_call" | custom-call | flops 1610612736 | bytes 10504192 | tf_op jit(solution)/shard_map/leave/pallas_call | solution.py:773
  378.9 2.8 collective-permute-done.56.rest_1_
  382.7 7.9 %leave.3 = (bf16[2,256,1024]{2,1,0:T(8,128)(2,1)}, bf16[2,256,1024]{2,1,0:T(8,128)(2,1)}, bf16[2,256,1024]{2,1,0:T(8,128)(2,1)}, f32[1,2,8,1024]{3,2,1,0:T(8,128)}) custom-call(s32[2]{0:T(128)} %pad_add_fusion.place_ref, f32[2,256,1024]{2,1,0:T(8,128)} %get-tuple-element.80.rest_4_.hidden_ref, ...), custom_call_target="tpu_custom_call", output_to_operand_aliasing={{0}: (18, {}), {1}: (19, {}), {2}: (20, {})} | custom-call | flops 1610612736 | bytes 10504192 | tf_op jit(solution)/shard_map/leave/pallas_call | solution.py:773
  395.9 2.4 collective-permute-done.62
  399.8 6.9 %weight_grad.5 = (bf16[4,4,256,256]{3,2,1,0:T(8,128)(2,1)}, bf16[4,4,256,256]{3,2,1,0:T(8,128)(2,1)}) custom-call(s32[2]{0:T(128)} %pad_add_fusion.place_ref, bf16[512,1024]{1,0:T(8,128)(2,1)} %bitcast.160, bf16[512,1024]{1,0:T(8,128)(2,1)} %bitcast.161, bf16[512,1024]{1,0:T(8,128)(2,1)} %bitcast.166, f32[6,1536]{1,0:T(8,128)} %add_add_fusion.rest_3_), custom_call_target="tpu_custom_call" | custom-call | flops 2147483648 | bytes 10485760 | tf_op jit(solution)/shard_map/weight_grad/pallas_call | solution.py:303
  411.1 4.2 convert_add_fusion
  419.2 2.7 collective-permute-start.76
  424.5 6.5 %reduce-scatter.3.cloned.1.call-done = bf16[1,4,128,2048]{3,2,1,0:T(8,128)(2,1)} async-done(((bf16[8,4,128,2048]{3,2,1,0:T(8,128)(2,1)}), bf16[1,4,128,2048]{3,2,1,0:T(8,128)(2,1)}) %reduce-scatter.3.cloned.1.call-update) | async-done | bytes 2097168 | tf_op jit(solution)/shard_map/reduce_scatter | solution.py:1027
  432.0 9.7 %collective-permute-done.67 = bf16[4,256,256]{2,1,0:T(8,128)(2,1)S(1)} collective-permute-done((bf16[4,256,256]{2,1,0:T(8,128)(2,1)S(1)}, bf16[4,256,256]{2,1,0:T(8,128)(2,1)S(1)}, u32[]{:S(2)}, u32[]{:S(2)}) %collective-permute-start.67) | collective-permute-done | bytes 524320 | tf_op jit(solution)/shard_map/ppermute | solution.py:41
  452.5 2.3 collective-permute-start.69
  454.8 3.4 collective-permute-done.68
  458.2 5.4 %collective-permute-start.70 = (bf16[256,256]{1,0:T(8,128)(2,1)}, bf16[256,256]{1,0:T(8,128)(2,1)S(1)}, u32[]{:S(2)}, u32[]{:S(2)}) collective-permute-start(bf16[256,256]{1,0:T(8,128)(2,1)} %get-tuple-element.175), channel_id=1, source_target_pairs={{0,24},{4,28},{8,16},{12,20},{16,8},{20,12},{24,0},{28,4},{1,25},{... | collective-permute-start | bytes 393224 | tf_op jit(solution)/shard_map/ppermute | solution.py:41
  463.6 2.4 fusion.16
  472.7 2.7 fusion.4.sums_ref
  475.4 2.3 unpack_sums.1
  (344 shorter events, 132.9 us)
Async XLA Ops:
  7.2 217.3 %all-gather.3.cloned.1.call-start = ((), (), s32[]{:S(2)}) async-start(), calls=%async_computation.4 | async-start | bytes 17301504 | tf_op jit(solution)/shard_map/all_gather | solution.py:968
  29.4 25.7 %collective-permute-start.18 = (bf16[4,256,256]{2,1,0:T(8,128)(2,1)S(1)}, bf16[4,256,256]{2,1,0:T(8,128)(2,1)S(1)}, u32[]{:S(2)}, u32[]{:S(2)}) collective-permute-start(bf16[4,256,256]{2,1,0:T(8,128)(2,1)S(1)} %pad_maximum_fusion.2.rest_0_.rest_6_), channel_id=1, source_target_pairs={{0,3},{1,2},{2,1},{3,0},{4,7},{5,6},{6,5},{7,4},{8,11},{9,10},{10,... | collective-permute-start | bytes 1572872 | tf_op jit(solution)/shard_map/ppermute | solution.py:41
  35.4 18.7 %collective-permute-start.1 = (bf16[2,128,768]{2,1,0:T(8,128)(2,1)S(1)}, bf16[2,128,768]{2,1,0:T(8,128)(2,1)S(1)}, u32[]{:S(2)}, u32[]{:S(2)}) collective-permute-start(bf16[2,128,768]{2,1,0:T(8,128)(2,1)S(1)} %pad_maximum_fusion.3), channel_id=1, source_target_pairs={{0,16},{4,20},{8,24},{12,28},{16,0},{20,4},{24,8},{28,12},{1,17},{... | collective-permute-start | bytes 1179656 | tf_op jit(solution)/shard_map/ppermute | solution.py:41
  57.9 373.1 %reduce-scatter.3.cloned.1.call-start = ((), (), s32[]{:S(2)}) async-start(), calls=%async_computation.2 | async-start | bytes 18874368 | tf_op jit(solution)/shard_map/reduce_scatter | solution.py:1027
  58.0 17.7 %collective-permute-start.16 = (bf16[4,256,256]{2,1,0:T(8,128)(2,1)S(1)}, bf16[4,256,256]{2,1,0:T(8,128)(2,1)S(1)}, u32[]{:S(2)}, u32[]{:S(2)}) collective-permute-start(bf16[4,256,256]{2,1,0:T(8,128)(2,1)S(1)} %pad_maximum_fusion.2.rest_0_.rest_6_), channel_id=1, source_target_pairs={{0,1},{1,0},{2,3},{3,2},{4,5},{5,4},{6,7},{7,6},{8,9},{9,8},{10,11... | collective-permute-start | bytes 1572872 | tf_op jit(solution)/shard_map/ppermute | solution.py:41
  59.5 17.3 %collective-permute-start.17 = (bf16[4,256,256]{2,1,0:T(8,128)(2,1)S(1)}, bf16[4,256,256]{2,1,0:T(8,128)(2,1)S(1)}, u32[]{:S(2)}, u32[]{:S(2)}) collective-permute-start(bf16[4,256,256]{2,1,0:T(8,128)(2,1)S(1)} %pad_maximum_fusion.2.rest_0_.rest_6_), channel_id=1, source_target_pairs={{0,2},{1,3},{2,0},{3,1},{4,6},{5,7},{6,4},{7,5},{8,10},{9,11},{10,... | collective-permute-start | bytes 1572872 | tf_op jit(solution)/shard_map/ppermute | solution.py:41
  64.8 18.0 %collective-permute-start.19 = (bf16[4,256,256]{2,1,0:T(8,128)(2,1)S(1)}, bf16[4,256,256]{2,1,0:T(8,128)(2,1)S(1)}, u32[]{:S(2)}, u32[]{:S(2)}) collective-permute-start(bf16[4,256,256]{2,1,0:T(8,128)(2,1)S(1)} %pad_maximum_fusion.2.rest_0_.rest_6_), channel_id=1, source_target_pairs={{0,4},{4,0},{8,12},{12,8},{16,20},{20,16},{24,28},{28,24},{1,5},{5... | collective-permute-start | bytes 1572872 | tf_op jit(solution)/shard_map/ppermute | solution.py:41
  65.0 17.8 %collective-permute-start.22 = (bf16[4,256,256]{2,1,0:T(8,128)(2,1)}, bf16[4,256,256]{2,1,0:T(8,128)(2,1)S(1)}, u32[]{:S(2)}, u32[]{:S(2)}) collective-permute-start(bf16[4,256,256]{2,1,0:T(8,128)(2,1)} %copy-done.1), channel_id=1, source_target_pairs={{0,4},{4,0},{8,12},{12,8},{16,20},{20,16},{24,28},{28,24},{1,5},{5... | collective-permute-start | bytes 1572872 | tf_op jit(solution)/shard_map/ppermute | solution.py:41
  82.3 38.8 %collective-permute-start.2 = (bf16[4,128,768]{2,1,0:T(8,128)(2,1)}, bf16[4,128,768]{2,1,0:T(8,128)(2,1)}, u32[]{:S(2)}, u32[]{:S(2)}) collective-permute-start(bf16[4,128,768]{2,1,0:T(8,128)(2,1)} %pad_maximum_fusion.1.rest_0_.refs_4_), channel_id=1, source_target_pairs={{0,4},{4,0},{8,12},{12,8},{16,20},{20,16},{24,28},{28,24},{1,5},{5... | collective-permute-start | bytes 2359304 | tf_op jit(solution)/shard_map/ppermute | solution.py:41
  90.3 26.8 %collective-permute-start.29 = (bf16[1,256,1024]{2,1,0:T(8,128)(2,1)}, bf16[1,256,1024]{2,1,0:T(8,128)(2,1)S(1)}, u32[]{:S(2)}, u32[]{:S(2)}) collective-permute-start(bf16[1,256,1024]{2,1,0:T(8,128)(2,1)} %get-tuple-element.81.rest_0_), channel_id=1, source_target_pairs={{0,3},{1,2},{2,1},{3,0},{4,7},{5,6},{6,5},{7,4},{8,11},{9,10},{10,... | collective-permute-start | bytes 1572872 | tf_op jit(solution)/shard_map/ppermute | solution.py:41
  91.9 35.5 %collective-permute-start.40 = (bf16[1,256,1024]{2,1,0:T(8,128)(2,1)}, bf16[1,256,1024]{2,1,0:T(8,128)(2,1)S(1)}, u32[]{:S(2)}, u32[]{:S(2)}) collective-permute-start(bf16[1,256,1024]{2,1,0:T(8,128)(2,1)} %get-tuple-element.81.rest_0_), channel_id=1, source_target_pairs={{0,1},{1,0},{2,3},{3,2},{4,5},{5,4},{6,7},{7,6},{8,9},{9,8},{10,11... | collective-permute-start | bytes 1572872 | tf_op jit(solution)/shard_map/ppermute | solution.py:41
  92.9 35.9 %collective-permute-start.41 = (bf16[1,256,1024]{2,1,0:T(8,128)(2,1)}, bf16[1,256,1024]{2,1,0:T(8,128)(2,1)S(1)}, u32[]{:S(2)}, u32[]{:S(2)}) collective-permute-start(bf16[1,256,1024]{2,1,0:T(8,128)(2,1)} %get-tuple-element.81.rest_0_), channel_id=1, source_target_pairs={{0,2},{1,3},{2,0},{3,1},{4,6},{5,7},{6,4},{7,5},{8,10},{9,11},{10,... | collective-permute-start | bytes 1572872 | tf_op jit(solution)/shard_map/ppermute | solution.py:41
  100.5 40.7 %collective-permute-start.23 = (bf16[1,256,1024]{2,1,0:T(8,128)(2,1)}, bf16[1,256,1024]{2,1,0:T(8,128)(2,1)S(1)}, u32[]{:S(2)}, u32[]{:S(2)}) collective-permute-start(bf16[1,256,1024]{2,1,0:T(8,128)(2,1)} %get-tuple-element.75.rest_0_), channel_id=1, source_target_pairs={{0,1},{1,0},{2,3},{3,2},{4,5},{5,4},{6,7},{7,6},{8,9},{9,8},{10,11... | collective-permute-start | bytes 1572872 | tf_op jit(solution)/shard_map/ppermute | solution.py:41
  121.1 35.1 %collective-permute-start.24 = (bf16[1,256,1024]{2,1,0:T(8,128)(2,1)}, bf16[1,256,1024]{2,1,0:T(8,128)(2,1)}, u32[]{:S(2)}, u32[]{:S(2)}) collective-permute-start(bf16[1,256,1024]{2,1,0:T(8,128)(2,1)} %get-tuple-element.75.rest_0_), channel_id=1, source_target_pairs={{0,2},{1,3},{2,0},{3,1},{4,6},{5,7},{6,4},{7,5},{8,10},{9,11},{10,... | collective-permute-start | bytes 1572872 | tf_op jit(solution)/shard_map/ppermute | solution.py:41
  127.4 36.3 %collective-permute-start.25 = (bf16[1,256,1024]{2,1,0:T(8,128)(2,1)S(1)}, bf16[1,256,1024]{2,1,0:T(8,128)(2,1)}, u32[]{:S(2)}, u32[]{:S(2)}) collective-permute-start(bf16[1,256,1024]{2,1,0:T(8,128)(2,1)S(1)} %copy-done.24), channel_id=1, source_target_pairs={{0,3},{1,2},{2,1},{3,0},{4,7},{5,6},{6,5},{7,4},{8,11},{9,10},{10,... | collective-permute-start | bytes 1572872 | tf_op jit(solution)/shard_map/ppermute | solution.py:41
  138.7 53.2 %collective-permute-start.33 = (bf16[4,128,256]{2,1,0:T(8,128)(2,1)S(1)}, bf16[4,128,256]{2,1,0:T(8,128)(2,1)S(1)}, u32[]{:S(2)}, u32[]{:S(2)}) collective-permute-start(bf16[4,128,256]{2,1,0:T(8,128)(2,1)S(1)} %pad_maximum_fusion.6.rest_8_.rest_0_), channel_id=1, source_target_pairs={{0,1},{1,0},{2,3},{3,2},{4,5},{5,4},{6,7},{7,6},{8,9},{9,8},{10,11... | collective-permute-start | bytes 786440 | tf_op jit(solution)/shard_map/ppermute | solution.py:41
  140.2 52.2 %collective-permute-start.34 = (bf16[4,128,256]{2,1,0:T(8,128)(2,1)S(1)}, bf16[4,128,256]{2,1,0:T(8,128)(2,1)S(1)}, u32[]{:S(2)}, u32[]{:S(2)}) collective-permute-start(bf16[4,128,256]{2,1,0:T(8,128)(2,1)S(1)} %pad_maximum_fusion.6.rest_8_.rest_0_), channel_id=1, source_target_pairs={{0,2},{1,3},{2,0},{3,1},{4,6},{5,7},{6,4},{7,5},{8,10},{9,11},{10,... | collective-permute-start | bytes 786440 | tf_op jit(solution)/shard_map/ppermute | solution.py:41
  141.2 51.3 %collective-permute-start.35 = (bf16[4,128,256]{2,1,0:T(8,128)(2,1)S(1)}, bf16[4,128,256]{2,1,0:T(8,128)(2,1)S(1)}, u32[]{:S(2)}, u32[]{:S(2)}) collective-permute-start(bf16[4,128,256]{2,1,0:T(8,128)(2,1)S(1)} %pad_maximum_fusion.6.rest_8_.rest_0_), channel_id=1, source_target_pairs={{0,3},{1,2},{2,1},{3,0},{4,7},{5,6},{6,5},{7,4},{8,11},{9,10},{10,... | collective-permute-start | bytes 786440 | tf_op jit(solution)/shard_map/ppermute | solution.py:41
  156.2 34.2 %collective-permute-start.42 = (bf16[1,256,256]{2,1,0:T(8,128)(2,1)}, bf16[1,256,256]{2,1,0:T(8,128)(2,1)S(1)}, u32[]{:S(2)}, u32[]{:S(2)}) collective-permute-start(bf16[1,256,256]{2,1,0:T(8,128)(2,1)} %get-tuple-element.83.rest_1_), channel_id=1, source_target_pairs={{0,1},{1,0},{2,3},{3,2},{4,5},{5,4},{6,7},{7,6},{8,9},{9,8},{10,11... | collective-permute-start | bytes 393224 | tf_op jit(solution)/shard_map/ppermute | solution.py:41
  163.7 28.2 %collective-permute-start.43 = (bf16[1,256,256]{2,1,0:T(8,128)(2,1)}, bf16[1,256,256]{2,1,0:T(8,128)(2,1)S(1)}, u32[]{:S(2)}, u32[]{:S(2)}) collective-permute-start(bf16[1,256,256]{2,1,0:T(8,128)(2,1)} %get-tuple-element.84.rest_2_), channel_id=1, source_target_pairs={{0,2},{1,3},{2,0},{3,1},{4,6},{5,7},{6,4},{7,5},{8,10},{9,11},{10,... | collective-permute-start | bytes 393224 | tf_op jit(solution)/shard_map/ppermute | solution.py:41
  190.4 16.7 %collective-permute-start.44 = (bf16[1,256,256]{2,1,0:T(8,128)(2,1)S(1)}, bf16[1,256,256]{2,1,0:T(8,128)(2,1)S(1)}, u32[]{:S(2)}, u32[]{:S(2)}) collective-permute-start(bf16[1,256,256]{2,1,0:T(8,128)(2,1)S(1)} %copy-done.48), channel_id=1, source_target_pairs={{0,3},{1,2},{2,1},{3,0},{4,7},{5,6},{6,5},{7,4},{8,11},{9,10},{10,... | collective-permute-start | bytes 393224 | tf_op jit(solution)/shard_map/ppermute | solution.py:41
  191.9 17.2 %collective-permute-start.36 = (bf16[4,128,256]{2,1,0:T(8,128)(2,1)S(1)}, bf16[4,128,256]{2,1,0:T(8,128)(2,1)S(1)}, u32[]{:S(2)}, u32[]{:S(2)}) collective-permute-start(bf16[4,128,256]{2,1,0:T(8,128)(2,1)S(1)} %pad_maximum_fusion.6.rest_8_.rest_0_), channel_id=1, source_target_pairs={{0,4},{4,0},{8,12},{12,8},{16,20},{20,16},{24,28},{28,24},{1,5},{5... | collective-permute-start | bytes 786440 | tf_op jit(solution)/shard_map/ppermute | solution.py:41
  192.0 17.3 %collective-permute-start.37 = (bf16[4,128,256]{2,1,0:T(8,128)(2,1)S(1)}, bf16[4,128,256]{2,1,0:T(8,128)(2,1)S(1)}, u32[]{:S(2)}, u32[]{:S(2)}) collective-permute-start(bf16[4,128,256]{2,1,0:T(8,128)(2,1)S(1)} %collective-permute-done.33.rest_9_.rest_1_), channel_id=1, source_target_pairs={{0,4},{4,0},{8,12},{12,8},{16,20},{20,16},{24,28},{28,24},{1,5},{5... | collective-permute-start | bytes 786440 | tf_op jit(solution)/shard_map/ppermute | solution.py:41
  192.4 18.2 %collective-permute-start.38 = (bf16[4,128,256]{2,1,0:T(8,128)(2,1)S(1)}, bf16[4,128,256]{2,1,0:T(8,128)(2,1)S(1)}, u32[]{:S(2)}, u32[]{:S(2)}) collective-permute-start(bf16[4,128,256]{2,1,0:T(8,128)(2,1)S(1)} %collective-permute-done.34.rest_10_.rest_2_), channel_id=1, source_target_pairs={{0,4},{4,0},{8,12},{12,8},{16,20},{20,16},{24,28},{28,24},{1,5},{5... | collective-permute-start | bytes 786440 | tf_op jit(solution)/shard_map/ppermute | solution.py:41
  192.5 18.1 %collective-permute-start.39 = (bf16[4,128,256]{2,1,0:T(8,128)(2,1)S(1)}, bf16[4,128,256]{2,1,0:T(8,128)(2,1)S(1)}, u32[]{:S(2)}, u32[]{:S(2)}) collective-permute-start(bf16[4,128,256]{2,1,0:T(8,128)(2,1)S(1)} %collective-permute-done.35.rest_11_.rest_3_), channel_id=1, source_target_pairs={{0,4},{4,0},{8,12},{12,8},{16,20},{20,16},{24,28},{28,24},{1,5},{5... | collective-permute-start | bytes 786440 | tf_op jit(solution)/shard_map/ppermute | solution.py:41
  259.2 218.5 %reduce-scatter.5.cloned.1.call-start = ((), (), s32[]{:S(2)}) async-start(), calls=%async_computation.3 | async-start | bytes 1310720 | tf_op jit(solution)/shard_map/reduce_scatter | solution.py:1081
  267.4 18.6 %collective-permute-start.48 = (bf16[1,256,256]{2,1,0:T(8,128)(2,1)}, bf16[1,256,256]{2,1,0:T(8,128)(2,1)S(1)}, u32[]{:S(2)}, u32[]{:S(2)}) collective-permute-start(bf16[1,256,256]{2,1,0:T(8,128)(2,1)} %get-tuple-element.109), channel_id=1, source_target_pairs={{0,1},{1,0},{2,3},{3,2},{4,5},{5,4},{6,7},{7,6},{8,9},{9,8},{10,11... | collective-permute-start | bytes 393224 | tf_op jit(solution)/shard_map/ppermute | solution.py:41
  269.4 18.0 %collective-permute-start.49 = (bf16[1,256,256]{2,1,0:T(8,128)(2,1)}, bf16[1,256,256]{2,1,0:T(8,128)(2,1)S(1)}, u32[]{:S(2)}, u32[]{:S(2)}) collective-permute-start(bf16[1,256,256]{2,1,0:T(8,128)(2,1)} %get-tuple-element.110), channel_id=1, source_target_pairs={{0,2},{1,3},{2,0},{3,1},{4,6},{5,7},{6,4},{7,5},{8,10},{9,11},{10,... | collective-permute-start | bytes 393224 | tf_op jit(solution)/shard_map/ppermute | solution.py:41
  269.5 17.8 %collective-permute-start.50 = (bf16[1,256,256]{2,1,0:T(8,128)(2,1)}, bf16[1,256,256]{2,1,0:T(8,128)(2,1)S(1)}, u32[]{:S(2)}, u32[]{:S(2)}) collective-permute-start(bf16[1,256,256]{2,1,0:T(8,128)(2,1)} %get-tuple-element.111), channel_id=1, source_target_pairs={{0,3},{1,2},{2,1},{3,0},{4,7},{5,6},{6,5},{7,4},{8,11},{9,10},{10,... | collective-permute-start | bytes 393224 | tf_op jit(solution)/shard_map/ppermute | solution.py:41
  278.6 35.7 %collective-permute-start.45 = (bf16[1,256,256]{2,1,0:T(8,128)(2,1)}, bf16[1,256,256]{2,1,0:T(8,128)(2,1)S(1)}, u32[]{:S(2)}, u32[]{:S(2)}) collective-permute-start(bf16[1,256,256]{2,1,0:T(8,128)(2,1)} %get-tuple-element.104), channel_id=1, source_target_pairs={{0,1},{1,0},{2,3},{3,2},{4,5},{5,4},{6,7},{7,6},{8,9},{9,8},{10,11... | collective-permute-start | bytes 393224 | tf_op jit(solution)/shard_map/ppermute | solution.py:41
  280.6 35.5 %collective-permute-start.46 = (bf16[1,256,256]{2,1,0:T(8,128)(2,1)}, bf16[1,256,256]{2,1,0:T(8,128)(2,1)}, u32[]{:S(2)}, u32[]{:S(2)}) collective-permute-start(bf16[1,256,256]{2,1,0:T(8,128)(2,1)} %get-tuple-element.105), channel_id=1, source_target_pairs={{0,2},{1,3},{2,0},{3,1},{4,6},{5,7},{6,4},{7,5},{8,10},{9,11},{10,... | collective-permute-start | bytes 393224 | tf_op jit(solution)/shard_map/ppermute | solution.py:41
  286.0 32.0 %collective-permute-start.47 = (bf16[1,256,256]{2,1,0:T(8,128)(2,1)S(1)}, bf16[1,256,256]{2,1,0:T(8,128)(2,1)}, u32[]{:S(2)}, u32[]{:S(2)}) collective-permute-start(bf16[1,256,256]{2,1,0:T(8,128)(2,1)S(1)} %copy-done.49), channel_id=1, source_target_pairs={{0,3},{1,2},{2,1},{3,0},{4,7},{5,6},{6,5},{7,4},{8,11},{9,10},{10,... | collective-permute-start | bytes 393224 | tf_op jit(solution)/shard_map/ppermute | solution.py:41
  287.3 24.4 %collective-permute-start.51 = (bf16[4,4,128,256]{3,2,1,0:T(8,128)(2,1)}, bf16[4,4,128,256]{3,2,1,0:T(8,128)(2,1)S(1)}, u32[]{:S(2)}, u32[]{:S(2)}) collective-permute-start(bf16[4,4,128,256]{3,2,1,0:T(8,128)(2,1)} %get-tuple-element.118), channel_id=1, source_target_pairs={{0,4},{4,0},{8,12},{12,8},{16,20},{20,16},{24,28},{28,24},{1,5},{5... | collective-permute-start | bytes 3145736 | tf_op jit(solution)/shard_map/ppermute | solution.py:41
  310.1 47.5 %collective-permute-start.60 = (bf16[1,256,1024]{2,1,0:T(8,128)(2,1)}, bf16[1,256,1024]{2,1,0:T(8,128)(2,1)S(1)}, u32[]{:S(2)}, u32[]{:S(2)}) collective-permute-start(bf16[1,256,1024]{2,1,0:T(8,128)(2,1)} %get-tuple-element.114.rest_10_), channel_id=1, source_target_pairs={{0,3},{1,2},{2,1},{3,0},{4,7},{5,6},{6,5},{7,4},{8,11},{9,10},{10,... | collective-permute-start | bytes 1572872 | tf_op jit(solution)/shard_map/ppermute | solution.py:41
  311.7 58.4 %collective-permute-start.58 = (bf16[1,256,1024]{2,1,0:T(8,128)(2,1)}, bf16[1,256,1024]{2,1,0:T(8,128)(2,1)}, u32[]{:S(2)}, u32[]{:S(2)}) collective-permute-start(bf16[1,256,1024]{2,1,0:T(8,128)(2,1)} %get-tuple-element.112.rest_8_), channel_id=1, source_target_pairs={{0,1},{1,0},{2,3},{3,2},{4,5},{5,4},{6,7},{7,6},{8,9},{9,8},{10,11... | collective-permute-start | bytes 1572872 | tf_op jit(solution)/shard_map/ppermute | solution.py:41
  315.0 27.1 %collective-permute-start.52 = (bf16[4,128,256]{2,1,0:T(8,128)(2,1)S(1)}, bf16[4,128,256]{2,1,0:T(8,128)(2,1)S(1)}, u32[]{:S(2)}, u32[]{:S(2)}) collective-permute-start(bf16[4,128,256]{2,1,0:T(8,128)(2,1)S(1)} %get-tuple-element.171), channel_id=1, source_target_pairs={{0,1},{1,0},{2,3},{3,2},{4,5},{5,4},{6,7},{7,6},{8,9},{9,8},{10,11... | collective-permute-start | bytes 786440 | tf_op jit(solution)/shard_map/ppermute | solution.py:41
  316.1 27.2 %collective-permute-start.53 = (bf16[4,128,256]{2,1,0:T(8,128)(2,1)S(1)}, bf16[4,128,256]{2,1,0:T(8,128)(2,1)}, u32[]{:S(2)}, u32[]{:S(2)}) collective-permute-start(bf16[4,128,256]{2,1,0:T(8,128)(2,1)S(1)} %get-tuple-element.173), channel_id=1, source_target_pairs={{0,2},{1,3},{2,0},{3,1},{4,6},{5,7},{6,4},{7,5},{8,10},{9,11},{10,... | collective-permute-start | bytes 786440 | tf_op jit(solution)/shard_map/ppermute | solution.py:41
  317.9 30.3 %collective-permute-start.54 = (bf16[4,128,256]{2,1,0:T(8,128)(2,1)S(1)}, bf16[4,128,256]{2,1,0:T(8,128)(2,1)}, u32[]{:S(2)}, u32[]{:S(2)}) collective-permute-start(bf16[4,128,256]{2,1,0:T(8,128)(2,1)S(1)} %get-tuple-element.172), channel_id=1, source_target_pairs={{0,3},{1,2},{2,1},{3,0},{4,7},{5,6},{6,5},{7,4},{8,11},{9,10},{10,... | collective-permute-start | bytes 786440 | tf_op jit(solution)/shard_map/ppermute | solution.py:41
  342.1 28.0 %collective-permute-start.59 = (bf16[1,256,1024]{2,1,0:T(8,128)(2,1)}, bf16[1,256,1024]{2,1,0:T(8,128)(2,1)S(1)}, u32[]{:S(2)}, u32[]{:S(2)}) collective-permute-start(bf16[1,256,1024]{2,1,0:T(8,128)(2,1)} %get-tuple-element.113.rest_9_), channel_id=1, source_target_pairs={{0,2},{1,3},{2,0},{3,1},{4,6},{5,7},{6,4},{7,5},{8,10},{9,11},{10,... | collective-permute-start | bytes 1572872 | tf_op jit(solution)/shard_map/ppermute | solution.py:41
  355.3 23.6 %collective-permute-start.55 = (bf16[1,256,1024]{2,1,0:T(8,128)(2,1)}, bf16[1,256,1024]{2,1,0:T(8,128)(2,1)S(1)}, u32[]{:S(2)}, u32[]{:S(2)}) collective-permute-start(bf16[1,256,1024]{2,1,0:T(8,128)(2,1)} %get-tuple-element.119), channel_id=1, source_target_pairs={{0,1},{1,0},{2,3},{3,2},{4,5},{5,4},{6,7},{7,6},{8,9},{9,8},{10,11... | collective-permute-start | bytes 1572872 | tf_op jit(solution)/shard_map/ppermute | solution.py:41
  357.3 24.4 %collective-permute-start.56 = (bf16[1,256,1024]{2,1,0:T(8,128)(2,1)}, bf16[1,256,1024]{2,1,0:T(8,128)(2,1)S(1)}, u32[]{:S(2)}, u32[]{:S(2)}) collective-permute-start(bf16[1,256,1024]{2,1,0:T(8,128)(2,1)} %get-tuple-element.120), channel_id=1, source_target_pairs={{0,2},{1,3},{2,0},{3,1},{4,6},{5,7},{6,4},{7,5},{8,10},{9,11},{10,... | collective-permute-start | bytes 1572872 | tf_op jit(solution)/shard_map/ppermute | solution.py:41
  357.5 24.2 %collective-permute-start.57 = (bf16[1,256,1024]{2,1,0:T(8,128)(2,1)}, bf16[1,256,1024]{2,1,0:T(8,128)(2,1)S(1)}, u32[]{:S(2)}, u32[]{:S(2)}) collective-permute-start(bf16[1,256,1024]{2,1,0:T(8,128)(2,1)} %get-tuple-element.121), channel_id=1, source_target_pairs={{0,3},{1,2},{2,1},{3,0},{4,7},{5,6},{6,5},{7,4},{8,11},{9,10},{10,... | collective-permute-start | bytes 1572872 | tf_op jit(solution)/shard_map/ppermute | solution.py:41
  415.5 16.5 %collective-permute-start.65 = (bf16[4,256,256]{2,1,0:T(8,128)(2,1)S(1)}, bf16[4,256,256]{2,1,0:T(8,128)(2,1)S(1)}, u32[]{:S(2)}, u32[]{:S(2)}) collective-permute-start(bf16[4,256,256]{2,1,0:T(8,128)(2,1)S(1)} %get-tuple-element.166), channel_id=1, source_target_pairs={{0,1},{1,0},{2,3},{3,2},{4,5},{5,4},{6,7},{7,6},{8,9},{9,8},{10,11... | collective-permute-start | bytes 1572872 | tf_op jit(solution)/shard_map/ppermute | solution.py:41
  417.3 24.4 %collective-permute-start.67 = (bf16[4,256,256]{2,1,0:T(8,128)(2,1)S(1)}, bf16[4,256,256]{2,1,0:T(8,128)(2,1)S(1)}, u32[]{:S(2)}, u32[]{:S(2)}) collective-permute-start(bf16[4,256,256]{2,1,0:T(8,128)(2,1)S(1)} %get-tuple-element.167), channel_id=1, source_target_pairs={{0,3},{1,2},{2,1},{3,0},{4,7},{5,6},{6,5},{7,4},{8,11},{9,10},{10,... | collective-permute-start | bytes 1572872 | tf_op jit(solution)/shard_map/ppermute | solution.py:41
  431.9 19.8 %collective-permute-start.78 = (f32[4,6,1536]{2,1,0:T(8,128)S(1)}, f32[4,6,1536]{2,1,0:T(8,128)S(1)}, u32[]{:S(2)}, u32[]{:S(2)}) collective-permute-start(f32[4,6,1536]{2,1,0:T(8,128)S(1)} %get-tuple-element.181), channel_id=1, source_target_pairs={{0,4},{4,0},{8,12},{12,8},{16,20},{20,16},{24,28},{28,24},{1,5},{5... | collective-permute-start | bytes 442376 | tf_op jit(solution)/shard_map/ppermute | solution.py:41
  448.2 21.5 %collective-permute-start.72 = (bf16[128,2048]{1,0:T(8,128)(2,1)}, bf16[128,2048]{1,0:T(8,128)(2,1)}, u32[]{:S(2)}, u32[]{:S(2)}) collective-permute-start(bf16[128,2048]{1,0:T(8,128)(2,1)} %get-tuple-element.163), channel_id=1, source_target_pairs={{0,1},{1,0},{2,3},{3,2},{4,5},{5,4},{6,7},{7,6},{8,9},{9,8},{10,11... | collective-permute-start | bytes 1572872 | tf_op jit(solution)/shard_map/ppermute | solution.py:41
  449.9 21.1 %collective-permute-start.73 = (bf16[128,2048]{1,0:T(8,128)(2,1)}, bf16[128,2048]{1,0:T(8,128)(2,1)}, u32[]{:S(2)}, u32[]{:S(2)}) collective-permute-start(bf16[128,2048]{1,0:T(8,128)(2,1)} %get-tuple-element.165), channel_id=1, source_target_pairs={{0,2},{1,3},{2,0},{3,1},{4,6},{5,7},{6,4},{7,5},{8,10},{9,11},{10,... | collective-permute-start | bytes 1572872 | tf_op jit(solution)/shard_map/ppermute | solution.py:41
  450.1 22.6 %collective-permute-start.74 = (bf16[128,2048]{1,0:T(8,128)(2,1)}, bf16[128,2048]{1,0:T(8,128)(2,1)}, u32[]{:S(2)}, u32[]{:S(2)}) collective-permute-start(bf16[128,2048]{1,0:T(8,128)(2,1)} %get-tuple-element.164), channel_id=1, source_target_pairs={{0,3},{1,2},{2,1},{3,0},{4,7},{5,6},{6,5},{7,4},{8,11},{9,10},{10,... | collective-permute-start | bytes 1572872 | tf_op jit(solution)/shard_map/ppermute | solution.py:41
  (88 other events, 734.7 us)
Sparse Core Ops, SparseCore 0:
  58.0 157.8 all-gather.2
  259.4 171.5 reduce-scatter.2
  433.3 31.3 reduce-scatter.4

commit v4 on v3

--- a/solution.py
+++ b/solution.py
@@ -284,10 +284,14 @@
             else:
                 xt_ref[piece * wide : (piece + 1) * wide, :] = ref[...].T
 
-    parts = [ref[...].reshape(-1, ref.shape[-1]) for ref in y_refs]
-    y = parts[0] if y_count == 1 else jnp.concatenate(parts)
     for core, out_ref in ((0, keep_ref), (1, give_ref)):
-        result = dot(split_rows(place_ref, xt_ref, rows, chip, core, by_mask), y).astype(BF16)
+        left = split_rows(place_ref, xt_ref, rows, chip, core, by_mask)
+        result, start = 0.0, 0
+        for ref in y_refs:
+            part = ref[...].reshape(-1, ref.shape[-1])
+            result = result + dot(left[:, start : start + part.shape[0]], part)
+            start += part.shape[0]
+        result = result.astype(BF16)
         for seq in range(seqs):
             out_ref[seq, 0] = result[:, seq * columns : (seq + 1) * columns]
 
@@ -685,7 +689,7 @@
     tokens, model = normed.shape
     seqs, owners = axis_size("seq"), axis_size("dp")
     units = bank.columns // 2
-    chunk = min(512, units)
+    chunk = min(1024, units)
     per_place = units // chunk
     whole = pl.BlockSpec((tokens, model), lambda i: (0, 0))
     hidden = seqs * units
@@ -761,9 +765,10 @@
 
 
 def row_call(kernel, name, place, row, by_row, fixed, pieces, weight_shape, outs, held, flops, earlier=()):
-    row_spec = lambda shape: pl.BlockSpec(
-        (1,) + tuple(shape[1:]), lambda i: (row if shape[0] > 1 else 0,) + (0,) * (len(shape) - 1)
-    )
+    def row_spec(shape):
+        lead = 0 if len(shape) == 4 and shape[1] == 1 else row if shape[0] > 1 else 0
+        return pl.BlockSpec((1,) + tuple(shape[1:]), lambda i: (lead,) + (0,) * (len(shape) - 1))
+
     fixed_specs = [pl.BlockSpec(array.shape, lambda i, n=array.ndim: (0,) * n) for array in fixed]
     size = sum(array.size * array.dtype.itemsize for array in by_row) + 2 * math.prod(weight_shape)
     first = len(place) + len(by_row) + len(fixed) + len(pieces.arrays)
@@ -853,7 +858,7 @@
     columns_ref, frames_ref, skip_ref, sums_ref, weight_ref, sems = rest[-6:]
     copies = start_weight(pieces, refs, weight_ref, sems, place_ref, False)
     owner, count = utterance_of(seg_ref), mod_ref.shape[1]
-    grad_norm = against(own_ref[0], qkv_ref[...])
+    grad_norm = against(own_ref[0, 0], qkv_ref[...])
     for ref in got:
         grad_norm = grad_norm + ref[0].astype(F32)
     standard, inverse = standardize(hidden_ref[0])
@@ -1087,7 +1092,7 @@
             "leave",
             [place],
             row,
-            [hidden, grad_middle, grad_qkv[row][0]] + got[row] + [seg_here, modulation],
+            [hidden, grad_middle, grad_qkv[row]] + got[row] + [seg_here, modulation],
             [qkv_full],
             skip_parts,
             (2 * model, model),
@@ -1121,7 +1126,7 @@
     wide = pick(sum_bank, seq, 0).astype(F32)
     for mask in partners:
         wide = wide + swap(pick(sum_bank, seq ^ mask, 0), "seq", mask).astype(F32)
-    sum_up, sum_down = unpack_sums(wide, units, min(512, units))
+    sum_up, sum_down = unpack_sums(wide, units, min(1024, units))
     skip_shard = send_chips(sum_skip)
     sum_out, sum_qkv = sum_pair[:, :width].T, sum_pair[:, width:]
     sum_qkv = jnp.stack(

time: 496 us -> 495 us (level)
  waiting for transfers between devices: 116 us -> 121 us
    unnamed x115 -> x113, local copies, waits for them, and re-layouts: 12.9 us -> 12.7 us
  transfers between devices with their start and end apart: 82 -> 82, of which waited for: 28 -> 28; matrix products, arithmetic and copies ran while one was open for 9% -> 8% of each run, Pallas kernels for 34% -> 35%
where the time goes in v4:
time: 495 us; the launch traced here: 487 us
  Pallas kernels  204 us (41%)
  waiting for transfers between devices  121 us (24%)
  starting transfers between devices  92 us (19%)
  other arithmetic  31.6 us (6%)
  local copies, waits for them, and re-layouts  20.1 us (4%)
  between operations  16 us (3%)
    ppermute x79, waiting for transfers between devices, swap(): lax.ppermute(values, AXES[axis], [(i, i ^ mask) for i in range(axis_size(...  114 us
    ppermute x79, starting transfers between devices, swap(): lax.ppermute(values, AXES[axis], [(i, i ^ mask) for i in range(axis_size(...  91.7 us
    pallas_call x8, Pallas kernels, row_call(): pl.pallas_call(kernel, grid=(1,), out_shape=tuple(outs), in_specs=[SMEM_S...  56.5 us
    pallas_call x2, Pallas kernels, attend_back(): pl.pallas_call(functools.partial(attend_back_kernel, heads, width, scale)...  33.9 us
    pallas_call x1, Pallas kernels, mlp(): pl.pallas_call(functools.partial(mlp_kernel, bank, chunk), grid=(seqs * p...  33.4 us
    pallas_call x2, Pallas kernels, attend(): pl.pallas_call(functools.partial(attend_kernel, heads, width), grid=(rows...  28.2 us
    pallas_call x3, Pallas kernels, weight_grad(): pl.pallas_call(functools.partial(weight_grad_kernel, len(xs), len(ys), by...  21.8 us
    unnamed x113, local copies, waits for them, and re-layouts  12.7 us
  transfers between devices with their start and end apart: 82, of which 28 were waited for; matrix products, arithmetic and copies ran while one was open for 8% of the time, Pallas kernels for 35%

profile of v4, /device:TPU:0, one launch (start us, length us, event | category | flops | bytes accessed | tf_op | source)
XLA Modules:
  0.0 487.2 jit_solution(10667087445580105418)
XLA Ops:
  8.7 3.0 collective-permute-start.3
  11.8 2.6 collective-permute-start.4
  15.3 3.5 collective-permute-start.14
  23.3 3.1 collective-permute-start.8
  26.4 2.9 collective-permute-done.15
  29.4 2.5 collective-permute-start.18
  46.0 8.1 %collective-permute-done.1 = bf16[2,128,768]{2,1,0:T(8,128)(2,1)S(1)} collective-permute-done((bf16[2,128,768]{2,1,0:T(8,128)(2,1)S(1)}, bf16[2,128,768]{2,1,0:T(8,128)(2,1)S(1)}, u32[]{:S(2)}, u32[]{:S(2)}) %collective-permute-start.1) | collective-permute-done | bytes 393248 | tf_op jit(solution)/shard_map/ppermute | solution.py:41
  65.3 10.4 %collective-permute-done.16.rest_1_.rest_7_ = bf16[4,256,256]{2,1,0:T(8,128)(2,1)S(1)} collective-permute-done((bf16[4,256,256]{2,1,0:T(8,128)(2,1)S(1)}, bf16[4,256,256]{2,1,0:T(8,128)(2,1)S(1)}, u32[]{:S(2)}, u32[]{:S(2)}) %collective-permute-start.16) | collective-permute-done | bytes 524320 | tf_op jit(solution)/shard_map/ppermute | solution.py:41
  83.9 6.4 %enter.2 = (f32[2,256,1024]{2,1,0:T(8,128)}, bf16[1,256,1024]{2,1,0:T(8,128)(2,1)}) custom-call(s32[2]{0:T(128)} %pad_add_fusion.place_ref, f32[2,3]{1,0:T(2,128)} %subtract_multiply_fusion.coef_ref, bf16[2,256,1024]{2,1,0:T(8,128)(2,1)} %frames_ref.3, bf16[2,256,1024]{2,1,0:T(8,128)(2,1)} %skip_ref.3, bf16[2,256,1024]{2,1,0:T(8,128)(2,1)} %cond_ref.3, ...), custom_call_target="tpu_custom_call" | custom-call | flops 1073741824 | bytes 7489536 | tf_op jit(solution)/shard_map/enter/pallas_call | solution.py:778
  94.0 6.5 %enter.3 = (f32[2,256,1024]{2,1,0:T(8,128)}, bf16[1,256,1024]{2,1,0:T(8,128)(2,1)}) custom-call(s32[2]{0:T(128)} %pad_add_fusion.place_ref, f32[2,3]{1,0:T(2,128)} %subtract_multiply_fusion.coef_ref, bf16[2,256,1024]{2,1,0:T(8,128)(2,1)} %frames_ref.3, bf16[2,256,1024]{2,1,0:T(8,128)(2,1)} %skip_ref.3, ...), custom_call_target="tpu_custom_call", output_to_operand_aliasing={{0}: (15, {})} | custom-call | flops 1073741824 | bytes 7489536 | tf_op jit(solution)/shard_map/enter/pallas_call | solution.py:778
  101.9 15.2 %collective-permute-done.29.refs_1_.rest_3_ = bf16[1,256,1024]{2,1,0:T(8,128)(2,1)S(1)} collective-permute-done((bf16[1,256,1024]{2,1,0:T(8,128)(2,1)}, bf16[1,256,1024]{2,1,0:T(8,128)(2,1)S(1)}, u32[]{:S(2)}, u32[]{:S(2)}) %collective-permute-start.29) | collective-permute-done | bytes 524320 | tf_op jit(solution)/shard_map/ppermute | solution.py:41
  117.9 3.3 multiply_sine_fusion
  121.7 3.4 assemble.1.w_ref.weight_ref.rest_5_
  125.1 2.3 collective-permute-done.40.rest_1_
  132.6 6.1 %project.3.qkv_ref = bf16[4,1,256,768]{3,2,1,0:T(8,128)(2,1)} custom-call(bf16[1024,768]{1,0:T(8,128)(2,1)} %assemble.1.w_ref.weight_ref.rest_5_, f32[4,256,128]{2,1,0:T(8,128)} %get-tuple-element.193.cos_ref, f32[4,256,128]{2,1,0:T(8,128)} %get-tuple-element.192.sin_ref, bf16[1,256,1024]{2,1,0:T(8,128)(2,1)} %get-tuple-element.81.rest_0_, ...), custom_call_target="tpu_custom_call" | custom-call | flops 1610612736 | bytes 3670016 | tf_op jit(solution)/shard_map/project/pallas_call | solution.py:348
  142.3 13.9 %attend.3 = (bf16[1,256,256]{2,1,0:T(8,128)(2,1)}, bf16[1,256,256]{2,1,0:T(8,128)(2,1)}, bf16[1,256,256]{2,1,0:T(8,128)(2,1)}, bf16[1,256,256]{2,1,0:T(8,128)(2,1)}, f32[1,4,4,256]{3,2,1,0:T(4,128)}) custom-call(bf16[4,1,256,768]{3,2,1,0:T(8,128)(2,1)} %project.3.qkv_ref, f32[2,4,256]{2,1,0:T(4,128)} %bitcast.202), custom_call_target="tpu_custom_call" | custom-call | flops 4294967296 | bytes 2097152 | tf_op jit(solution)/shard_map/attend/pallas_call | solution.py:506
  157.7 5.9 %collective-permute-done.25.rest_3_ = bf16[1,256,1024]{2,1,0:T(8,128)(2,1)} collective-permute-done((bf16[1,256,1024]{2,1,0:T(8,128)(2,1)S(1)}, bf16[1,256,1024]{2,1,0:T(8,128)(2,1)}, u32[]{:S(2)}, u32[]{:S(2)}) %collective-permute-start.25) | collective-permute-done | bytes 524320 | tf_op jit(solution)/shard_map/ppermute | solution.py:41
  164.2 6.0 %project.2.qkv_ref = bf16[4,1,256,768]{3,2,1,0:T(8,128)(2,1)} custom-call(bf16[1024,768]{1,0:T(8,128)(2,1)} %assemble.1.w_ref.weight_ref.rest_5_, f32[4,256,128]{2,1,0:T(8,128)} %get-tuple-element.193.cos_ref, f32[4,256,128]{2,1,0:T(8,128)} %get-tuple-element.192.sin_ref, bf16[1,256,1024]{2,1,0:T(8,128)(2,1)} %get-tuple-element.75.rest_0_, ...), custom_call_target="tpu_custom_call" | custom-call | flops 1610612736 | bytes 3670016 | tf_op jit(solution)/shard_map/project/pallas_call | solution.py:348
  170.1 20.3 %collective-permute-done.42.rest_1_ = bf16[1,256,256]{2,1,0:T(8,128)(2,1)S(1)} collective-permute-done((bf16[1,256,256]{2,1,0:T(8,128)(2,1)}, bf16[1,256,256]{2,1,0:T(8,128)(2,1)S(1)}, u32[]{:S(2)}, u32[]{:S(2)}) %collective-permute-start.42) | collective-permute-done | bytes 131104 | tf_op jit(solution)/shard_map/ppermute | solution.py:41
  192.9 14.3 %attend.2 = (bf16[1,256,256]{2,1,0:T(8,128)(2,1)}, bf16[1,256,256]{2,1,0:T(8,128)(2,1)}, bf16[1,256,256]{2,1,0:T(8,128)(2,1)}, bf16[1,256,256]{2,1,0:T(8,128)(2,1)}, f32[1,4,4,256]{3,2,1,0:T(4,128)}) custom-call(bf16[4,1,256,768]{3,2,1,0:T(8,128)(2,1)} %project.2.qkv_ref, f32[2,4,256]{2,1,0:T(4,128)} %bitcast.203), custom_call_target="tpu_custom_call" | custom-call | flops 4294967296 | bytes 2097152 | tf_op jit(solution)/shard_map/attend/pallas_call | solution.py:506
  211.6 6.4 %branch.2 = (bf16[2,256,1024]{2,1,0:T(8,128)(2,1)}, f32[2,256,1024]{2,1,0:T(8,128)}, f32[2,256,1024]{2,1,0:T(8,128)}, bf16[2,256,1024]{2,1,0:T(8,128)(2,1)}, bf16[2,256,1024]{2,1,0:T(8,128)(2,1)}) custom-call(s32[2]{0:T(128)} %pad_add_fusion.place_ref, bf16[1,256,256]{2,1,0:T(8,128)(2,1)} %get-tuple-element.82.rest_0_, bf16[1,256,256]{2,1,0:T(8,128)(2,1)} %copy-done.38, ...), custom_call_target="tpu_custom_call" | custom-call | flops 536870912 | bytes 5916672 | tf_op jit(solution)/shard_map/branch/pallas_call | solution.py:778
  218.8 6.1 %branch.3 = (bf16[2,256,1024]{2,1,0:T(8,128)(2,1)}, f32[2,256,1024]{2,1,0:T(8,128)}, f32[2,256,1024]{2,1,0:T(8,128)}, bf16[2,256,1024]{2,1,0:T(8,128)(2,1)}, bf16[2,256,1024]{2,1,0:T(8,128)(2,1)}) custom-call(s32[2]{0:T(128)} %pad_add_fusion.place_ref, ...), custom_call_target="tpu_custom_call", output_to_operand_aliasing={{0}: (17, {}), {1}: (18, {}), {2}: (19, {}), {3}: (20, {}),... | custom-call | flops 536870912 | bytes 5916672 | tf_op jit(solution)/shard_map/branch/pallas_call | solution.py:778
  224.9 33.4 %mlp.1 = (f32[512,1024]{1,0:T(8,128)}, f32[512,1024]{1,0:T(8,128)}, bf16[8,4,128,2048]{3,2,1,0:T(8,128)(2,1)}) custom-call(s32[2]{0:T(128)} %pad_add_fusion.place_ref, bf16[512,1024]{1,0:T(8,128)(2,1)} %bitcast.165, bf16[512,1024]{1,0:T(8,128)(2,1)} %bitcast.166, bf16[8,4,128,2048]{3,2,1,0:T(8,128)(2,1)} %bitcast.216), custom_call_target="tpu_custom_call" | custom-call | flops 25769803776 | bytes 39845888 | tf_op jit(solution)/shard_map/mlp/pallas_call | solution.py:696
  258.6 7.7 %middle_back.2 = (bf16[2,256,1024]{2,1,0:T(8,128)(2,1)}, f32[2,256,1024]{2,1,0:T(8,128)}, bf16[2,256,1024]{2,1,0:T(8,128)(2,1)}, f32[1,4,8,1024]{3,2,1,0:T(8,128...) custom-call(s32[2]{0:T(128)} %pad_add_fusion.place_ref, ...), custom_call_target="tpu_custom_call" | custom-call | flops 536870912 | bytes 11683840 | tf_op jit(solution)/shard_map/middle_back/pallas_call | solution.py:778
  269.8 7.7 %middle_back.3 = (bf16[2,256,1024]{2,1,0:T(8,128)(2,1)}, f32[2,256,1024]{2,1,0:T(8,128)}, bf16[2,256,1024]{2,1,0:T(8,128)(2,1)}, f32[1,4,8,1024]{3,2,1,0:T(8,128...) custom-call(s32[2]{0:T(128)} %pad_add_fusion.place_ref, ...), custom_call_target="tpu_custom_call", output_to_operand_aliasing={{0}: (16, {}), {1}: (17, {}), {2}: (18, {})} | custom-call | flops 536870912 | bytes 11683840 | tf_op jit(solution)/shard_map/middle_back/pallas_call | solution.py:778
  279.4 5.2 %weight_grad.3 = (bf16[4,4,128,256]{3,2,1,0:T(8,128)(2,1)}, bf16[4,4,128,256]{3,2,1,0:T(8,128)(2,1)}) custom-call(s32[2]{0:T(128)} %pad_add_fusion.place_ref, bf16[512,1024]{1,0:T(8,128)(2,1)} %bitcast.163, bf16[512,1024]{1,0:T(8,128)(2,1)} %bitcast.164), custom_call_target="tpu_custom_call" | custom-call | flops 1073741824 | bytes 5242880 | tf_op jit(solution)/shard_map/weight_grad/pallas_call | solution.py:307
  287.0 16.9 %attend_back.2.grad_ref.rest_8_.own_ref = bf16[4,1,256,768]{3,2,1,0:T(8,128)(2,1)} custom-call(bf16[4,1,256,768]{3,2,1,0:T(8,128)(2,1)} %project.3.qkv_ref, f32[2,4,256]{2,1,0:T(4,128)} %bitcast.204, f32[1,4,4,256]{3,2,1,0:T(4,128)} %get-tuple-element.107.lse_ref, f32[4,256,128]{2,1,0:T(8,128)} %get-tuple-element.193.cos_ref, ...), custom_call_target="tpu_custom_call" | custom-call | flops 10737418240 | bytes 4194304 | tf_op jit(solution)/shard_map/attend_back/pallas_call | solution.py:603
  303.9 5.1 %spread_back.2 = (bf16[1,256,1024]{2,1,0:T(8,128)(2,1)}, bf16[1,256,1024]{2,1,0:T(8,128)(2,1)}, bf16[1,256,1024]{2,1,0:T(8,128)(2,1)}) custom-call(bf16[4,1,256,768]{3,2,1,0:T(8,128)(2,1)} %attend_back.2.grad_ref.rest_8_.own_ref, bf16[1024,768]{1,0:T(8,128)(2,1)} %assemble.1.w_ref.weight_ref.rest_5_), custom_call_target="tpu_custom_call" | custom-call | flops 1207959552 | bytes 3670016 | tf_op jit(solution)/shard_map/spread_back/pallas_call | solution.py:436
  317.2 17.0 %attend_back.3.grad_ref.rest_9_.own_ref = bf16[4,1,256,768]{3,2,1,0:T(8,128)(2,1)} custom-call(bf16[4,1,256,768]{3,2,1,0:T(8,128)(2,1)} %project.2.qkv_ref, f32[2,4,256]{2,1,0:T(4,128)} %bitcast.205, f32[1,4,4,256]{3,2,1,0:T(4,128)} %get-tuple-element.102.lse_ref, f32[4,256,128]{2,1,0:T(8,128)} %get-tuple-element.193.cos_ref, ...), custom_call_target="tpu_custom_call" | custom-call | flops 10737418240 | bytes 4194304 | tf_op jit(solution)/shard_map/attend_back/pallas_call | solution.py:603
  334.2 6.7 %collective-permute-done.52 = bf16[4,128,256]{2,1,0:T(8,128)(2,1)S(1)} collective-permute-done((bf16[4,128,256]{2,1,0:T(8,128)(2,1)S(1)}, bf16[4,128,256]{2,1,0:T(8,128)(2,1)S(1)}, u32[]{:S(2)}, u32[]{:S(2)}) %collective-permute-start.52) | collective-permute-done | bytes 262176 | tf_op jit(solution)/shard_map/ppermute | solution.py:41
  342.3 4.9 %collective-permute-done.54 = bf16[4,128,256]{2,1,0:T(8,128)(2,1)} collective-permute-done((bf16[4,128,256]{2,1,0:T(8,128)(2,1)S(1)}, bf16[4,128,256]{2,1,0:T(8,128)(2,1)}, u32[]{:S(2)}, u32[]{:S(2)}) %collective-permute-start.54) | collective-permute-done | bytes 262176 | tf_op jit(solution)/shard_map/ppermute | solution.py:41
  349.2 5.0 %spread_back.3 = (bf16[1,256,1024]{2,1,0:T(8,128)(2,1)}, bf16[1,256,1024]{2,1,0:T(8,128)(2,1)}, bf16[1,256,1024]{2,1,0:T(8,128)(2,1)}) custom-call(bf16[4,1,256,768]{3,2,1,0:T(8,128)(2,1)} %attend_back.3.grad_ref.rest_9_.own_ref, bf16[1024,768]{1,0:T(8,128)(2,1)} %assemble.1.w_ref.weight_ref.rest_5_, f32[4,128,256]{2,1,0:T(8,128)} %get-tuple-element.158.rest_0_), custom_call_target="tpu_custom_call" | custom-call | flops 1207959552 | bytes 3670016 | tf_op jit(solution)/shard_map/spread_back/pallas_call | solution.py:436
  357.7 9.6 %weight_grad.4 = (bf16[1,4,128,768]{3,2,1,0:T(8,128)(2,1)}, bf16[1,4,128,768]{3,2,1,0:T(8,128)(2,1)}) custom-call(s32[2]{0:T(128)} %pad_add_fusion.place_ref, bf16[256,1024]{1,0:T(8,128)(2,1)} %bitcast.176, bf16[256,1024]{1,0:T(8,128)(2,1)} %bitcast.177, bf16[256,1024]{1,0:T(8,128)(2,1)} %bitcast.178, bf16[256,1024]{1,0:T(8,128)(2,1)} %bitcast.159, ...), custom_call_target="tpu_custom_call" | custom-call | flops 3221225472 | bytes 7340032 | tf_op jit(solution)/shard_map/weight_grad/pallas_call | solution.py:307
  368.1 7.9 %leave.2 = (bf16[2,256,1024]{2,1,0:T(8,128)(2,1)}, bf16[2,256,1024]{2,1,0:T(8,128)(2,1)}, bf16[2,256,1024]{2,1,0:T(8,128)(2,1)}, f32[1,2,8,1024]{3,2,1,0:T(8,128)}) custom-call(s32[2]{0:T(128)} %pad_add_fusion.place_ref, f32[2,256,1024]{2,1,0:T(8,128)} %get-tuple-element.80.rest_4_.hidden_ref, f32[2,256,1024]{2,1,0:T(8,128)} %get-tuple-element.101.grad_middle_ref, ...), custom_call_target="tpu_custom_call" | custom-call | flops 1610612736 | bytes 11683840 | tf_op jit(solution)/shard_map/leave/pallas_call | solution.py:778
  376.0 4.7 collective-permute-done.56.rest_1_
  381.5 7.9 %leave.3 = (bf16[2,256,1024]{2,1,0:T(8,128)(2,1)}, bf16[2,256,1024]{2,1,0:T(8,128)(2,1)}, bf16[2,256,1024]{2,1,0:T(8,128)(2,1)}, f32[1,2,8,1024]{3,2,1,0:T(8,128)}) custom-call(s32[2]{0:T(128)} %pad_add_fusion.place_ref, f32[2,256,1024]{2,1,0:T(8,128)} %get-tuple-element.80.rest_4_.hidden_ref, ...), custom_call_target="tpu_custom_call", output_to_operand_aliasing={{0}: (18, {}), {1}: (19, {}), {2}: (20, {})} | custom-call | flops 1610612736 | bytes 11683840 | tf_op jit(solution)/shard_map/leave/pallas_call | solution.py:778
  398.3 7.0 %weight_grad.5 = (bf16[4,4,256,256]{3,2,1,0:T(8,128)(2,1)}, bf16[4,4,256,256]{3,2,1,0:T(8,128)(2,1)}) custom-call(s32[2]{0:T(128)} %pad_add_fusion.place_ref, bf16[512,1024]{1,0:T(8,128)(2,1)} %bitcast.156, bf16[512,1024]{1,0:T(8,128)(2,1)} %bitcast.157, bf16[512,1024]{1,0:T(8,128)(2,1)} %bitcast.162, f32[6,1536]{1,0:T(8,128)} %add_add_fusion.rest_3_), custom_call_target="tpu_custom_call" | custom-call | flops 2147483648 | bytes 10485760 | tf_op jit(solution)/shard_map/weight_grad/pallas_call | solution.py:307
  409.7 4.2 convert_add_fusion
  417.8 2.4 collective-permute-start.76
  423.1 6.9 %reduce-scatter.3.cloned.1.call-done = bf16[1,4,128,2048]{3,2,1,0:T(8,128)(2,1)} async-done(((bf16[8,4,128,2048]{3,2,1,0:T(8,128)(2,1)}), bf16[1,4,128,2048]{3,2,1,0:T(8,128)(2,1)}) %reduce-scatter.3.cloned.1.call-update) | async-done | bytes 2097168 | tf_op jit(solution)/shard_map/reduce_scatter | solution.py:1032
  430.9 7.8 %collective-permute-done.66 = bf16[4,256,256]{2,1,0:T(8,128)(2,1)S(1)} collective-permute-done((bf16[4,256,256]{2,1,0:T(8,128)(2,1)S(1)}, bf16[4,256,256]{2,1,0:T(8,128)(2,1)S(1)}, u32[]{:S(2)}, u32[]{:S(2)}) %collective-permute-start.66) | collective-permute-done | bytes 524320 | tf_op jit(solution)/shard_map/ppermute | solution.py:41
  453.3 3.7 collective-permute-done.68
  457.0 4.0 collective-permute-start.70
  461.0 2.4 fusion.16
  463.4 3.6 collective-permute-done.69
  468.7 2.5 collective-permute-done.74
  471.2 2.7 fusion.4.sums_ref
  473.9 2.3 unpack_sums.1
  (340 shorter events, 129.9 us)
Async XLA Ops:
  7.2 217.7 %all-gather.3.cloned.1.call-start = ((), (), s32[]{:S(2)}) async-start(), calls=%async_computation.4 | async-start | bytes 17301504 | tf_op jit(solution)/shard_map/all_gather | solution.py:973
  29.4 25.7 %collective-permute-start.18 = (bf16[4,256,256]{2,1,0:T(8,128)(2,1)S(1)}, bf16[4,256,256]{2,1,0:T(8,128)(2,1)S(1)}, u32[]{:S(2)}, u32[]{:S(2)}) collective-permute-start(bf16[4,256,256]{2,1,0:T(8,128)(2,1)S(1)} %pad_maximum_fusion.2.rest_0_.rest_6_), channel_id=1, source_target_pairs={{0,3},{1,2},{2,1},{3,0},{4,7},{5,6},{6,5},{7,4},{8,11},{9,10},{10,... | collective-permute-start | bytes 1572872 | tf_op jit(solution)/shard_map/ppermute | solution.py:41
  35.4 18.7 %collective-permute-start.1 = (bf16[2,128,768]{2,1,0:T(8,128)(2,1)S(1)}, bf16[2,128,768]{2,1,0:T(8,128)(2,1)S(1)}, u32[]{:S(2)}, u32[]{:S(2)}) collective-permute-start(bf16[2,128,768]{2,1,0:T(8,128)(2,1)S(1)} %pad_maximum_fusion.3), channel_id=1, source_target_pairs={{0,16},{4,20},{8,24},{12,28},{16,0},{20,4},{24,8},{28,12},{1,17},{... | collective-permute-start | bytes 1179656 | tf_op jit(solution)/shard_map/ppermute | solution.py:41
  57.9 372.1 %reduce-scatter.3.cloned.1.call-start = ((), (), s32[]{:S(2)}) async-start(), calls=%async_computation.2 | async-start | bytes 18874368 | tf_op jit(solution)/shard_map/reduce_scatter | solution.py:1032
  58.0 17.7 %collective-permute-start.16 = (bf16[4,256,256]{2,1,0:T(8,128)(2,1)S(1)}, bf16[4,256,256]{2,1,0:T(8,128)(2,1)S(1)}, u32[]{:S(2)}, u32[]{:S(2)}) collective-permute-start(bf16[4,256,256]{2,1,0:T(8,128)(2,1)S(1)} %pad_maximum_fusion.2.rest_0_.rest_6_), channel_id=1, source_target_pairs={{0,1},{1,0},{2,3},{3,2},{4,5},{5,4},{6,7},{7,6},{8,9},{9,8},{10,11... | collective-permute-start | bytes 1572872 | tf_op jit(solution)/shard_map/ppermute | solution.py:41
  59.5 17.3 %collective-permute-start.17 = (bf16[4,256,256]{2,1,0:T(8,128)(2,1)S(1)}, bf16[4,256,256]{2,1,0:T(8,128)(2,1)S(1)}, u32[]{:S(2)}, u32[]{:S(2)}) collective-permute-start(bf16[4,256,256]{2,1,0:T(8,128)(2,1)S(1)} %pad_maximum_fusion.2.rest_0_.rest_6_), channel_id=1, source_target_pairs={{0,2},{1,3},{2,0},{3,1},{4,6},{5,7},{6,4},{7,5},{8,10},{9,11},{10,... | collective-permute-start | bytes 1572872 | tf_op jit(solution)/shard_map/ppermute | solution.py:41
  64.7 18.1 %collective-permute-start.19 = (bf16[4,256,256]{2,1,0:T(8,128)(2,1)S(1)}, bf16[4,256,256]{2,1,0:T(8,128)(2,1)S(1)}, u32[]{:S(2)}, u32[]{:S(2)}) collective-permute-start(bf16[4,256,256]{2,1,0:T(8,128)(2,1)S(1)} %pad_maximum_fusion.2.rest_0_.rest_6_), channel_id=1, source_target_pairs={{0,4},{4,0},{8,12},{12,8},{16,20},{20,16},{24,28},{28,24},{1,5},{5... | collective-permute-start | bytes 1572872 | tf_op jit(solution)/shard_map/ppermute | solution.py:41
  64.9 17.9 %collective-permute-start.22 = (bf16[4,256,256]{2,1,0:T(8,128)(2,1)}, bf16[4,256,256]{2,1,0:T(8,128)(2,1)S(1)}, u32[]{:S(2)}, u32[]{:S(2)}) collective-permute-start(bf16[4,256,256]{2,1,0:T(8,128)(2,1)} %copy-done.1), channel_id=1, source_target_pairs={{0,4},{4,0},{8,12},{12,8},{16,20},{20,16},{24,28},{28,24},{1,5},{5... | collective-permute-start | bytes 1572872 | tf_op jit(solution)/shard_map/ppermute | solution.py:41
  82.3 38.8 %collective-permute-start.2 = (bf16[4,128,768]{2,1,0:T(8,128)(2,1)}, bf16[4,128,768]{2,1,0:T(8,128)(2,1)}, u32[]{:S(2)}, u32[]{:S(2)}) collective-permute-start(bf16[4,128,768]{2,1,0:T(8,128)(2,1)} %pad_maximum_fusion.1.rest_0_.refs_4_), channel_id=1, source_target_pairs={{0,4},{4,0},{8,12},{12,8},{16,20},{20,16},{24,28},{28,24},{1,5},{5... | collective-permute-start | bytes 2359304 | tf_op jit(solution)/shard_map/ppermute | solution.py:41
  90.4 26.7 %collective-permute-start.29 = (bf16[1,256,1024]{2,1,0:T(8,128)(2,1)}, bf16[1,256,1024]{2,1,0:T(8,128)(2,1)S(1)}, u32[]{:S(2)}, u32[]{:S(2)}) collective-permute-start(bf16[1,256,1024]{2,1,0:T(8,128)(2,1)} %get-tuple-element.81.rest_0_), channel_id=1, source_target_pairs={{0,3},{1,2},{2,1},{3,0},{4,7},{5,6},{6,5},{7,4},{8,11},{9,10},{10,... | collective-permute-start | bytes 1572872 | tf_op jit(solution)/shard_map/ppermute | solution.py:41
  91.9 35.5 %collective-permute-start.40 = (bf16[1,256,1024]{2,1,0:T(8,128)(2,1)}, bf16[1,256,1024]{2,1,0:T(8,128)(2,1)S(1)}, u32[]{:S(2)}, u32[]{:S(2)}) collective-permute-start(bf16[1,256,1024]{2,1,0:T(8,128)(2,1)} %get-tuple-element.81.rest_0_), channel_id=1, source_target_pairs={{0,1},{1,0},{2,3},{3,2},{4,5},{5,4},{6,7},{7,6},{8,9},{9,8},{10,11... | collective-permute-start | bytes 1572872 | tf_op jit(solution)/shard_map/ppermute | solution.py:41
  92.9 35.9 %collective-permute-start.41 = (bf16[1,256,1024]{2,1,0:T(8,128)(2,1)}, bf16[1,256,1024]{2,1,0:T(8,128)(2,1)S(1)}, u32[]{:S(2)}, u32[]{:S(2)}) collective-permute-start(bf16[1,256,1024]{2,1,0:T(8,128)(2,1)} %get-tuple-element.81.rest_0_), channel_id=1, source_target_pairs={{0,2},{1,3},{2,0},{3,1},{4,6},{5,7},{6,4},{7,5},{8,10},{9,11},{10,... | collective-permute-start | bytes 1572872 | tf_op jit(solution)/shard_map/ppermute | solution.py:41
  100.5 40.7 %collective-permute-start.23 = (bf16[1,256,1024]{2,1,0:T(8,128)(2,1)}, bf16[1,256,1024]{2,1,0:T(8,128)(2,1)S(1)}, u32[]{:S(2)}, u32[]{:S(2)}) collective-permute-start(bf16[1,256,1024]{2,1,0:T(8,128)(2,1)} %get-tuple-element.75.rest_0_), channel_id=1, source_target_pairs={{0,1},{1,0},{2,3},{3,2},{4,5},{5,4},{6,7},{7,6},{8,9},{9,8},{10,11... | collective-permute-start | bytes 1572872 | tf_op jit(solution)/shard_map/ppermute | solution.py:41
  121.1 35.1 %collective-permute-start.24 = (bf16[1,256,1024]{2,1,0:T(8,128)(2,1)}, bf16[1,256,1024]{2,1,0:T(8,128)(2,1)}, u32[]{:S(2)}, u32[]{:S(2)}) collective-permute-start(bf16[1,256,1024]{2,1,0:T(8,128)(2,1)} %get-tuple-element.75.rest_0_), channel_id=1, source_target_pairs={{0,2},{1,3},{2,0},{3,1},{4,6},{5,7},{6,4},{7,5},{8,10},{9,11},{10,... | collective-permute-start | bytes 1572872 | tf_op jit(solution)/shard_map/ppermute | solution.py:41
  127.4 36.3 %collective-permute-start.25 = (bf16[1,256,1024]{2,1,0:T(8,128)(2,1)S(1)}, bf16[1,256,1024]{2,1,0:T(8,128)(2,1)}, u32[]{:S(2)}, u32[]{:S(2)}) collective-permute-start(bf16[1,256,1024]{2,1,0:T(8,128)(2,1)S(1)} %copy-done.24), channel_id=1, source_target_pairs={{0,3},{1,2},{2,1},{3,0},{4,7},{5,6},{6,5},{7,4},{8,11},{9,10},{10,... | collective-permute-start | bytes 1572872 | tf_op jit(solution)/shard_map/ppermute | solution.py:41
  138.7 53.2 %collective-permute-start.33 = (bf16[4,128,256]{2,1,0:T(8,128)(2,1)S(1)}, bf16[4,128,256]{2,1,0:T(8,128)(2,1)S(1)}, u32[]{:S(2)}, u32[]{:S(2)}) collective-permute-start(bf16[4,128,256]{2,1,0:T(8,128)(2,1)S(1)} %pad_maximum_fusion.6.rest_8_.rest_0_), channel_id=1, source_target_pairs={{0,1},{1,0},{2,3},{3,2},{4,5},{5,4},{6,7},{7,6},{8,9},{9,8},{10,11... | collective-permute-start | bytes 786440 | tf_op jit(solution)/shard_map/ppermute | solution.py:41
  140.2 52.2 %collective-permute-start.34 = (bf16[4,128,256]{2,1,0:T(8,128)(2,1)S(1)}, bf16[4,128,256]{2,1,0:T(8,128)(2,1)S(1)}, u32[]{:S(2)}, u32[]{:S(2)}) collective-permute-start(bf16[4,128,256]{2,1,0:T(8,128)(2,1)S(1)} %pad_maximum_fusion.6.rest_8_.rest_0_), channel_id=1, source_target_pairs={{0,2},{1,3},{2,0},{3,1},{4,6},{5,7},{6,4},{7,5},{8,10},{9,11},{10,... | collective-permute-start | bytes 786440 | tf_op jit(solution)/shard_map/ppermute | solution.py:41
  141.2 51.3 %collective-permute-start.35 = (bf16[4,128,256]{2,1,0:T(8,128)(2,1)S(1)}, bf16[4,128,256]{2,1,0:T(8,128)(2,1)S(1)}, u32[]{:S(2)}, u32[]{:S(2)}) collective-permute-start(bf16[4,128,256]{2,1,0:T(8,128)(2,1)S(1)} %pad_maximum_fusion.6.rest_8_.rest_0_), channel_id=1, source_target_pairs={{0,3},{1,2},{2,1},{3,0},{4,7},{5,6},{6,5},{7,4},{8,11},{9,10},{10,... | collective-permute-start | bytes 786440 | tf_op jit(solution)/shard_map/ppermute | solution.py:41
  156.3 34.1 %collective-permute-start.42 = (bf16[1,256,256]{2,1,0:T(8,128)(2,1)}, bf16[1,256,256]{2,1,0:T(8,128)(2,1)S(1)}, u32[]{:S(2)}, u32[]{:S(2)}) collective-permute-start(bf16[1,256,256]{2,1,0:T(8,128)(2,1)} %get-tuple-element.83.rest_1_), channel_id=1, source_target_pairs={{0,1},{1,0},{2,3},{3,2},{4,5},{5,4},{6,7},{7,6},{8,9},{9,8},{10,11... | collective-permute-start | bytes 393224 | tf_op jit(solution)/shard_map/ppermute | solution.py:41
  163.7 28.2 %collective-permute-start.43 = (bf16[1,256,256]{2,1,0:T(8,128)(2,1)}, bf16[1,256,256]{2,1,0:T(8,128)(2,1)S(1)}, u32[]{:S(2)}, u32[]{:S(2)}) collective-permute-start(bf16[1,256,256]{2,1,0:T(8,128)(2,1)} %get-tuple-element.84.rest_2_), channel_id=1, source_target_pairs={{0,2},{1,3},{2,0},{3,1},{4,6},{5,7},{6,4},{7,5},{8,10},{9,11},{10,... | collective-permute-start | bytes 393224 | tf_op jit(solution)/shard_map/ppermute | solution.py:41
  190.4 16.9 %collective-permute-start.44 = (bf16[1,256,256]{2,1,0:T(8,128)(2,1)S(1)}, bf16[1,256,256]{2,1,0:T(8,128)(2,1)S(1)}, u32[]{:S(2)}, u32[]{:S(2)}) collective-permute-start(bf16[1,256,256]{2,1,0:T(8,128)(2,1)S(1)} %copy-done.47), channel_id=1, source_target_pairs={{0,3},{1,2},{2,1},{3,0},{4,7},{5,6},{6,5},{7,4},{8,11},{9,10},{10,... | collective-permute-start | bytes 393224 | tf_op jit(solution)/shard_map/ppermute | solution.py:41
  191.8 17.3 %collective-permute-start.36 = (bf16[4,128,256]{2,1,0:T(8,128)(2,1)S(1)}, bf16[4,128,256]{2,1,0:T(8,128)(2,1)S(1)}, u32[]{:S(2)}, u32[]{:S(2)}) collective-permute-start(bf16[4,128,256]{2,1,0:T(8,128)(2,1)S(1)} %pad_maximum_fusion.6.rest_8_.rest_0_), channel_id=1, source_target_pairs={{0,4},{4,0},{8,12},{12,8},{16,20},{20,16},{24,28},{28,24},{1,5},{5... | collective-permute-start | bytes 786440 | tf_op jit(solution)/shard_map/ppermute | solution.py:41
  191.9 17.5 %collective-permute-start.37 = (bf16[4,128,256]{2,1,0:T(8,128)(2,1)S(1)}, bf16[4,128,256]{2,1,0:T(8,128)(2,1)S(1)}, u32[]{:S(2)}, u32[]{:S(2)}) collective-permute-start(bf16[4,128,256]{2,1,0:T(8,128)(2,1)S(1)} %collective-permute-done.33.rest_9_.rest_1_), channel_id=1, source_target_pairs={{0,4},{4,0},{8,12},{12,8},{16,20},{20,16},{24,28},{28,24},{1,5},{5... | collective-permute-start | bytes 786440 | tf_op jit(solution)/shard_map/ppermute | solution.py:41
  192.4 18.4 %collective-permute-start.38 = (bf16[4,128,256]{2,1,0:T(8,128)(2,1)S(1)}, bf16[4,128,256]{2,1,0:T(8,128)(2,1)S(1)}, u32[]{:S(2)}, u32[]{:S(2)}) collective-permute-start(bf16[4,128,256]{2,1,0:T(8,128)(2,1)S(1)} %collective-permute-done.34.rest_10_.rest_2_), channel_id=1, source_target_pairs={{0,4},{4,0},{8,12},{12,8},{16,20},{20,16},{24,28},{28,24},{1,5},{5... | collective-permute-start | bytes 786440 | tf_op jit(solution)/shard_map/ppermute | solution.py:41
  192.5 18.3 %collective-permute-start.39 = (bf16[4,128,256]{2,1,0:T(8,128)(2,1)S(1)}, bf16[4,128,256]{2,1,0:T(8,128)(2,1)S(1)}, u32[]{:S(2)}, u32[]{:S(2)}) collective-permute-start(bf16[4,128,256]{2,1,0:T(8,128)(2,1)S(1)} %collective-permute-done.35.rest_11_.rest_3_), channel_id=1, source_target_pairs={{0,4},{4,0},{8,12},{12,8},{16,20},{20,16},{24,28},{28,24},{1,5},{5... | collective-permute-start | bytes 786440 | tf_op jit(solution)/shard_map/ppermute | solution.py:41
  258.3 217.9 %reduce-scatter.5.cloned.1.call-start = ((), (), s32[]{:S(2)}) async-start(), calls=%async_computation.3 | async-start | bytes 1310720 | tf_op jit(solution)/shard_map/reduce_scatter | solution.py:1086
  266.2 18.4 %collective-permute-start.48 = (bf16[1,256,256]{2,1,0:T(8,128)(2,1)}, bf16[1,256,256]{2,1,0:T(8,128)(2,1)S(1)}, u32[]{:S(2)}, u32[]{:S(2)}) collective-permute-start(bf16[1,256,256]{2,1,0:T(8,128)(2,1)} %get-tuple-element.109), channel_id=1, source_target_pairs={{0,1},{1,0},{2,3},{3,2},{4,5},{5,4},{6,7},{7,6},{8,9},{9,8},{10,11... | collective-permute-start | bytes 393224 | tf_op jit(solution)/shard_map/ppermute | solution.py:41
  268.1 18.2 %collective-permute-start.49 = (bf16[1,256,256]{2,1,0:T(8,128)(2,1)}, bf16[1,256,256]{2,1,0:T(8,128)(2,1)S(1)}, u32[]{:S(2)}, u32[]{:S(2)}) collective-permute-start(bf16[1,256,256]{2,1,0:T(8,128)(2,1)} %get-tuple-element.110), channel_id=1, source_target_pairs={{0,2},{1,3},{2,0},{3,1},{4,6},{5,7},{6,4},{7,5},{8,10},{9,11},{10,... | collective-permute-start | bytes 393224 | tf_op jit(solution)/shard_map/ppermute | solution.py:41
  268.1 18.2 %collective-permute-start.50 = (bf16[1,256,256]{2,1,0:T(8,128)(2,1)}, bf16[1,256,256]{2,1,0:T(8,128)(2,1)S(1)}, u32[]{:S(2)}, u32[]{:S(2)}) collective-permute-start(bf16[1,256,256]{2,1,0:T(8,128)(2,1)} %get-tuple-element.111), channel_id=1, source_target_pairs={{0,3},{1,2},{2,1},{3,0},{4,7},{5,6},{6,5},{7,4},{8,11},{9,10},{10,... | collective-permute-start | bytes 393224 | tf_op jit(solution)/shard_map/ppermute | solution.py:41
  277.5 35.6 %collective-permute-start.45 = (bf16[1,256,256]{2,1,0:T(8,128)(2,1)}, bf16[1,256,256]{2,1,0:T(8,128)(2,1)S(1)}, u32[]{:S(2)}, u32[]{:S(2)}) collective-permute-start(bf16[1,256,256]{2,1,0:T(8,128)(2,1)} %get-tuple-element.104), channel_id=1, source_target_pairs={{0,1},{1,0},{2,3},{3,2},{4,5},{5,4},{6,7},{7,6},{8,9},{9,8},{10,11... | collective-permute-start | bytes 393224 | tf_op jit(solution)/shard_map/ppermute | solution.py:41
  279.4 35.4 %collective-permute-start.46 = (bf16[1,256,256]{2,1,0:T(8,128)(2,1)}, bf16[1,256,256]{2,1,0:T(8,128)(2,1)}, u32[]{:S(2)}, u32[]{:S(2)}) collective-permute-start(bf16[1,256,256]{2,1,0:T(8,128)(2,1)} %get-tuple-element.105), channel_id=1, source_target_pairs={{0,2},{1,3},{2,0},{3,1},{4,6},{5,7},{6,4},{7,5},{8,10},{9,11},{10,... | collective-permute-start | bytes 393224 | tf_op jit(solution)/shard_map/ppermute | solution.py:41
  284.6 32.1 %collective-permute-start.47 = (bf16[1,256,256]{2,1,0:T(8,128)(2,1)S(1)}, bf16[1,256,256]{2,1,0:T(8,128)(2,1)}, u32[]{:S(2)}, u32[]{:S(2)}) collective-permute-start(bf16[1,256,256]{2,1,0:T(8,128)(2,1)S(1)} %copy-done.48), channel_id=1, source_target_pairs={{0,3},{1,2},{2,1},{3,0},{4,7},{5,6},{6,5},{7,4},{8,11},{9,10},{10,... | collective-permute-start | bytes 393224 | tf_op jit(solution)/shard_map/ppermute | solution.py:41
  286.3 24.1 %collective-permute-start.51 = (bf16[4,4,128,256]{3,2,1,0:T(8,128)(2,1)}, bf16[4,4,128,256]{3,2,1,0:T(8,128)(2,1)S(1)}, u32[]{:S(2)}, u32[]{:S(2)}) collective-permute-start(bf16[4,4,128,256]{3,2,1,0:T(8,128)(2,1)} %get-tuple-element.118), channel_id=1, source_target_pairs={{0,4},{4,0},{8,12},{12,8},{16,20},{20,16},{24,28},{28,24},{1,5},{5... | collective-permute-start | bytes 3145736 | tf_op jit(solution)/shard_map/ppermute | solution.py:41
  309.0 47.2 %collective-permute-start.60 = (bf16[1,256,1024]{2,1,0:T(8,128)(2,1)}, bf16[1,256,1024]{2,1,0:T(8,128)(2,1)S(1)}, u32[]{:S(2)}, u32[]{:S(2)}) collective-permute-start(bf16[1,256,1024]{2,1,0:T(8,128)(2,1)} %get-tuple-element.114.rest_10_), channel_id=1, source_target_pairs={{0,3},{1,2},{2,1},{3,0},{4,7},{5,6},{6,5},{7,4},{8,11},{9,10},{10,... | collective-permute-start | bytes 1572872 | tf_op jit(solution)/shard_map/ppermute | solution.py:41
  310.4 56.9 %collective-permute-start.58 = (bf16[1,256,1024]{2,1,0:T(8,128)(2,1)}, bf16[1,256,1024]{2,1,0:T(8,128)(2,1)}, u32[]{:S(2)}, u32[]{:S(2)}) collective-permute-start(bf16[1,256,1024]{2,1,0:T(8,128)(2,1)} %get-tuple-element.112.rest_8_), channel_id=1, source_target_pairs={{0,1},{1,0},{2,3},{3,2},{4,5},{5,4},{6,7},{7,6},{8,9},{9,8},{10,11... | collective-permute-start | bytes 1572872 | tf_op jit(solution)/shard_map/ppermute | solution.py:41
  313.7 27.2 %collective-permute-start.52 = (bf16[4,128,256]{2,1,0:T(8,128)(2,1)S(1)}, bf16[4,128,256]{2,1,0:T(8,128)(2,1)S(1)}, u32[]{:S(2)}, u32[]{:S(2)}) collective-permute-start(bf16[4,128,256]{2,1,0:T(8,128)(2,1)S(1)} %get-tuple-element.171), channel_id=1, source_target_pairs={{0,1},{1,0},{2,3},{3,2},{4,5},{5,4},{6,7},{7,6},{8,9},{9,8},{10,11... | collective-permute-start | bytes 786440 | tf_op jit(solution)/shard_map/ppermute | solution.py:41
  314.8 27.5 %collective-permute-start.53 = (bf16[4,128,256]{2,1,0:T(8,128)(2,1)S(1)}, bf16[4,128,256]{2,1,0:T(8,128)(2,1)}, u32[]{:S(2)}, u32[]{:S(2)}) collective-permute-start(bf16[4,128,256]{2,1,0:T(8,128)(2,1)S(1)} %get-tuple-element.173), channel_id=1, source_target_pairs={{0,2},{1,3},{2,0},{3,1},{4,6},{5,7},{6,4},{7,5},{8,10},{9,11},{10,... | collective-permute-start | bytes 786440 | tf_op jit(solution)/shard_map/ppermute | solution.py:41
  316.8 30.4 %collective-permute-start.54 = (bf16[4,128,256]{2,1,0:T(8,128)(2,1)S(1)}, bf16[4,128,256]{2,1,0:T(8,128)(2,1)}, u32[]{:S(2)}, u32[]{:S(2)}) collective-permute-start(bf16[4,128,256]{2,1,0:T(8,128)(2,1)S(1)} %get-tuple-element.172), channel_id=1, source_target_pairs={{0,3},{1,2},{2,1},{3,0},{4,7},{5,6},{6,5},{7,4},{8,11},{9,10},{10,... | collective-permute-start | bytes 786440 | tf_op jit(solution)/shard_map/ppermute | solution.py:41
  340.9 26.4 %collective-permute-start.59 = (bf16[1,256,1024]{2,1,0:T(8,128)(2,1)}, bf16[1,256,1024]{2,1,0:T(8,128)(2,1)S(1)}, u32[]{:S(2)}, u32[]{:S(2)}) collective-permute-start(bf16[1,256,1024]{2,1,0:T(8,128)(2,1)} %get-tuple-element.113.rest_9_), channel_id=1, source_target_pairs={{0,2},{1,3},{2,0},{3,1},{4,6},{5,7},{6,4},{7,5},{8,10},{9,11},{10,... | collective-permute-start | bytes 1572872 | tf_op jit(solution)/shard_map/ppermute | solution.py:41
  354.2 21.8 %collective-permute-start.55 = (bf16[1,256,1024]{2,1,0:T(8,128)(2,1)}, bf16[1,256,1024]{2,1,0:T(8,128)(2,1)S(1)}, u32[]{:S(2)}, u32[]{:S(2)}) collective-permute-start(bf16[1,256,1024]{2,1,0:T(8,128)(2,1)} %get-tuple-element.119), channel_id=1, source_target_pairs={{0,1},{1,0},{2,3},{3,2},{4,5},{5,4},{6,7},{7,6},{8,9},{9,8},{10,11... | collective-permute-start | bytes 1572872 | tf_op jit(solution)/shard_map/ppermute | solution.py:41
  356.2 24.6 %collective-permute-start.56 = (bf16[1,256,1024]{2,1,0:T(8,128)(2,1)}, bf16[1,256,1024]{2,1,0:T(8,128)(2,1)S(1)}, u32[]{:S(2)}, u32[]{:S(2)}) collective-permute-start(bf16[1,256,1024]{2,1,0:T(8,128)(2,1)} %get-tuple-element.120), channel_id=1, source_target_pairs={{0,2},{1,3},{2,0},{3,1},{4,6},{5,7},{6,4},{7,5},{8,10},{9,11},{10,... | collective-permute-start | bytes 1572872 | tf_op jit(solution)/shard_map/ppermute | solution.py:41
  356.2 24.5 %collective-permute-start.57 = (bf16[1,256,1024]{2,1,0:T(8,128)(2,1)}, bf16[1,256,1024]{2,1,0:T(8,128)(2,1)}, u32[]{:S(2)}, u32[]{:S(2)}) collective-permute-start(bf16[1,256,1024]{2,1,0:T(8,128)(2,1)} %get-tuple-element.121), channel_id=1, source_target_pairs={{0,3},{1,2},{2,1},{3,0},{4,7},{5,6},{6,5},{7,4},{8,11},{9,10},{10,... | collective-permute-start | bytes 1572872 | tf_op jit(solution)/shard_map/ppermute | solution.py:41
  415.0 23.7 %collective-permute-start.66 = (bf16[4,256,256]{2,1,0:T(8,128)(2,1)S(1)}, bf16[4,256,256]{2,1,0:T(8,128)(2,1)S(1)}, u32[]{:S(2)}, u32[]{:S(2)}) collective-permute-start(bf16[4,256,256]{2,1,0:T(8,128)(2,1)S(1)} %get-tuple-element.168), channel_id=1, source_target_pairs={{0,2},{1,3},{2,0},{3,1},{4,6},{5,7},{6,4},{7,5},{8,10},{9,11},{10,... | collective-permute-start | bytes 1572872 | tf_op jit(solution)/shard_map/ppermute | solution.py:41
  416.2 24.3 %collective-permute-start.67 = (bf16[4,256,256]{2,1,0:T(8,128)(2,1)S(1)}, bf16[4,256,256]{2,1,0:T(8,128)(2,1)S(1)}, u32[]{:S(2)}, u32[]{:S(2)}) collective-permute-start(bf16[4,256,256]{2,1,0:T(8,128)(2,1)S(1)} %get-tuple-element.167), channel_id=1, source_target_pairs={{0,3},{1,2},{2,1},{3,0},{4,7},{5,6},{6,5},{7,4},{8,11},{9,10},{10,... | collective-permute-start | bytes 1572872 | tf_op jit(solution)/shard_map/ppermute | solution.py:41
  430.8 19.4 %collective-permute-start.78 = (f32[4,6,1536]{2,1,0:T(8,128)S(1)}, f32[4,6,1536]{2,1,0:T(8,128)S(1)}, u32[]{:S(2)}, u32[]{:S(2)}) collective-permute-start(f32[4,6,1536]{2,1,0:T(8,128)S(1)} %get-tuple-element.181), channel_id=1, source_target_pairs={{0,4},{4,0},{8,12},{12,8},{16,20},{20,16},{24,28},{28,24},{1,5},{5... | collective-permute-start | bytes 442376 | tf_op jit(solution)/shard_map/ppermute | solution.py:41
  446.7 21.9 %collective-permute-start.72 = (bf16[128,2048]{1,0:T(8,128)(2,1)}, bf16[128,2048]{1,0:T(8,128)(2,1)}, u32[]{:S(2)}, u32[]{:S(2)}) collective-permute-start(bf16[128,2048]{1,0:T(8,128)(2,1)} %get-tuple-element.163), channel_id=1, source_target_pairs={{0,1},{1,0},{2,3},{3,2},{4,5},{5,4},{6,7},{7,6},{8,9},{9,8},{10,11... | collective-permute-start | bytes 1572872 | tf_op jit(solution)/shard_map/ppermute | solution.py:41
  448.4 20.3 %collective-permute-start.73 = (bf16[128,2048]{1,0:T(8,128)(2,1)}, bf16[128,2048]{1,0:T(8,128)(2,1)}, u32[]{:S(2)}, u32[]{:S(2)}) collective-permute-start(bf16[128,2048]{1,0:T(8,128)(2,1)} %get-tuple-element.165), channel_id=1, source_target_pairs={{0,2},{1,3},{2,0},{3,1},{4,6},{5,7},{6,4},{7,5},{8,10},{9,11},{10,... | collective-permute-start | bytes 1572872 | tf_op jit(solution)/shard_map/ppermute | solution.py:41
  448.8 22.4 %collective-permute-start.74 = (bf16[128,2048]{1,0:T(8,128)(2,1)}, bf16[128,2048]{1,0:T(8,128)(2,1)}, u32[]{:S(2)}, u32[]{:S(2)}) collective-permute-start(bf16[128,2048]{1,0:T(8,128)(2,1)} %get-tuple-element.164), channel_id=1, source_target_pairs={{0,3},{1,2},{2,1},{3,0},{4,7},{5,6},{6,5},{7,4},{8,11},{9,10},{10,... | collective-permute-start | bytes 1572872 | tf_op jit(solution)/shard_map/ppermute | solution.py:41
  (87 other events, 730.1 us)
Sparse Core Ops, SparseCore 0:
  58.0 157.6 all-gather.2
  258.5 171.4 reduce-scatter.2
  432.2 32.4 reduce-scatter.4
